TPU v7x, 256 devices: a whole 4x4x8 slice. The times are simulated.
256 devices in a mesh: dp: 32 (over y, x, core), seq: 8 (over z).
Axes of the slice: x: 4, y: 4, z: 8, core: 2. Of those that a mesh axis runs over, the one named last changes fastest.
Arguments:
- streams: bfloat16 [32, 1024, 12288], P('dp', 'seq'), may hold values from -6 to 6
- short_filter: bfloat16 [7, 12288], P(None, 'dp'), may hold values from -2 to 2
- long_filter: bfloat16 [256, 128], P('dp'), may hold values from -0.5 to 0.5
- skip: bfloat16 [4096], P('dp'), may hold values from 0.5 to 1.5
- grad_out: bfloat16 [32, 1024, 4096], P('dp', 'seq'), may hold values from -6 to 6
Outputs:
- grad_streams: bfloat16 [32, 1024, 12288], P('dp', 'seq')
- grad_short: float32 [7, 12288], P(None, 'dp')
- grad_long: float32 [256, 128], P('dp')
- grad_skip: float32 [4096], P('dp')
All inputs are finite; a program needn't handle non-finite values.
Results may differ from a plain program's by a relative error of at most 0.01.
Values may be sent and summed in bfloat16 or wider, within the bound.
No kernel may reach another device: no remote copies, remote signals or barrier semaphores. Data moves between devices by JAX's collectives and lax.ppermute only.
A program may use at most 192 MiB of HBM per device.

v0:
```python
import math

import jax
import jax.numpy as jnp
from jax import lax
from jax.sharding import PartitionSpec as P


def passed_along(block, axis, distance):
    devices = range(lax.axis_size(axis))
    route = [(i - distance, i) for i in devices if i - distance in devices]
    return lax.ppermute(block, axis, route)


def toeplitz(filters, tok_rows):
    group_count, long_taps = filters.shape
    span_cols = tok_rows + long_taps - 1
    kernel_line = jnp.concatenate(
        [filters[:, ::-1], jnp.zeros((group_count, tok_rows), filters.dtype)], axis=1
    )
    tiled = jnp.tile(kernel_line, (1, tok_rows))[:, : tok_rows * span_cols]
    return tiled.reshape(group_count, tok_rows, span_cols)


def lag_sums(gate_part, context_part, long_taps):
    group_count, members, tok_rows = gate_part.shape
    span_cols = context_part.shape[2]
    correlation = jnp.einsum(
        "gks,gkm->gsm", gate_part, context_part, preferred_element_type=jnp.float32
    )
    flat_corr = correlation.reshape(group_count, tok_rows * span_cols)
    flat_corr = jnp.concatenate(
        [flat_corr, jnp.zeros((group_count, tok_rows), jnp.float32)], axis=1
    )
    skewed = flat_corr.reshape(group_count, tok_rows, span_cols + 1)[:, :, :long_taps]
    return jnp.sum(skewed, axis=1)[:, ::-1]


def local(streams, short_filter, long_filter, skip, grad_out):
    tok_rows = streams.shape[1]
    chan_width = grad_out.shape[2]
    short_taps = short_filter.shape[0]
    long_taps = long_filter.shape[1]
    reach_rows = long_taps - 1
    short_all, long_all, skip_all = (
        lax.all_gather(short_filter, "dp", axis=1, tiled=True),
        lax.all_gather(long_filter, "dp", axis=0, tiled=True),
        lax.all_gather(skip, "dp", axis=0, tiled=True),
    )
    groups = long_all.shape[0]
    members = chan_width // groups
    source = streams[0]
    cotangent = grad_out[0].astype(jnp.float32)
    short_vals = short_all.astype(jnp.float32)
    skip_vals = skip_all.astype(jnp.float32)
    before = passed_along(source[tok_rows - short_taps + 1 :], "seq", 1)
    extended = jnp.concatenate([before, source], axis=0).astype(jnp.float32)
    mixed_feat = short_vals[0] * extended[short_taps - 1 :]
    for lag_step in range(1, short_taps):
        mixed_feat = (
            mixed_feat
            + short_vals[lag_step]
            * extended[short_taps - 1 - lag_step : short_taps - 1 - lag_step + tok_rows]
        )
    query_feat = mixed_feat[:, :chan_width]
    key_feat = mixed_feat[:, chan_width : 2 * chan_width]
    value_feat = mixed_feat[:, 2 * chan_width :]
    product = (key_feat * value_feat).astype(jnp.bfloat16)
    prior_rows = passed_along(product[tok_rows - reach_rows :], "seq", 1)
    context_cols = jnp.concatenate([prior_rows, product], axis=0).T
    gate_grad = (cotangent * query_feat).astype(jnp.bfloat16)
    gate_cols = gate_grad.T
    ahead_rows = passed_along(gate_grad[:reach_rows], "seq", -1)
    ahead_cols = ahead_rows.T
    block_count = 4
    block_groups = groups // block_count
    block_width = block_groups * members
    span_cols = tok_rows + reach_rows
    filtered_list = []
    back_list = []
    lag_list = []
    for block_index in range(block_count):
        chan_lo = block_index * block_width
        matrix = toeplitz(
            long_all[block_index * block_groups : (block_index + 1) * block_groups], tok_rows
        )
        context_part = context_cols[chan_lo : chan_lo + block_width].reshape(
            block_groups, members, span_cols
        )
        gate_part = gate_cols[chan_lo : chan_lo + block_width].reshape(
            block_groups, members, tok_rows
        )
        filtered = jnp.einsum(
            "gsm,gkm->gks", matrix, context_part, preferred_element_type=jnp.float32
        )
        filtered_list.append(filtered.reshape(block_width, tok_rows))
        back_part = jnp.einsum(
            "gsm,gks->gkm", matrix[:, :, reach_rows:], gate_part, preferred_element_type=jnp.float32
        )
        ahead_part = ahead_cols[chan_lo : chan_lo + block_width].reshape(
            block_groups, members, reach_rows
        )
        edge_part = jnp.einsum(
            "gsm,gks->gkm",
            matrix[:, :reach_rows, :reach_rows],
            ahead_part,
            preferred_element_type=jnp.float32,
        )
        back_part = jnp.concatenate(
            [
                back_part[:, :, : tok_rows - reach_rows],
                back_part[:, :, tok_rows - reach_rows :] + edge_part,
            ],
            axis=2,
        )
        back_list.append(back_part.reshape(block_width, tok_rows))
        lag_list.append(lag_sums(gate_part, context_part, long_taps))
    product_vals = product.astype(jnp.float32)
    gate_vals = gate_grad.astype(jnp.float32)
    wave = jnp.concatenate(filtered_list, axis=0).T + skip_vals * product_vals
    back_all = jnp.concatenate(back_list, axis=0).T
    prod_grad = back_all + skip_vals * gate_vals
    mixed_grad = jnp.concatenate(
        [cotangent * wave, prod_grad * value_feat, prod_grad * key_feat], axis=1
    )
    after_rows = passed_along(mixed_grad[: short_taps - 1].astype(jnp.bfloat16), "seq", -1).astype(
        jnp.float32
    )
    tailed = jnp.concatenate([mixed_grad, after_rows], axis=0)
    input_grad = short_vals[0] * mixed_grad
    for lag_step in range(1, short_taps):
        input_grad = input_grad + short_vals[lag_step] * tailed[lag_step : lag_step + tok_rows]
    scale = 1.0 / math.sqrt(lax.axis_size("dp") * lax.axis_size("seq") * tok_rows)
    short_terms = (
        jnp.stack(
            [
                jnp.sum(
                    mixed_grad
                    * extended[short_taps - 1 - lag_step : short_taps - 1 - lag_step + tok_rows],
                    axis=0,
                )
                for lag_step in range(short_taps)
            ],
            axis=0,
        )
        * scale
    )
    long_terms = jnp.concatenate(lag_list, axis=0) * scale
    skip_terms = jnp.sum(gate_vals * product_vals, axis=0) * scale
    summed = lax.psum((short_terms, long_terms, skip_terms), "seq")
    grad_short, grad_long, grad_skip = (
        lax.psum_scatter(summed[0], "dp", scatter_dimension=1, tiled=True),
        lax.psum_scatter(summed[1], "dp", scatter_dimension=0, tiled=True),
        lax.psum_scatter(summed[2], "dp", scatter_dimension=0, tiled=True),
    )
    return (input_grad.astype(jnp.bfloat16)[None], grad_short, grad_long, grad_skip)


def solution(mesh):
    placed = (P("dp", "seq", None), P(None, "dp"), P("dp", None), P("dp"), P("dp", "seq", None))
    return jax.shard_map(
        local,
        mesh=mesh,
        in_specs=placed,
        out_specs=(P("dp", "seq", None), P(None, "dp"), P("dp", None), P("dp")),
        check_vma=False,
    )
```

profile of v0, /device:TPU:2, one launch (start us, length us, event | category | flops | bytes accessed | tf_op | source)
XLA Modules:
  0.0 710.7 jit_solution(16374908507433870716)
XLA Ops:
  7.2 1.7 slice_bitcast_fusion
  8.9 4.5 collective-permute-start
  13.4 24.7 %all_gather.9 = bf16[7,12288]{1,0:T(8,128)(2,1)S(1)} all-gather(bf16[7,384]{1,0:T(8,128)(2,1)} %param.6), channel_id=1, replica_groups=mesh['dp'=32,'seq'=8] {'dp'}, dimensions={1}, use_global_device_ids=true | all-gather | bytes 177408 | tf_op jit(solution)/shard_map/all_gather | solution.py:46
  38.3 19.3 %all-gather = bf16[32,1,128]{2,1,0:T(2,128)(2,1)S(1)} all-gather(bf16[1,1,128]{2,1,0:T(2,128)(2,1)} %bitcast.183), channel_id=1, replica_groups=mesh['dp'=32,'seq'=8] {'dp'}, dimensions={0}, use_global_device_ids=true | all-gather | bytes 8448 | tf_op jit(solution)/shard_map/all_gather | solution.py:48
  57.6 23.5 %all_gather.10 = bf16[256,128]{1,0:T(8,128)(2,1)S(1)} all-gather(bf16[8,128]{1,0:T(8,128)(2,1)} %param.7), channel_id=1, replica_groups=mesh['dp'=32,'seq'=8] {'dp'}, dimensions={0}, use_global_device_ids=true | all-gather | bytes 67584 | tf_op jit(solution)/shard_map/all_gather | solution.py:47
  81.5 2.6 copy.72
  84.1 2.2 slice.315
  86.3 16.3 %reshape.134 = bf16[64,128,255]{2,1,0:T(8,128)(2,1)} reshape(bf16[64,32640]{1,0:T(8,128)(2,1)} %slice.315) | data formatting | bytes 8355840 | tf_op jit(solution)/shard_map/reshape | solution.py:22
  103.0 2.6 copy.71
  105.6 2.2 slice.312
  107.9 15.9 %reshape.131 = bf16[64,128,255]{2,1,0:T(8,128)(2,1)} reshape(bf16[64,32640]{1,0:T(8,128)(2,1)} %slice.312) | data formatting | bytes 8355840 | tf_op jit(solution)/shard_map/reshape | solution.py:22
  124.1 2.6 copy.70
  126.7 2.2 slice.309
  128.9 16.0 %reshape.128 = bf16[64,128,255]{2,1,0:T(8,128)(2,1)} reshape(bf16[64,32640]{1,0:T(8,128)(2,1)} %slice.309) | data formatting | bytes 8355840 | tf_op jit(solution)/shard_map/reshape | solution.py:22
  145.3 2.6 copy.69
  147.9 2.2 slice.306
  150.1 16.0 %reshape.125 = bf16[64,128,255]{2,1,0:T(8,128)(2,1)} reshape(bf16[64,32640]{1,0:T(8,128)(2,1)} %slice.306) | data formatting | bytes 8355840 | tf_op jit(solution)/shard_map/reshape | solution.py:22
  168.0 1.8 maximum_convert_fusion
  169.9 5.2 multiply_add_fusion
  175.8 1.9 copy-done.5
  177.8 1.3 collective-permute-start.2
  181.8 5.5 collective-permute-start.1
  187.3 121.0 %all-reduce.9 = f32[4096]{0:T(1024)S(1)} all-reduce(f32[4096]{0:T(1024)S(1)} %broadcast_multiply_fusion.1), channel_id=4, replica_groups=mesh['dp'=32,'seq'=8] {'dp'}, use_global_device_ids=true, to_apply=%region_17.0.clone | all-reduce | flops 4096 | bytes 32768
  308.9 4.1 fusion.14
  313.0 3.8 fusion.18
  318.6 2.0 fusion.43
  322.3 2.5 fusion.37
  324.7 3.3 fusion.34
  329.0 2.1 copy.68
  331.0 1.2 pad_maximum_fusion.4
  334.5 2.2 fusion.31
  338.1 2.2 fusion.28
  341.6 1.5 maximum_bitcast_fusion
  344.3 3.5 fusion.49
  349.1 3.5 fusion.48
  355.0 3.5 fusion.47
  360.6 4.5 fusion.46
  365.1 2.0 copy.53
  367.1 4.5 slice_multiply_fusion.6
  371.7 1.3 copy-done.3
  373.6 2.0 pad_maximum_fusion.1
  375.7 9.4 %multiply_reduce_fusion = (f32[12288]{0:T(1024)S(1)}, f32[12288]{0:T(1024)S(1)}, f32[12288]{0:T(1024)S(1)}, f32[12288]{0:T(1024)S(1)}, f32[12288]{0:T(1024)S(1)}, /*index=5*/f32[12288]{0:T(1024)}, f32[12288]{0:T(1024)}) fusion(f32[134,12288]{1,0:T(8,128)S(1)} %bitcast.109, f32[128,4096]{1,0:T(8,128)} %copy-done.3, f32[128,4096]{1,0:T(8,128)S(1)} %get-tuple-element.20, ...), kind=kLoop, calls=%fused_computation.15 | loop fusion | flops 25079808 | bytes 50675712 | tf_op jit(solution)/shard_map/reduce_sum | solution.py:137
  385.1 4.5 fusion.53
  389.7 4.5 fusion.52
  394.2 4.5 fusion.51
  398.8 4.5 fusion.50
  404.2 1.3 collective-permute-start.3
  405.5 9.3 %reshape.154 = f32[64,32640]{1,0:T(8,128)} reshape(f32[64,128,255]{2,1,0:T(8,128)} %fusion.53) | data formatting | bytes 16711680 | tf_op jit(solution)/shard_map/reshape | solution.py:31
  414.8 4.0 concatenate.74
  418.9 2.5 copy.76
  422.0 9.3 %reshape.152 = f32[64,32640]{1,0:T(8,128)} reshape(f32[64,128,255]{2,1,0:T(8,128)} %fusion.52) | data formatting | bytes 16711680 | tf_op jit(solution)/shard_map/reshape | solution.py:31
  431.2 4.0 concatenate.73
  435.3 2.5 copy.75
  438.4 9.5 %reshape.150 = f32[64,32640]{1,0:T(8,128)} reshape(f32[64,128,255]{2,1,0:T(8,128)} %fusion.51) | data formatting | bytes 16711680 | tf_op jit(solution)/shard_map/reshape | solution.py:31
  447.9 4.0 concatenate.72
  451.9 2.5 copy.74
  455.0 9.3 %reshape.148 = f32[64,32640]{1,0:T(8,128)} reshape(f32[64,128,255]{2,1,0:T(8,128)} %fusion.50) | data formatting | bytes 16711680 | tf_op jit(solution)/shard_map/reshape | solution.py:31
  464.3 4.0 concatenate.71
  468.3 2.5 copy.73
  473.6 112.6 %all-reduce.13.cloned.1.call-done = f32[256,128]{1,0:T(8,128)} async-done(((f32[256,128]{1,0:T(8,128)}), f32[256,128]{1,0:T(8,128)}) %all-reduce.13.cloned.1.call-update) | async-done | bytes 131088
  587.0 2.8 pad_maximum_fusion
  590.0 7.6 %fusion.7 = bf16[1,128,12288]{2,1,0:T(8,128)(2,1)} fusion(f32[134,12288]{1,0:T(8,128)S(1)} %pad_maximum_fusion, f32[12288]{0:T(1024)S(1)} %bitcast.174, f32[12288]{0:T(1024)S(1)} %bitcast.172, f32[12288]{0:T(1024)S(1)} %bitcast.170, f32[12288]{0:T(1024)S(1)} %bitcast.168, f32[12288]{0:T(1024)S(1)} %bitcast.166, f32[12288]{0:T(1024)S(1)} %bitcast.164, ...), kind=kLoop, calls=%fused_computation.28 | loop fusion | flops 25165824 | bytes 47529984 | tf_op jit(solution)/shard_map/broadcast_in_dim | solution.py:156
  597.5 75.1 %reduce-scatter.2.cloned.1.call-done = f32[7,384]{1,0:T(8,128)} async-done(((f32[7,12288]{1,0:T(8,128)}), f32[7,384]{1,0:T(8,128)}) %reduce-scatter.2.cloned.1.call-update) | async-done | bytes 10768 | tf_op jit(solution)/shard_map/reduce_scatter | solution.py:152
  672.6 31.0 %all-reduce.10 = (f32[7,384]{1,0:T(8,128)}, f32[8,128]{1,0:T(8,128)}, f32[128]{0:T(128)}) all-reduce(f32[7,384]{1,0:T(8,128)} %reduce-scatter.2.cloned.1.call-done, f32[8,128]{1,0:T(8,128)S(1)} %constant_dynamic-slice_fusion, f32[128]{0:T(128)S(1)} %copy-done.44), channel_id=1, replica_groups=mesh['dp'=32,'seq'=8] {'seq'}, use_global_device_ids=true, to_apply=%region_7.0 | all-reduce | flops 3840 | bytes 30720 | tf_op jit(solution)/shard_map/psum | solution.py:150
  (162 shorter events, 29.2 us)
Async XLA Ops:
  7.2 579.1 %all-reduce.13.cloned.1.call-start = ((), (), s32[]{:S(2)}) async-start(), calls=%async_computation.2 | async-start | bytes 262144
  8.9 159.1 %collective-permute-start = (bf16[6,12288]{1,0:T(8,128)(2,1)}, bf16[6,12288]{1,0:T(8,128)(2,1)}, u32[]{:S(2)}, u32[]{:S(2)}) collective-permute-start(bf16[6,12288]{1,0:T(8,128)(2,1)} %slice_bitcast_fusion), channel_id=1, source_target_pairs={{0,1},{1,2},{2,3},{3,4},{4,5},{5,6},{6,7},{8,9},{9,10},{10,11},{11... | collective-permute-start | bytes 442376 | tf_op jit(solution)/shard_map/ppermute | solution.py:12
  38.2 131.6 %copy-start.28 = (f32[1,12288]{1,0:T(1,128)}, f32[1,12288]{1,0:T(1,128)S(1)}, u32[]{:S(2)}) copy-start(f32[1,12288]{1,0:T(1,128)S(1)} %get-tuple-element.34) | copy-start | bytes 147460
  38.2 131.6 %copy-start.30 = (f32[1,12288]{1,0:T(1,128)}, f32[1,12288]{1,0:T(1,128)S(1)}, u32[]{:S(2)}) copy-start(f32[1,12288]{1,0:T(1,128)S(1)} %get-tuple-element.35) | copy-start | bytes 147460
  38.3 131.6 %copy-start.32 = (f32[1,12288]{1,0:T(1,128)}, f32[1,12288]{1,0:T(1,128)S(1)}, u32[]{:S(2)}) copy-start(f32[1,12288]{1,0:T(1,128)S(1)} %get-tuple-element.36) | copy-start | bytes 147460
  38.3 131.6 %copy-start.34 = (f32[1,12288]{1,0:T(1,128)}, f32[1,12288]{1,0:T(1,128)S(1)}, u32[]{:S(2)}) copy-start(f32[1,12288]{1,0:T(1,128)S(1)} %get-tuple-element.37) | copy-start | bytes 147460
  38.3 131.6 %copy-start.36 = (f32[1,12288]{1,0:T(1,128)}, f32[1,12288]{1,0:T(1,128)S(1)}, u32[]{:S(2)}) copy-start(f32[1,12288]{1,0:T(1,128)S(1)} %get-tuple-element.38) | copy-start | bytes 147460
  38.3 131.6 %copy-start.38 = (f32[1,12288]{1,0:T(1,128)}, f32[1,12288]{1,0:T(1,128)S(1)}, u32[]{:S(2)}) copy-start(f32[1,12288]{1,0:T(1,128)S(1)} %get-tuple-element.39) | copy-start | bytes 147460
  38.3 131.6 %copy-start.40 = (f32[1,12288]{1,0:T(1,128)}, f32[1,12288]{1,0:T(1,128)S(1)}, u32[]{:S(2)}) copy-start(f32[1,12288]{1,0:T(1,128)S(1)} %get-tuple-element.40) | copy-start | bytes 147460
  150.1 16.0 %copy-start.45 = (u32[256]{0:T(256)S(1)}, u32[256]{0:T(256)}, u32[]{:S(2)}) copy-start(u32[256]{0:T(256)} %constant.30) | copy-start | bytes 3076
  150.1 17.9 %copy-start.19 = (bf16[1,128,12288]{2,1,0:T(8,128)(2,1)S(1)}, bf16[1,128,12288]{2,1,0:T(8,128)(2,1)}, u32[]{:S(2)}) copy-start(bf16[1,128,12288]{2,1,0:T(8,128)(2,1)} %param.5) | copy-start | bytes 9437188
  169.8 5.3 copy-start
  169.9 5.2 copy-start.18
  175.1 2.7 copy-start.5
  177.8 135.2 %copy-start.8 = (bf16[128,4096]{1,0:T(8,128)(2,1)}, bf16[128,4096]{1,0:T(8,128)(2,1)S(1)}, u32[]{:S(2)}) copy-start(bf16[128,4096]{1,0:T(8,128)(2,1)S(1)} %get-tuple-element.16) | copy-start | bytes 3145732
  177.8 140.8 %collective-permute-start.2 = (bf16[127,4096]{1,0:T(8,128)(2,1)S(1)}, bf16[127,4096]{1,0:T(8,128)(2,1)}, u32[]{:S(2)}, u32[]{:S(2)}) collective-permute-start(bf16[127,4096]{1,0:T(8,128)(2,1)S(1)} %bitcast.126), channel_id=1, source_target_pairs={{1,0},{2,1},{3,2},{4,3},{5,4},{6,5},{7,6},{9,8},{10,9},{11,10},{12... | collective-permute-start | bytes 3121160 | tf_op jit(solution)/shard_map/ppermute | solution.py:12
  179.3 137.5 %copy-start.26 = (bf16[1024,128]{1,0:T(8,128)(2,1)}, bf16[1024,128]{1,0:T(8,128)(2,1)S(1)}, u32[]{:S(2)}) copy-start(bf16[1024,128]{1,0:T(8,128)(2,1)S(1)} %copy.63) | copy-start | bytes 786436
  179.5 137.3 %copy-start.24 = (bf16[1024,128]{1,0:T(8,128)(2,1)}, bf16[1024,128]{1,0:T(8,128)(2,1)S(1)}, u32[]{:S(2)}) copy-start(bf16[1024,128]{1,0:T(8,128)(2,1)S(1)} %copy.61) | copy-start | bytes 786436
  179.7 137.2 %copy-start.20 = (bf16[1024,128]{1,0:T(8,128)(2,1)}, bf16[1024,128]{1,0:T(8,128)(2,1)S(1)}, u32[]{:S(2)}) copy-start(bf16[1024,128]{1,0:T(8,128)(2,1)S(1)} %copy.59) | copy-start | bytes 786436
  181.8 159.8 %collective-permute-start.1 = (bf16[127,4096]{1,0:T(8,128)(2,1)}, bf16[127,4096]{1,0:T(8,128)(2,1)}, u32[]{:S(2)}, u32[]{:S(2)}) collective-permute-start(bf16[127,4096]{1,0:T(8,128)(2,1)} %slice.303), channel_id=1, source_target_pairs={{0,1},{1,2},{2,3},{3,4},{4,5},{5,6},{6,7},{8,9},{9,10},{10,11},{11... | collective-permute-start | bytes 3121160 | tf_op jit(solution)/shard_map/ppermute | solution.py:12
  308.3 8.6 %copy-start.6 = (bf16[64,128,255]{2,1,0:T(8,128)(2,1)S(1)}, bf16[64,128,255]{2,1,0:T(8,128)(2,1)}, u32[]{:S(2)}) copy-start(bf16[64,128,255]{2,1,0:T(8,128)(2,1)} %reshape.128) | copy-start | bytes 12533764
  308.9 8.8 %copy-start.7 = (bf16[64,128,255]{2,1,0:T(8,128)(2,1)S(1)}, bf16[64,128,255]{2,1,0:T(8,128)(2,1)}, u32[]{:S(2)}) copy-start(bf16[64,128,255]{2,1,0:T(8,128)(2,1)} %reshape.125) | copy-start | bytes 12533764
  308.9 8.8 %copy-start.22 = (bf16[1024,128]{1,0:T(8,128)(2,1)S(1)}, bf16[1024,128]{1,0:T(8,128)(2,1)}, u32[]{:S(2)}) copy-start(bf16[1024,128]{1,0:T(8,128)(2,1)} %copy.57) | copy-start | bytes 786436
  320.5 7.4 %copy-start.17 = (f32[64,16,128]{2,1,0:T(8,128)S(1)}, f32[64,16,128]{2,1,0:T(8,128)}, u32[]{:S(2)}) copy-start(f32[64,16,128]{2,1,0:T(8,128)} %fusion.14) | copy-start | bytes 1572868
  322.2 8.8 %copy-start.16 = (f32[64,16,128]{2,1,0:T(8,128)S(1)}, f32[64,16,128]{2,1,0:T(8,128)}, u32[]{:S(2)}) copy-start(f32[64,16,128]{2,1,0:T(8,128)} %fusion.18) | copy-start | bytes 1572868
  344.3 8.4 %copy-start.9 = (bf16[1024,255]{1,0:T(8,128)(2,1)}, bf16[1024,255]{1,0:T(8,128)(2,1)S(1)}, u32[]{:S(2)}) copy-start(bf16[1024,255]{1,0:T(8,128)(2,1)S(1)} %copy.52) | copy-start | bytes 1566724
  349.1 9.4 %copy-start.11 = (bf16[1024,255]{1,0:T(8,128)(2,1)}, bf16[1024,255]{1,0:T(8,128)(2,1)S(1)}, u32[]{:S(2)}) copy-start(bf16[1024,255]{1,0:T(8,128)(2,1)S(1)} %copy.51) | copy-start | bytes 1566724
  354.9 5.6 copy-start.13
  360.6 15.1 %slice-start = ((s8[6684672]{0:T(1024)(128)(4,1)}), s8[2490368]{0:T(1024)(128)(4,1)S(1)}, s32[]{:S(2)}) async-start(s8[6684672]{0:T(1024)(128)(4,1)} %bitcast.108), calls=%async_computation.3 | async-start | bytes 4980736
  367.1 8.5 %slice-start.1 = ((s8[6684672]{0:T(1024)(128)(4,1)}), s8[4194304]{0:T(1024)(128)(4,1)S(1)}, s32[]{:S(2)}) async-start(s8[6684672]{0:T(1024)(128)(4,1)} %bitcast.108), calls=%async_computation.4 | async-start | bytes 8388608
  371.7 1.4 copy-start.3
  371.7 1.9 copy-start.4
  371.7 3.9 copy-start.1
  375.7 9.5 %copy-start.10 = (bf16[1024,255]{1,0:T(8,128)(2,1)S(1)}, bf16[1024,255]{1,0:T(8,128)(2,1)}, u32[]{:S(2)}) copy-start(bf16[1024,255]{1,0:T(8,128)(2,1)} %copy-done.9) | copy-start | bytes 1566724
  375.7 9.5 %copy-start.27 = (bf16[1024,128]{1,0:T(8,128)(2,1)S(1)}, bf16[1024,128]{1,0:T(8,128)(2,1)}, u32[]{:S(2)}) copy-start(bf16[1024,128]{1,0:T(8,128)(2,1)} %copy-done.26) | copy-start | bytes 786436
  385.1 4.5 copy-start.12
  385.1 4.5 copy-start.25
  389.7 4.5 copy-start.14
  389.7 4.5 copy-start.21
  394.2 4.6 copy-start.15
  394.2 4.6 copy-start.23
  404.2 182.7 %collective-permute-start.3 = (bf16[6,12288]{1,0:T(8,128)(2,1)S(1)}, bf16[6,12288]{1,0:T(8,128)(2,1)S(1)}, u32[]{:S(2)}, u32[]{:S(2)}) collective-permute-start(bf16[6,12288]{1,0:T(8,128)(2,1)S(1)} %slice.448), channel_id=1, source_target_pairs={{1,0},{2,1},{3,2},{4,3},{5,4},{6,5},{7,6},{9,8},{10,9},{11,10},{12... | collective-permute-start | bytes 442376 | tf_op jit(solution)/shard_map/ppermute | solution.py:12
  470.8 1.4 copy-start.42
  470.9 1.4 copy-start.43
  470.9 116.1 %copy-start.2 = (f32[128,4096]{1,0:T(8,128)S(1)}, f32[128,4096]{1,0:T(8,128)}, u32[]{:S(2)}) copy-start(f32[128,4096]{1,0:T(8,128)} %copy-done.1) | copy-start | bytes 6291460
  472.2 200.5 %reduce-scatter.2.cloned.1.call-start = ((), (), s32[]{:S(2)}) async-start(), calls=%async_computation.1 | async-start | bytes 405504 | tf_op jit(solution)/shard_map/reduce_scatter | solution.py:152
  587.0 2.9 copy-start.29
  587.0 2.9 copy-start.31
  587.0 2.9 copy-start.33
  587.0 2.9 copy-start.35
  587.0 2.9 copy-start.37
  587.0 2.9 copy-start.39
  587.0 2.9 copy-start.41
  589.9 82.7 %copy-start.44 = (f32[128]{0:T(128)S(1)}, f32[128]{0:T(128)}, u32[]{:S(2)}) copy-start(f32[128]{0:T(128)} %dynamic-slice.3) | copy-start | bytes 1540
Sparse Core Ops, SparseCore 0:
  472.3 113.8 all-reduce.12
  590.5 82.1 reduce-scatter.1
where the time goes:
time: 717 us; the launch traced here: 711 us
  blocking collectives  219 us (31%)
  waiting for transfers between devices  188 us (26%)
  local copies, waits for them, and re-layouts  180 us (25%)
  matrix products  53.1 us (7%)
  other arithmetic  41.9 us (6%)
  between operations  16.3 us (2%)
  starting transfers between devices  12.6 us (2%)
    unnamed x1, blocking collectives  121 us
    unnamed x3, waiting for transfers between devices  113 us
    reduce_scatter x1, waiting for transfers between devices, local(): lax.psum_scatter(summed[0], 'dp', scatter_dimension=1, tiled=True)  75.1 us
    reshape x4, local copies, waits for them, and re-layouts, toeplitz(): return tiled.reshape(group_count, tok_rows, span_cols)  64.2 us
    reshape x4, local copies, waits for them, and re-layouts, lag_sums(): flat_corr = correlation.reshape(group_count, tok_rows * span_cols)  37.3 us
    psum x1, blocking collectives, local(): summed = lax.psum((short_terms, long_terms, skip_terms), 'seq')  31 us
    unnamed x107, local copies, waits for them, and re-layouts  26.3 us
    all_gather x1, blocking collectives, local(): lax.all_gather(short_filter, 'dp', axis=1, tiled=True)  24.7 us
  transfers between devices with their start and end apart: 6, of which 2 were waited for; matrix products, arithmetic and copies ran while one was open for 28% of the time, Pallas kernels for 0%

commit v1 on v0

v1 whole, which is shorter than its diff:
```python
import functools
import math

import jax
import jax.numpy as jnp
from jax import lax
from jax.experimental import pallas as pl
from jax.experimental.pallas import tpu as pltpu
from jax.sharding import PartitionSpec as P

LANES = 128
GROUP = 16
SHORT = 7
ROWS = 128
PIECE = 16
SPAN = PIECE + 128
BF = jnp.bfloat16
F32 = jnp.float32


def params(mib):
    return pltpu.CompilerParams(vmem_limit_bytes=mib * 1024 * 1024)


def whole():
    return pl.BlockSpec(memory_space=pltpu.VMEM)


def anywhere():
    return pl.BlockSpec(memory_space=pl.ANY)


def pack_kernel(short_ref, long_ref, skip_ref, streams_ref, out_ref, tail_ref, sem):
    copy = pltpu.make_async_copy(streams_ref.at[0, pl.ds(ROWS - 16, 16), :], tail_ref, sem)
    copy.start()
    short = short_ref[...].astype(F32)
    skip = skip_ref[...].astype(F32)
    nothing = jnp.zeros((1, LANES), F32)
    rows = []
    for part in range(3):
        rows.append(short[:, part * LANES : (part + 1) * LANES])
        rows.append(skip if part == 0 else nothing)
    packed = jnp.concatenate(rows + [long_ref[...].astype(F32)], axis=0).astype(BF)
    out_ref[...] = jnp.broadcast_to(packed[None], out_ref.shape)
    copy.wait()


def pack(short_filter, long_filter, skip, streams, shards):
    return pl.pallas_call(
        pack_kernel,
        out_shape=(
            jax.ShapeDtypeStruct((shards, 32, LANES), BF),
            jax.ShapeDtypeStruct((16, streams.shape[2]), BF),
        ),
        in_specs=[whole(), whole(), whole(), anywhere()],
        out_specs=(whole(), anywhere()),
        scratch_shapes=[pltpu.SemaphoreType.DMA],
        compiler_params=params(16),
        name="pack",
    )(short_filter, long_filter, skip[None], streams)


def taps_of(table, tile):
    return table[tile // 3, pl.ds(pl.multiple_of(tile % 3 * 8, 8), 8), :]


def gates_kernel(
    first_tile, tiles, count, g_ref, sq, sk, sv, hq, hk, hv, cot, prod, gate, key, val, table, ext
):
    step = pl.program_id(0)

    @pl.when(step == 0)
    def _():
        table[...] = g_ref[...].astype(F32)

    for t in range(tiles):
        tile = first_tile + step * tiles + t
        cols = slice(t * LANES, (t + 1) * LANES)
        mixed = []
        for part, (source, halo) in enumerate(((sq, hq), (sk, hk), (sv, hv))):
            taps = taps_of(table, tile + part * count)
            slot = ext.at[t % 2, part]
            slot[0:8, :] = halo[:, cols].astype(F32)[8:16]
            slot[8 : 8 + ROWS, :] = source[0, :, cols].astype(F32)
            running = taps[0:1] * slot[8 : 8 + ROWS, :]
            for lag in range(1, SHORT):
                running = running + taps[lag : lag + 1] * slot[8 - lag : 8 - lag + ROWS, :]
            mixed.append(running)
        prod[:, cols] = (mixed[1] * mixed[2]).astype(BF)
        gate[:, cols] = (cot[0, :, cols].astype(F32) * mixed[0]).astype(BF)
        key[:, cols] = mixed[1].astype(BF)
        val[:, cols] = mixed[2].astype(BF)


def gates(first, width, gathered, streams, before, grad_out):
    count = grad_out.shape[2] // LANES
    step_width = min(width, 512)
    steps = width // step_width
    tiles = step_width // LANES
    blocks = grad_out.shape[2] // step_width
    lead = first // step_width

    def stream(part):
        return pl.BlockSpec((1, ROWS, step_width), lambda i: (0, 0, part * blocks + lead + i))

    def halo(part):
        return pl.BlockSpec((16, step_width), lambda i: (0, part * blocks + lead + i))

    out = jax.ShapeDtypeStruct((ROWS, width), BF)
    out_spec = pl.BlockSpec((ROWS, step_width), lambda i: (0, i))
    return pl.pallas_call(
        functools.partial(gates_kernel, first // LANES, tiles, count),
        grid=(steps,),
        out_shape=(out,) * 4,
        in_specs=[pl.BlockSpec(gathered.shape, lambda i: (0, 0, 0))]
        + [stream(part) for part in range(3)]
        + [halo(part) for part in range(3)]
        + [pl.BlockSpec((1, ROWS, step_width), lambda i: (0, 0, lead + i))],
        out_specs=(out_spec,) * 4,
        scratch_shapes=[
            pltpu.VMEM(gathered.shape, F32),
            pltpu.VMEM((2, 3, 8 + ROWS, LANES), F32),
        ],
        compiler_params=params(40),
        cost_estimate=pl.CostEstimate(
            flops=60 * 3 * ROWS * width, bytes_accessed=16 * ROWS * width, transcendentals=0
        ),
        name="gates",
    )(gathered, streams, streams, streams, before, before, before, grad_out)


def windows(block, pair):
    low = 2 * PIECE * pair
    return jnp.concatenate(
        [block[low : low + SPAN], block[low + PIECE : low + PIECE + SPAN]], axis=1
    )


def picked(result, owner):
    out = result[0:PIECE]
    for g in range(1, LANES // GROUP):
        out = jnp.where(owner == g, result[g * PIECE : (g + 1) * PIECE], out)
    return out


def toeplitz_rows(filters, shift):
    pieces = []
    for g in range(LANES // GROUP):
        line = jnp.concatenate([filters[g : g + 1], jnp.zeros((1, LANES), F32)], axis=1)
        line = jnp.broadcast_to(line, (PIECE, 2 * LANES))
        pieces.append(pltpu.roll(line, shift, 1, stride=1, stride_axis=0))
    return jnp.concatenate(pieces, axis=0).astype(BF)[:, :SPAN]


def back_kernel(
    first_tile, tiles, count, chained, g_ref, sq, sk, sv, hq, hk, hv, cot, prod, prior, gate, ahead, key, val, *rest
):
    if chained:
        rest = rest[1:]
    gs_ref, tail_ref, head_ref, short_ref, long_ref, table, mixed, corr, held, sems = rest
    step = pl.program_id(0)
    steps = pl.num_programs(0)
    slot = lax.rem(step, 2)
    width = tiles * LANES
    groups = LANES // GROUP

    def copies(at_step, at_slot):
        return [
            pltpu.make_async_copy(
                held.at[at_slot, part],
                gs_ref.at[0, :, pl.ds(pl.multiple_of((part * count + first_tile + at_step * tiles) * LANES, LANES), width)],
                sems.at[at_slot, part],
            )
            for part in range(3)
        ]

    @pl.when(step == 0)
    def _():
        table[...] = g_ref[...].astype(F32)
        mixed[...] = jnp.zeros(mixed.shape, F32)

    @pl.when(step >= 2)
    def _():
        for copy in copies(step - 2, slot):
            copy.wait()

    lane = lax.broadcasted_iota(jnp.int32, (1, LANES), 1)
    owner = lane // GROUP
    flip = (
        lax.broadcasted_iota(jnp.int32, (LANES, LANES), 0)
        + lax.broadcasted_iota(jnp.int32, (LANES, LANES), 1)
        == LANES - 1
    ).astype(F32).astype(BF)
    upside = (
        lax.broadcasted_iota(jnp.int32, (ROWS, ROWS), 0) ^ (PIECE - 1)
        == lax.broadcasted_iota(jnp.int32, (ROWS, ROWS), 1)
    ).astype(F32).astype(BF)
    owners = [(owner == g).astype(F32).astype(BF) for g in range(groups)]
    owners = [jnp.concatenate([m, m], axis=1) for m in owners]

    for t in range(tiles):
        tile = first_tile + step * tiles + t
        cols = slice(t * LANES, (t + 1) * LANES)
        filters = table[tile, 24:32, :]
        skip = taps_of(table, tile * 3)[7:8]
        flipped = jnp.dot(filters.astype(BF), flip, preferred_element_type=F32)
        forward = toeplitz_rows(flipped, 1)
        backward = toeplitz_rows(filters, 0)
        product = prod[:, cols]
        gated = gate[:, cols]
        context = jnp.concatenate([prior[:, cols], product], axis=0)
        coming = jnp.concatenate([gated, ahead[:, cols]], axis=0)
        turned = jnp.dot(upside, product, preferred_element_type=F32).astype(BF)
        wave, prod_grad = [], []
        lagged = None
        for pair in range(ROWS // (2 * PIECE)):
            low = 2 * PIECE * pair
            result = jnp.dot(forward, windows(context, pair), preferred_element_type=F32)
            wave += [picked(result[:, :LANES], owner), picked(result[:, LANES:], owner)]
            seen = windows(coming, pair)
            result = jnp.dot(backward, seen, preferred_element_type=F32)
            prod_grad += [picked(result[:, :LANES], owner), picked(result[:, LANES:], owner)]
            own = jnp.concatenate([turned[low : low + PIECE], turned[low + PIECE : low + 2 * PIECE]], axis=1)
            masked = jnp.concatenate([own * m for m in owners], axis=0)
            term = lax.dot_general(masked, seen, (((1,), (1,)), ((), ())), preferred_element_type=F32)
            lagged = term if lagged is None else lagged + term
        product = product.astype(F32)
        gated = gated.astype(F32)
        wave = jnp.concatenate(wave, axis=0) + skip * product
        prod_grad = jnp.concatenate(prod_grad, axis=0) + skip * gated
        corr[:, :SPAN] = lagged
        for g in range(groups):
            skewed = pltpu.roll(
                corr[g * PIECE : (g + 1) * PIECE, :], 2 * LANES - PIECE + 1, 1, stride=1, stride_axis=0
            )
            long_ref[t, g : g + 1, :] = jnp.sum(skewed[:, :LANES], axis=0, keepdims=True)
        long_ref[t, 8:9, :] = jnp.sum(gated * product, axis=0, keepdims=True)
        long_ref[t, 9:16, :] = jnp.zeros((7, LANES), F32)
        mixed[0, 8 : 8 + ROWS, :] = cot[0, :, cols].astype(F32) * wave
        mixed[1, 8 : 8 + ROWS, :] = prod_grad * val[:, cols].astype(F32)
        mixed[2, 8 : 8 + ROWS, :] = prod_grad * key[:, cols].astype(F32)
        heads = []
        for part, (source, halo) in enumerate(((sq, hq), (sk, hk), (sv, hv))):
            taps = taps_of(table, tile + part * count)
            feature = mixed.at[part]
            heads.append(feature[8:16, :])
            early = halo[:, cols].astype(F32)[8:16]
            values = source[0, :, cols].astype(F32)
            running = None
            sums = []
            for lag in range(SHORT):
                shifted = feature[8 + lag : 8 + lag + ROWS, :]
                term = taps[lag : lag + 1] * shifted
                running = term if running is None else running + term
                terms = shifted * values
                total = feature[lag : lag + 8, :] * early
                for r in range(ROWS // 8):
                    total = total + terms[r * 8 : (r + 1) * 8]
                sums.append(jnp.sum(total, axis=0, keepdims=True))
            sums.append(jnp.zeros((1, LANES), F32))
            short_ref[part, t, :, :] = jnp.concatenate(sums, axis=0)
            held[slot, part, :, cols] = running.astype(BF)
            tail_ref[part, :, cols] = running[ROWS - 16 :]
        head_ref[0, t * 24 : (t + 1) * 24, :] = jnp.concatenate(heads, axis=0).astype(BF)

    for copy in copies(step, slot):
        copy.start()

    @pl.when(step == steps - 1)
    def _():
        for copy in copies(step, slot):
            copy.wait()

    @pl.when(jnp.logical_and(step == steps - 1, step >= 1))
    def _():
        for copy in copies(step - 1, 1 - slot):
            copy.wait()


def back(first, width, gathered, streams, before, grad_out, made, prior, ahead, grads):
    count = grad_out.shape[2] // LANES
    step_width = min(width, 512)
    steps = width // step_width
    tiles = step_width // LANES
    blocks = grad_out.shape[2] // step_width
    lead = first // step_width
    product, gate, key, value = made

    def stream(part):
        return pl.BlockSpec((1, ROWS, step_width), lambda i: (0, 0, part * blocks + lead + i))

    def halo(part):
        return pl.BlockSpec((16, step_width), lambda i: (0, part * blocks + lead + i))

    local = pl.BlockSpec((ROWS, step_width), lambda i: (0, i))
    chained = grads is not None
    operands = [gathered, streams, streams, streams, before, before, before, grad_out, product, prior, gate, ahead, key, value]
    in_specs = (
        [pl.BlockSpec(gathered.shape, lambda i: (0, 0, 0))]
        + [stream(part) for part in range(3)]
        + [halo(part) for part in range(3)]
        + [pl.BlockSpec((1, ROWS, step_width), lambda i: (0, 0, lead + i))]
        + [local] * 6
    )
    if chained:
        operands.append(grads)
        in_specs.append(anywhere())
    return pl.pallas_call(
        functools.partial(back_kernel, first // LANES, tiles, count, chained),
        grid=(steps,),
        out_shape=(
            jax.ShapeDtypeStruct(streams.shape, BF),
            jax.ShapeDtypeStruct((3, 16, width), F32),
            jax.ShapeDtypeStruct((steps, tiles * 24, LANES), BF),
            jax.ShapeDtypeStruct((3, width // LANES, 8, LANES), F32),
            jax.ShapeDtypeStruct((width // LANES, 16, LANES), F32),
        ),
        in_specs=in_specs,
        out_specs=(
            anywhere(),
            pl.BlockSpec((3, 16, step_width), lambda i: (0, 0, i)),
            pl.BlockSpec((1, tiles * 24, LANES), lambda i: (i, 0, 0)),
            pl.BlockSpec((3, tiles, 8, LANES), lambda i: (0, i, 0, 0)),
            pl.BlockSpec((tiles, 16, LANES), lambda i: (i, 0, 0)),
        ),
        scratch_shapes=[
            pltpu.VMEM(gathered.shape, F32),
            pltpu.VMEM((3, 8 + ROWS + 8, LANES), F32),
            pltpu.VMEM((LANES, 2 * LANES), F32),
            pltpu.VMEM((2, 3, ROWS, step_width), BF),
            pltpu.SemaphoreType.DMA((2, 3)),
        ],
        input_output_aliases={len(operands) - 1: 0} if chained else {},
        compiler_params=params(48),
        cost_estimate=pl.CostEstimate(
            flops=600 * 3 * ROWS * width, bytes_accessed=24 * ROWS * width, transcendentals=0
        ),
        name="back",
    )(*operands)


def finish_kernel(chunks, count, g_ref, *refs):
    tails = refs[:chunks]
    heads = refs[chunks : 2 * chunks]
    _, gs_ref, strip, sem = refs[2 * chunks :]
    per_chunk = count // chunks
    for c in range(chunks):
        steps = heads[c].shape[0]
        per_step = heads[c].shape[1] // 24
        for step in range(steps):
            block = heads[c][step].astype(F32)
            for t in range(per_step):
                here = step * per_step + t
                for part in range(3):
                    tile = part * count + c * per_chunk + here
                    low = 24 * t + 8 * part
                    taps = g_ref[tile // 3].astype(F32)[tile % 3 * 8 : tile % 3 * 8 + 8]
                    after = jnp.concatenate([jnp.zeros((8, LANES), F32), block[low : low + 8]], axis=0)
                    tail = tails[c][part, :, here * LANES : (here + 1) * LANES]
                    last = tail[8:16]
                    for lag in range(1, SHORT):
                        last = last + taps[lag : lag + 1] * after[lag : lag + 8]
                    strip[:, tile * LANES : (tile + 1) * LANES] = jnp.concatenate([tail[0:8], last], axis=0).astype(BF)
    copy = pltpu.make_async_copy(strip, gs_ref.at[0, pl.ds(ROWS - 16, 16), :], sem)
    copy.start()
    copy.wait()


def finish(gathered, tails, heads, grads):
    chunks = len(tails)
    count = grads.shape[2] // LANES // 3
    return pl.pallas_call(
        functools.partial(finish_kernel, chunks, count),
        out_shape=jax.ShapeDtypeStruct(grads.shape, BF),
        in_specs=[whole()] * (1 + 2 * chunks) + [anywhere()],
        out_specs=anywhere(),
        scratch_shapes=[pltpu.VMEM((16, grads.shape[2]), BF), pltpu.SemaphoreType.DMA],
        input_output_aliases={1 + 2 * chunks: 0},
        compiler_params=params(32),
        cost_estimate=pl.CostEstimate(flops=10000000, bytes_accessed=2000000, transcendentals=0),
        name="finish",
    )(gathered, *tails, *heads, grads)


def bundle_kernel(chunks, shards, *refs):
    shorts, longs, out_ref = refs[:chunks], refs[chunks : 2 * chunks], refs[2 * chunks]
    per_chunk = shards // chunks

    def short(tile):
        part, here = divmod(tile, shards)
        return shorts[here // per_chunk][part, here % per_chunk]

    for d in range(shards):
        long = longs[d // per_chunk][d % per_chunk]
        rows = [short(3 * d)[0:7], long[8:9], short(3 * d + 1), short(3 * d + 2), long[0:8]]
        out_ref[d] = jnp.concatenate(rows, axis=0).astype(BF)


def bundle(shorts, longs, shards):
    chunks = len(shorts)
    return pl.pallas_call(
        functools.partial(bundle_kernel, chunks, shards),
        out_shape=jax.ShapeDtypeStruct((shards, 32, LANES), BF),
        in_specs=[whole()] * (2 * chunks),
        out_specs=whole(),
        compiler_params=params(16),
        name="bundle",
    )(*shorts, *longs)


def total_kernel(parts_ref, out_ref):
    out_ref[...] = jnp.sum(parts_ref[...].astype(F32), axis=0)


def total(parts):
    return pl.pallas_call(
        total_kernel,
        out_shape=jax.ShapeDtypeStruct(parts.shape[1:], F32),
        in_specs=[whole()],
        out_specs=whole(),
        compiler_params=params(16),
        name="total",
    )(parts)


def spread_kernel(scale, place_ref, *refs):
    parts, (short_ref, long_ref, skip_ref, held) = refs[:-4], refs[-4:]
    count = len(parts)
    for i in range(count):
        held[i] = parts[i][...]
    summed = None
    for device in range(count):
        part = held[lax.rem(place_ref[0] - device + count, count)]
        summed = part if summed is None else summed + part
    summed = summed * scale
    for part in range(3):
        short_ref[:, part * LANES : (part + 1) * LANES] = summed[8 * part : 8 * part + SHORT]
    long_ref[...] = summed[24:32]
    skip_ref[...] = summed[7:8]


def spread(place, parts, scale):
    return pl.pallas_call(
        functools.partial(spread_kernel, scale),
        out_shape=(
            jax.ShapeDtypeStruct((SHORT, 3 * LANES), F32),
            jax.ShapeDtypeStruct((8, LANES), F32),
            jax.ShapeDtypeStruct((1, LANES), F32),
        ),
        in_specs=[pl.BlockSpec(memory_space=pltpu.SMEM)] + [whole()] * len(parts),
        out_specs=(whole(),) * 3,
        scratch_shapes=[pltpu.VMEM((len(parts), 32, LANES), F32)],
        compiler_params=params(16),
        name="spread",
    )(place, *parts)


def passed_along(block, axis, distance):
    devices = range(lax.axis_size(axis))
    route = [(i - distance, i) for i in devices if i - distance in devices]
    return lax.ppermute(block, axis, route)


CHUNKS = 4


def local(streams, short_filter, long_filter, skip, grad_out):
    shards = lax.axis_size("dp")
    ring = lax.axis_size("seq")
    width = grad_out.shape[2] // CHUNKS
    payload, tail_rows = pack(short_filter, long_filter, skip, streams, shards)
    before = passed_along(tail_rows, "seq", 1)
    gathered = lax.all_to_all(payload, "dp", 0, 0, tiled=True)
    made = [gates(c * width, width, gathered, streams, before, grad_out) for c in range(CHUNKS)]
    prior = [passed_along(m[0], "seq", 1) for m in made]
    ahead = [passed_along(m[1], "seq", -1) for m in made]
    grads = None
    tails, heads, shorts, longs = [], [], [], []
    for c in range(CHUNKS):
        grads, tail, head, short, long = back(
            c * width, width, gathered, streams, before, grad_out, made[c], prior[c], ahead[c], grads
        )
        tails.append(tail)
        heads.append(head)
        shorts.append(short)
        longs.append(long)
    after = [passed_along(head, "seq", -1) for head in heads]
    grads = finish(gathered, tails, after, grads)
    own = total(lax.all_to_all(bundle(shorts, longs, shards), "dp", 0, 0, tiled=True))
    parts = [own]
    for distance in range(1, ring):
        parts.append(lax.ppermute(own, "seq", [(i, (i + distance) % ring) for i in range(ring)]))
    scale = 1.0 / math.sqrt(shards * ring * streams.shape[1])
    place = lax.axis_index("seq").astype(jnp.int32)[None]
    grad_short, grad_long, grad_skip = spread(place, parts, scale)
    return grads, grad_short, grad_long, grad_skip[0]


def solution(mesh):
    placed = (P("dp", "seq", None), P(None, "dp"), P("dp", None), P("dp"), P("dp", "seq", None))
    return jax.shard_map(
        local,
        mesh=mesh,
        in_specs=placed,
        out_specs=(P("dp", "seq", None), P(None, "dp"), P("dp", None), P("dp")),
        check_vma=False,
    )
```

time: 717 us -> 122 us (0.17)
  blocking collectives: 219 us -> 15.1 us
  waiting for transfers between devices: 188 us -> 5.15 us
  local copies, waits for them, and re-layouts: 180 us -> 5.15 us
  matrix products: 53.1 us -> 0 us
  starting transfers between devices: 12.6 us -> 60.2 us
  other arithmetic: 41.9 us -> 0 us
  Pallas kernels: 0 us -> 34.4 us
  between operations: 16.3 us -> 0.95 us
    unnamed x1 -> x0, blocking collectives: 121 us -> none
    unnamed x3 -> x0, waiting for transfers between devices: 113 us -> none
    reshape x16 -> x0, local copies, waits for them, and re-layouts: 112 us -> none  [the longest x4 64.2 us: toeplitz(): return tiled.reshape(group_count, tok_rows, span_cols)]
    reduce_scatter x1 -> x0, waiting for transfers between devices: 75.1 us -> none  [local(): lax.psum_scatter(summed[0], 'dp', scatter_dimension=1, tiled=True)]
    all_gather x3 -> x0, blocking collectives: 67.4 us -> none  [the longest x1 24.7 us: local(): lax.all_gather(short_filter, 'dp', axis=1, tiled=True)]
    dot_general x16 -> x0, matrix products: 53.1 us -> none  [the longest x4 18.1 us: lag_sums(): jnp.einsum('gks,gkm->gsm', gate_part, context_part, preferred_element_typ...]
    pallas_call x0 -> x13, Pallas kernels: none -> 34.4 us  [the longest x4 25.8 us: back(): pl.pallas_call(functools.partial(back_kernel, first // LANES, tiles, coun...]
    psum x1 -> x0, blocking collectives: 31 us -> none  [local(): summed = lax.psum((short_terms, long_terms, skip_terms), 'seq')]
  transfers between devices with their start and end apart: 6 -> 21, of which waited for: 2 -> 2; matrix products, arithmetic and copies ran while one was open for 28% -> 0% of each run, Pallas kernels for 0% -> 21%
where the time goes in v1:
time: 122 us; the launch traced here: 121 us
  starting transfers between devices  60.2 us (49%)
  Pallas kernels  34.4 us (28%)
  blocking collectives  15.1 us (12%)
  local copies, waits for them, and re-layouts  5.15 us (4%)
  waiting for transfers between devices  5.15 us (4%)
    ppermute x13, starting transfers between devices, passed_along(): return lax.ppermute(block, axis, route)  33.1 us
    pallas_call x4, Pallas kernels, back(): pl.pallas_call(functools.partial(back_kernel, first // LANES, tiles, coun...  25.8 us
    ppermute x7, starting transfers between devices, local(): lax.ppermute(own, 'seq', [(i, (i + distance) % ring) for i in range(ring)])  22.1 us
    all_to_all x1, blocking collectives, local(): gathered = lax.all_to_all(payload, 'dp', 0, 0, tiled=True)  15.1 us
    pallas_call x4, Pallas kernels, gates(): pl.pallas_call(functools.partial(gates_kernel, first // LANES, tiles, cou...  5.65 us
    unnamed x14, local copies, waits for them, and re-layouts  5.15 us
    all_to_all x1, starting transfers between devices, local(): lax.all_to_all(bundle(shorts, longs, shards), 'dp', 0, 0, tiled=True)  4.98 us
    all_to_all x1, waiting for transfers between devices, local(): lax.all_to_all(bundle(shorts, longs, shards), 'dp', 0, 0, tiled=True)  2.59 us
  transfers between devices with their start and end apart: 21, of which 2 were waited for; matrix products, arithmetic and copies ran while one was open for 0% of the time, Pallas kernels for 21%

profile of v1, /device:TPU:2, one launch (start us, length us, event | category | flops | bytes accessed | tf_op | source)
XLA Modules:
  0.0 121.0 jit_solution(9578149884604526947)
XLA Ops:
  0.6 0.0 copy-start
  0.6 1.9 %copy-done = bf16[1,128,12288]{2,1,0:T(8,128)(2,1)S(1)} copy-done((bf16[1,128,12288]{2,1,0:T(8,128)(2,1)S(1)}, bf16[1,128,12288]{2,1,0:T(8,128)(2,1)}, u32[]{:S(2)}) %copy-start) | copy-done | bytes 3145752
  2.5 0.7 copy-done.4
  3.2 0.7 copy-done.5
  3.9 0.7 copy-done.6
  4.6 0.2 pack.1
  4.8 4.0 %collective-permute-start = (bf16[16,12288]{1,0:T(8,128)(2,1)S(1)}, bf16[16,12288]{1,0:T(8,128)(2,1)S(1)}, u32[]{:S(2)}, u32[]{:S(2)}) collective-permute-start(bf16[16,12288]{1,0:T(8,128)(2,1)S(1)} %get-tuple-element.46), channel_id=1, source_target_pairs={{0,1},{1,2},{2,3},{3,4},{4,5},{5,6},{6,7},{8,9},{9,10},{10,11},{11... | collective-permute-start | bytes 1179656 | tf_op jit(solution)/shard_map/ppermute | solution.py:461
  8.8 15.1 %all_to_all.10.g_ref = bf16[32,32,128]{2,1,0:T(8,128)(2,1)S(1)} all-to-all(bf16[32,32,128]{2,1,0:T(8,128)(2,1)S(1)} %get-tuple-element.45), channel_id=1, replica_groups=mesh['dp'=32,'seq'=8] {'dp'}, dimensions={0} | all-to-all | bytes 524288 | tf_op jit(solution)/shard_map/all_to_all | solution.py:473
  23.9 0.0 collective-permute-done.hq.hk.hv
  23.9 1.2 %copy-done.2 = bf16[1,128,4096]{2,1,0:T(8,128)(2,1)S(1)} copy-done((bf16[1,128,4096]{2,1,0:T(8,128)(2,1)S(1)}, bf16[1,128,4096]{2,1,0:T(8,128)(2,1)}, u32[]{:S(2)}) %copy-start.2) | copy-done | bytes 1048600
  25.1 1.4 %gates.4 = (bf16[128,1024]{1,0:T(8,128)(2,1)S(1)}, bf16[128,1024]{1,0:T(8,128)(2,1)S(1)}, bf16[128,1024]{1,0:T(8,128)(2,1)S(1)}, bf16[128,1024]{1,0:T(8,128)(2,1)S(1)}) custom-call(bf16[32,32,128]{2,1,0:T(8,128)(2,1)S(1)} %all_to_all.10.g_ref, bf16[1,128,12288]{2,1,0:T(8,128)(2,1)S(1)} %copy-done.1, bf16[1,128,12288]{2,1,0:T(8,128)(2,1)S(1)} %copy-done.1, ...), custom_call_target="tpu_custom_call" | custom-call | flops 23592960 | bytes 2097152 | tf_op jit(solution)/shard_map/gates/pallas_call | solution.py:111
  26.5 3.8 %collective-permute-start.1 = (bf16[128,1024]{1,0:T(8,128)(2,1)S(1)}, bf16[128,1024]{1,0:T(8,128)(2,1)S(1)}, u32[]{:S(2)}, u32[]{:S(2)}) collective-permute-start(bf16[128,1024]{1,0:T(8,128)(2,1)S(1)} %get-tuple-element.47.prod), channel_id=1, source_target_pairs={{0,1},{1,2},{2,3},{3,4},{4,5},{5,6},{6,7},{8,9},{9,10},{10,11},{11... | collective-permute-start | bytes 786440 | tf_op jit(solution)/shard_map/ppermute | solution.py:461
  30.3 1.3 %collective-permute-start.2 = (bf16[128,1024]{1,0:T(8,128)(2,1)S(1)}, bf16[128,1024]{1,0:T(8,128)(2,1)S(1)}, u32[]{:S(2)}, u32[]{:S(2)}) collective-permute-start(bf16[128,1024]{1,0:T(8,128)(2,1)S(1)} %get-tuple-element.48.gate), channel_id=1, source_target_pairs={{1,0},{2,1},{3,2},{4,3},{5,4},{6,5},{7,6},{9,8},{10,9},{11,10},{12... | collective-permute-start | bytes 786440 | tf_op jit(solution)/shard_map/ppermute | solution.py:461
  31.6 1.4 %gates.5 = (bf16[128,1024]{1,0:T(8,128)(2,1)S(1)}, bf16[128,1024]{1,0:T(8,128)(2,1)S(1)}, bf16[128,1024]{1,0:T(8,128)(2,1)S(1)}, bf16[128,1024]{1,0:T(8,128)(2,1)S(1)}) custom-call(bf16[32,32,128]{2,1,0:T(8,128)(2,1)S(1)} %all_to_all.10.g_ref, bf16[1,128,12288]{2,1,0:T(8,128)(2,1)S(1)} %copy-done.1, bf16[1,128,12288]{2,1,0:T(8,128)(2,1)S(1)} %copy-done.1, ...), custom_call_target="tpu_custom_call" | custom-call | flops 23592960 | bytes 2097152 | tf_op jit(solution)/shard_map/gates/pallas_call | solution.py:111
  33.0 4.6 %collective-permute-start.3 = (bf16[128,1024]{1,0:T(8,128)(2,1)S(1)}, bf16[128,1024]{1,0:T(8,128)(2,1)S(1)}, u32[]{:S(2)}, u32[]{:S(2)}) collective-permute-start(bf16[128,1024]{1,0:T(8,128)(2,1)S(1)} %get-tuple-element.52.prod), channel_id=1, source_target_pairs={{0,1},{1,2},{2,3},{3,4},{4,5},{5,6},{6,7},{8,9},{9,10},{10,11},{11... | collective-permute-start | bytes 786440 | tf_op jit(solution)/shard_map/ppermute | solution.py:461
  37.6 1.3 %collective-permute-start.4 = (bf16[128,1024]{1,0:T(8,128)(2,1)S(1)}, bf16[128,1024]{1,0:T(8,128)(2,1)S(1)}, u32[]{:S(2)}, u32[]{:S(2)}) collective-permute-start(bf16[128,1024]{1,0:T(8,128)(2,1)S(1)} %get-tuple-element.53.gate), channel_id=1, source_target_pairs={{1,0},{2,1},{3,2},{4,3},{5,4},{6,5},{7,6},{9,8},{10,9},{11,10},{12... | collective-permute-start | bytes 786440 | tf_op jit(solution)/shard_map/ppermute | solution.py:461
  38.9 1.4 %gates.6 = (bf16[128,1024]{1,0:T(8,128)(2,1)S(1)}, bf16[128,1024]{1,0:T(8,128)(2,1)S(1)}, bf16[128,1024]{1,0:T(8,128)(2,1)S(1)}, bf16[128,1024]{1,0:T(8,128)(2,1)S(1)}) custom-call(bf16[32,32,128]{2,1,0:T(8,128)(2,1)S(1)} %all_to_all.10.g_ref, bf16[1,128,12288]{2,1,0:T(8,128)(2,1)S(1)} %copy-done.1, bf16[1,128,12288]{2,1,0:T(8,128)(2,1)S(1)} %copy-done.1, ...), custom_call_target="tpu_custom_call" | custom-call | flops 23592960 | bytes 2097152 | tf_op jit(solution)/shard_map/gates/pallas_call | solution.py:111
  40.3 5.6 %collective-permute-start.5 = (bf16[128,1024]{1,0:T(8,128)(2,1)S(1)}, bf16[128,1024]{1,0:T(8,128)(2,1)S(1)}, u32[]{:S(2)}, u32[]{:S(2)}) collective-permute-start(bf16[128,1024]{1,0:T(8,128)(2,1)S(1)} %get-tuple-element.58.prod), channel_id=1, source_target_pairs={{0,1},{1,2},{2,3},{3,4},{4,5},{5,6},{6,7},{8,9},{9,10},{10,11},{11... | collective-permute-start | bytes 786440 | tf_op jit(solution)/shard_map/ppermute | solution.py:461
  45.9 0.0 collective-permute-done.1.prior
  45.9 0.0 copy-start.3
  45.9 1.4 %collective-permute-start.6 = (bf16[128,1024]{1,0:T(8,128)(2,1)S(1)}, bf16[128,1024]{1,0:T(8,128)(2,1)S(1)}, u32[]{:S(2)}, u32[]{:S(2)}) collective-permute-start(bf16[128,1024]{1,0:T(8,128)(2,1)S(1)} %get-tuple-element.59.gate), channel_id=1, source_target_pairs={{1,0},{2,1},{3,2},{4,3},{5,4},{6,5},{7,6},{9,8},{10,9},{11,10},{12... | collective-permute-start | bytes 786440 | tf_op jit(solution)/shard_map/ppermute | solution.py:461
  47.4 1.4 %gates.7 = (bf16[128,1024]{1,0:T(8,128)(2,1)S(1)}, bf16[128,1024]{1,0:T(8,128)(2,1)S(1)}, bf16[128,1024]{1,0:T(8,128)(2,1)S(1)}, bf16[128,1024]{1,0:T(8,128)(2,1)S(1)}) custom-call(bf16[32,32,128]{2,1,0:T(8,128)(2,1)S(1)} %all_to_all.10.g_ref, bf16[1,128,12288]{2,1,0:T(8,128)(2,1)S(1)} %copy-done.1, bf16[1,128,12288]{2,1,0:T(8,128)(2,1)S(1)} %copy-done.1, ...), custom_call_target="tpu_custom_call" | custom-call | flops 23592960 | bytes 2097152 | tf_op jit(solution)/shard_map/gates/pallas_call | solution.py:111
  48.8 0.0 collective-permute-done.2.ahead
  48.8 4.6 %collective-permute-start.7 = (bf16[128,1024]{1,0:T(8,128)(2,1)S(1)}, bf16[128,1024]{1,0:T(8,128)(2,1)S(1)}, u32[]{:S(2)}, u32[]{:S(2)}) collective-permute-start(bf16[128,1024]{1,0:T(8,128)(2,1)S(1)} %get-tuple-element.64.prod), channel_id=1, source_target_pairs={{0,1},{1,2},{2,3},{3,4},{4,5},{5,6},{6,7},{8,9},{9,10},{10,11},{11... | collective-permute-start | bytes 786440 | tf_op jit(solution)/shard_map/ppermute | solution.py:461
  53.4 0.0 collective-permute-done.3.prior
  53.4 1.5 %collective-permute-start.8 = (bf16[128,1024]{1,0:T(8,128)(2,1)S(1)}, bf16[128,1024]{1,0:T(8,128)(2,1)S(1)}, u32[]{:S(2)}, u32[]{:S(2)}) collective-permute-start(bf16[128,1024]{1,0:T(8,128)(2,1)S(1)} %get-tuple-element.65.gate), channel_id=1, source_target_pairs={{1,0},{2,1},{3,2},{4,3},{5,4},{6,5},{7,6},{9,8},{10,9},{11,10},{12... | collective-permute-start | bytes 786440 | tf_op jit(solution)/shard_map/ppermute | solution.py:461
  54.9 0.0 copy-done.3
  54.9 6.4 %back.4 = (bf16[1,128,12288]{2,1,0:T(8,128)(2,1)}, f32[3,16,1024]{2,1,0:T(8,128)S(1)}, bf16[2,96,128]{2,1,0:T(8,128)(2,1)S(1)}, f32[3,8,8,128]{3,2,1,0:T(8,128)S(1)}, f32[8,16,128]{2,1,0:T(8,128)S(1)}) custom-call(bf16[32,32,128]{2,1,0:T(8,128)(2,1)S(1)} %all_to_all.10.g_ref, bf16[1,128,12288]{2,1,0:T(8,128)(2,1)} %sv.15, bf16[1,128,12288]{2,1,0:T(8,128)(2,1)} %sv.15, ...), custom_call_target="tpu_custom_call" | custom-call | flops 235929600 | bytes 3145728 | tf_op jit(solution)/shard_map/back/pallas_call | solution.py:308
  61.3 0.0 collective-permute-done.4.ahead
  61.3 6.4 %back.5 = (bf16[1,128,12288]{2,1,0:T(8,128)(2,1)}, f32[3,16,1024]{2,1,0:T(8,128)S(1)}, bf16[2,96,128]{2,1,0:T(8,128)(2,1)S(1)}, f32[3,8,8,128]{3,2,1,0:T(8,128)S(1)}, f32[8,16,128]{2,1,0:T(8,128)S(1)}) custom-call(bf16[32,32,128]{2,1,0:T(8,128)(2,1)S(1)} %all_to_all.10.g_ref, bf16[1,128,12288]{2,1,0:T(8,128)(2,1)} %sv.15, ...), custom_call_target="tpu_custom_call", output_to_operand_aliasing={{0}: (14, {})} | custom-call | flops 235929600 | bytes 3145728 | tf_op jit(solution)/shard_map/back/pallas_call | solution.py:308
  67.8 0.0 collective-permute-done.5.prior
  67.8 0.0 collective-permute-done.6.ahead
  67.8 6.5 %back.6 = (bf16[1,128,12288]{2,1,0:T(8,128)(2,1)}, f32[3,16,1024]{2,1,0:T(8,128)S(1)}, bf16[2,96,128]{2,1,0:T(8,128)(2,1)S(1)}, f32[3,8,8,128]{3,2,1,0:T(8,128)S(1)}, f32[8,16,128]{2,1,0:T(8,128)S(1)}) custom-call(bf16[32,32,128]{2,1,0:T(8,128)(2,1)S(1)} %all_to_all.10.g_ref, bf16[1,128,12288]{2,1,0:T(8,128)(2,1)} %sv.15, ...), custom_call_target="tpu_custom_call", output_to_operand_aliasing={{0}: (14, {})} | custom-call | flops 235929600 | bytes 3145728 | tf_op jit(solution)/shard_map/back/pallas_call | solution.py:308
  74.3 0.0 collective-permute-done.7.prior
  74.3 0.0 collective-permute-done.8.ahead
  74.3 6.5 %back.7 = (bf16[1,128,12288]{2,1,0:T(8,128)(2,1)}, f32[3,16,1024]{2,1,0:T(8,128)S(1)}, bf16[2,96,128]{2,1,0:T(8,128)(2,1)S(1)}, f32[3,8,8,128]{3,2,1,0:T(8,128)S(1)}, f32[8,16,128]{2,1,0:T(8,128)S(1)}) custom-call(bf16[32,32,128]{2,1,0:T(8,128)(2,1)S(1)} %all_to_all.10.g_ref, bf16[1,128,12288]{2,1,0:T(8,128)(2,1)} %sv.15, ...), custom_call_target="tpu_custom_call", output_to_operand_aliasing={{0}: (14, {})} | custom-call | flops 235929600 | bytes 3145728 | tf_op jit(solution)/shard_map/back/pallas_call | solution.py:308
  80.8 0.7 bundle.1
  81.5 5.0 %all-to-all-start.1 = ((bf16[32,32,128]{2,1,0:T(8,128)(2,1)}), bf16[32,32,128]{2,1,0:T(8,128)(2,1)S(1)}, u32[]{:S(2)}, u32[]{:S(2)}) async-start(bf16[32,32,128]{2,1,0:T(8,128)(2,1)} %bundle.1), calls=%async_computation.1 | async-start | bytes 524288 | tf_op jit(solution)/shard_map/all_to_all | solution.py:489
  86.5 1.3 %collective-permute-start.12 = (bf16[2,96,128]{2,1,0:T(8,128)(2,1)S(1)}, bf16[2,96,128]{2,1,0:T(8,128)(2,1)S(1)}, u32[]{:S(2)}, u32[]{:S(2)}) collective-permute-start(bf16[2,96,128]{2,1,0:T(8,128)(2,1)S(1)} %get-tuple-element.73), channel_id=1, source_target_pairs={{1,0},{2,1},{3,2},{4,3},{5,4},{6,5},{7,6},{9,8},{10,9},{11,10},{12... | collective-permute-start | bytes 147464 | tf_op jit(solution)/shard_map/ppermute | solution.py:461
  87.8 1.3 %collective-permute-start.11 = (bf16[2,96,128]{2,1,0:T(8,128)(2,1)S(1)}, bf16[2,96,128]{2,1,0:T(8,128)(2,1)S(1)}, u32[]{:S(2)}, u32[]{:S(2)}) collective-permute-start(bf16[2,96,128]{2,1,0:T(8,128)(2,1)S(1)} %get-tuple-element.72), channel_id=1, source_target_pairs={{1,0},{2,1},{3,2},{4,3},{5,4},{6,5},{7,6},{9,8},{10,9},{11,10},{12... | collective-permute-start | bytes 147464 | tf_op jit(solution)/shard_map/ppermute | solution.py:461
  89.1 1.3 %collective-permute-start.10 = (bf16[2,96,128]{2,1,0:T(8,128)(2,1)S(1)}, bf16[2,96,128]{2,1,0:T(8,128)(2,1)S(1)}, u32[]{:S(2)}, u32[]{:S(2)}) collective-permute-start(bf16[2,96,128]{2,1,0:T(8,128)(2,1)S(1)} %get-tuple-element.71), channel_id=1, source_target_pairs={{1,0},{2,1},{3,2},{4,3},{5,4},{6,5},{7,6},{9,8},{10,9},{11,10},{12... | collective-permute-start | bytes 147464 | tf_op jit(solution)/shard_map/ppermute | solution.py:461
  90.4 1.3 %collective-permute-start.9 = (bf16[2,96,128]{2,1,0:T(8,128)(2,1)S(1)}, bf16[2,96,128]{2,1,0:T(8,128)(2,1)S(1)}, u32[]{:S(2)}, u32[]{:S(2)}) collective-permute-start(bf16[2,96,128]{2,1,0:T(8,128)(2,1)S(1)} %get-tuple-element.70), channel_id=1, source_target_pairs={{1,0},{2,1},{3,2},{4,3},{5,4},{6,5},{7,6},{9,8},{10,9},{11,10},{12... | collective-permute-start | bytes 147464 | tf_op jit(solution)/shard_map/ppermute | solution.py:461
  91.7 2.6 %all-to-all-done.1.parts_ref = bf16[32,32,128]{2,1,0:T(8,128)(2,1)S(1)} async-done(((bf16[32,32,128]{2,1,0:T(8,128)(2,1)}), bf16[32,32,128]{2,1,0:T(8,128)(2,1)S(1)}, u32[]{:S(2)}, u32[]{:S(2)}) %all-to-all-start.1) | async-done | bytes 262176 | tf_op jit(solution)/shard_map/all_to_all | solution.py:489
  94.3 0.1 total.1.refs_0_
  94.3 2.9 %collective-permute-start.13 = (f32[32,128]{1,0:T(8,128)S(1)}, f32[32,128]{1,0:T(8,128)S(1)}, u32[]{:S(2)}, u32[]{:S(2)}) collective-permute-start(f32[32,128]{1,0:T(8,128)S(1)} %total.1.refs_0_), channel_id=1, source_target_pairs={{0,1},{1,2},{2,3},{3,4},{4,5},{5,6},{6,7},{7,0},{8,9},{9,10},{10,1... | collective-permute-start | bytes 49160 | tf_op jit(solution)/shard_map/ppermute | solution.py:492
  97.2 0.0 collective-permute-done.12.refs_7_
  97.2 5.9 %collective-permute-start.14 = (f32[32,128]{1,0:T(8,128)S(1)}, f32[32,128]{1,0:T(8,128)S(1)}, u32[]{:S(2)}, u32[]{:S(2)}) collective-permute-start(f32[32,128]{1,0:T(8,128)S(1)} %total.1.refs_0_), channel_id=1, source_target_pairs={{0,2},{1,3},{2,4},{3,5},{4,6},{5,7},{6,0},{7,1},{8,10},{9,11},{10,... | collective-permute-start | bytes 49160 | tf_op jit(solution)/shard_map/ppermute | solution.py:492
  103.1 0.0 collective-permute-done.11.refs_6_
  103.1 6.1 %collective-permute-start.15 = (f32[32,128]{1,0:T(8,128)S(1)}, f32[32,128]{1,0:T(8,128)S(1)}, u32[]{:S(2)}, u32[]{:S(2)}) collective-permute-start(f32[32,128]{1,0:T(8,128)S(1)} %total.1.refs_0_), channel_id=1, source_target_pairs={{0,3},{1,4},{2,5},{3,6},{4,7},{5,0},{6,1},{7,2},{8,11},{9,12},{10,... | collective-permute-start | bytes 49160 | tf_op jit(solution)/shard_map/ppermute | solution.py:492
  109.2 0.0 collective-permute-done.10.refs_5_
  109.2 1.8 %collective-permute-start.16 = (f32[32,128]{1,0:T(8,128)S(1)}, f32[32,128]{1,0:T(8,128)S(1)}, u32[]{:S(2)}, u32[]{:S(2)}) collective-permute-start(f32[32,128]{1,0:T(8,128)S(1)} %total.1.refs_0_), channel_id=1, source_target_pairs={{0,4},{1,5},{2,6},{3,7},{4,0},{5,1},{6,2},{7,3},{8,12},{9,13},{10,... | collective-permute-start | bytes 49160 | tf_op jit(solution)/shard_map/ppermute | solution.py:492
  111.0 0.0 collective-permute-done.9.refs_4_
  111.0 4.7 %collective-permute-start.17 = (f32[32,128]{1,0:T(8,128)S(1)}, f32[32,128]{1,0:T(8,128)S(1)}, u32[]{:S(2)}, u32[]{:S(2)}) collective-permute-start(f32[32,128]{1,0:T(8,128)S(1)} %total.1.refs_0_), channel_id=1, source_target_pairs={{0,5},{1,6},{2,7},{3,0},{4,1},{5,2},{6,3},{7,4},{8,13},{9,14},{10,... | collective-permute-start | bytes 49160 | tf_op jit(solution)/shard_map/ppermute | solution.py:492
  115.7 0.0 collective-permute-done.13.refs_1_
  115.7 0.7 collective-permute-start.18
  116.4 0.0 collective-permute-done.14.refs_2_
  116.4 0.1 collective-permute-start.19
  116.4 1.3 %finish.1 = bf16[1,128,12288]{2,1,0:T(8,128)(2,1)} custom-call(bf16[32,32,128]{2,1,0:T(8,128)(2,1)S(1)} %all_to_all.10.g_ref, f32[3,16,1024]{2,1,0:T(8,128)S(1)} %get-tuple-element.51.refs_0_, f32[3,16,1024]{2,1,0:T(8,128)S(1)} %get-tuple-element.57.refs_1_, f32[3,16,1024]{2,1,0:T(8,128)S(1)} %get-tuple-element.63.refs_2_, ...), custom_call_target="tpu_custom_call", output_to_operand_aliasing={{}: (9, {})} | custom-call | flops 10000000 | bytes 2000000 | tf_op jit(solution)/shard_map/finish/pallas_call | solution.py:372
  117.8 0.0 collective-permute-done.15.refs_3_
  117.8 0.0 collective-permute-done.16.refs_4_
  117.8 0.0 collective-permute-done.17.refs_5_
  117.8 2.5 %collective-permute-done.18.refs_6_ = f32[32,128]{1,0:T(8,128)S(1)} collective-permute-done((f32[32,128]{1,0:T(8,128)S(1)}, f32[32,128]{1,0:T(8,128)S(1)}, u32[]{:S(2)}, u32[]{:S(2)}) %collective-permute-start.18) | collective-permute-done | bytes 16416 | tf_op jit(solution)/shard_map/ppermute | solution.py:492
  120.3 0.0 collective-permute-done.19.refs_7_
  120.3 0.6 spread.1
  (6 shorter events, 0.0 us)
Async XLA Ops:
  0.6 1.9 %copy-start = (bf16[1,128,12288]{2,1,0:T(8,128)(2,1)S(1)}, bf16[1,128,12288]{2,1,0:T(8,128)(2,1)}, u32[]{:S(2)}) copy-start(bf16[1,128,12288]{2,1,0:T(8,128)(2,1)} %sv.15) | copy-start | bytes 9437188
  2.5 0.7 copy-start.4
  3.2 0.7 copy-start.5
  3.9 0.7 copy-start.6
  4.6 19.3 %copy-start.1 = (bf16[1,128,12288]{2,1,0:T(8,128)(2,1)S(1)}, bf16[1,128,12288]{2,1,0:T(8,128)(2,1)}, u32[]{:S(2)}) copy-start(bf16[1,128,12288]{2,1,0:T(8,128)(2,1)} %sv.15) | copy-start | bytes 9437188
  4.8 19.1 %collective-permute-start = (bf16[16,12288]{1,0:T(8,128)(2,1)S(1)}, bf16[16,12288]{1,0:T(8,128)(2,1)S(1)}, u32[]{:S(2)}, u32[]{:S(2)}) collective-permute-start(bf16[16,12288]{1,0:T(8,128)(2,1)S(1)} %get-tuple-element.46), channel_id=1, source_target_pairs={{0,1},{1,2},{2,3},{3,4},{4,5},{5,6},{6,7},{8,9},{9,10},{10,11},{11... | collective-permute-start | bytes 1179656 | tf_op jit(solution)/shard_map/ppermute | solution.py:461
  23.9 1.2 %copy-start.2 = (bf16[1,128,4096]{2,1,0:T(8,128)(2,1)S(1)}, bf16[1,128,4096]{2,1,0:T(8,128)(2,1)}, u32[]{:S(2)}) copy-start(bf16[1,128,4096]{2,1,0:T(8,128)(2,1)} %cot.15) | copy-start | bytes 3145732
  26.5 19.4 %collective-permute-start.1 = (bf16[128,1024]{1,0:T(8,128)(2,1)S(1)}, bf16[128,1024]{1,0:T(8,128)(2,1)S(1)}, u32[]{:S(2)}, u32[]{:S(2)}) collective-permute-start(bf16[128,1024]{1,0:T(8,128)(2,1)S(1)} %get-tuple-element.47.prod), channel_id=1, source_target_pairs={{0,1},{1,2},{2,3},{3,4},{4,5},{5,6},{6,7},{8,9},{9,10},{10,11},{11... | collective-permute-start | bytes 786440 | tf_op jit(solution)/shard_map/ppermute | solution.py:461
  30.3 18.5 %collective-permute-start.2 = (bf16[128,1024]{1,0:T(8,128)(2,1)S(1)}, bf16[128,1024]{1,0:T(8,128)(2,1)S(1)}, u32[]{:S(2)}, u32[]{:S(2)}) collective-permute-start(bf16[128,1024]{1,0:T(8,128)(2,1)S(1)} %get-tuple-element.48.gate), channel_id=1, source_target_pairs={{1,0},{2,1},{3,2},{4,3},{5,4},{6,5},{7,6},{9,8},{10,9},{11,10},{12... | collective-permute-start | bytes 786440 | tf_op jit(solution)/shard_map/ppermute | solution.py:461
  33.0 20.3 %collective-permute-start.3 = (bf16[128,1024]{1,0:T(8,128)(2,1)S(1)}, bf16[128,1024]{1,0:T(8,128)(2,1)S(1)}, u32[]{:S(2)}, u32[]{:S(2)}) collective-permute-start(bf16[128,1024]{1,0:T(8,128)(2,1)S(1)} %get-tuple-element.52.prod), channel_id=1, source_target_pairs={{0,1},{1,2},{2,3},{3,4},{4,5},{5,6},{6,7},{8,9},{9,10},{10,11},{11... | collective-permute-start | bytes 786440 | tf_op jit(solution)/shard_map/ppermute | solution.py:461
  37.6 23.7 %collective-permute-start.4 = (bf16[128,1024]{1,0:T(8,128)(2,1)S(1)}, bf16[128,1024]{1,0:T(8,128)(2,1)S(1)}, u32[]{:S(2)}, u32[]{:S(2)}) collective-permute-start(bf16[128,1024]{1,0:T(8,128)(2,1)S(1)} %get-tuple-element.53.gate), channel_id=1, source_target_pairs={{1,0},{2,1},{3,2},{4,3},{5,4},{6,5},{7,6},{9,8},{10,9},{11,10},{12... | collective-permute-start | bytes 786440 | tf_op jit(solution)/shard_map/ppermute | solution.py:461
  40.3 27.4 %collective-permute-start.5 = (bf16[128,1024]{1,0:T(8,128)(2,1)S(1)}, bf16[128,1024]{1,0:T(8,128)(2,1)S(1)}, u32[]{:S(2)}, u32[]{:S(2)}) collective-permute-start(bf16[128,1024]{1,0:T(8,128)(2,1)S(1)} %get-tuple-element.58.prod), channel_id=1, source_target_pairs={{0,1},{1,2},{2,3},{3,4},{4,5},{5,6},{6,7},{8,9},{9,10},{10,11},{11... | collective-permute-start | bytes 786440 | tf_op jit(solution)/shard_map/ppermute | solution.py:461
  45.9 8.9 %copy-start.3 = (bf16[1,128,4096]{2,1,0:T(8,128)(2,1)S(1)}, bf16[1,128,4096]{2,1,0:T(8,128)(2,1)}, u32[]{:S(2)}) copy-start(bf16[1,128,4096]{2,1,0:T(8,128)(2,1)} %cot.15) | copy-start | bytes 3145732
  45.9 21.9 %collective-permute-start.6 = (bf16[128,1024]{1,0:T(8,128)(2,1)S(1)}, bf16[128,1024]{1,0:T(8,128)(2,1)S(1)}, u32[]{:S(2)}, u32[]{:S(2)}) collective-permute-start(bf16[128,1024]{1,0:T(8,128)(2,1)S(1)} %get-tuple-element.59.gate), channel_id=1, source_target_pairs={{1,0},{2,1},{3,2},{4,3},{5,4},{6,5},{7,6},{9,8},{10,9},{11,10},{12... | collective-permute-start | bytes 786440 | tf_op jit(solution)/shard_map/ppermute | solution.py:461
  48.8 25.5 %collective-permute-start.7 = (bf16[128,1024]{1,0:T(8,128)(2,1)S(1)}, bf16[128,1024]{1,0:T(8,128)(2,1)S(1)}, u32[]{:S(2)}, u32[]{:S(2)}) collective-permute-start(bf16[128,1024]{1,0:T(8,128)(2,1)S(1)} %get-tuple-element.64.prod), channel_id=1, source_target_pairs={{0,1},{1,2},{2,3},{3,4},{4,5},{5,6},{6,7},{8,9},{9,10},{10,11},{11... | collective-permute-start | bytes 786440 | tf_op jit(solution)/shard_map/ppermute | solution.py:461
  53.4 20.9 %collective-permute-start.8 = (bf16[128,1024]{1,0:T(8,128)(2,1)S(1)}, bf16[128,1024]{1,0:T(8,128)(2,1)S(1)}, u32[]{:S(2)}, u32[]{:S(2)}) collective-permute-start(bf16[128,1024]{1,0:T(8,128)(2,1)S(1)} %get-tuple-element.65.gate), channel_id=1, source_target_pairs={{1,0},{2,1},{3,2},{4,3},{5,4},{6,5},{7,6},{9,8},{10,9},{11,10},{12... | collective-permute-start | bytes 786440 | tf_op jit(solution)/shard_map/ppermute | solution.py:461
  81.5 12.8 %all-to-all-start.1 = ((bf16[32,32,128]{2,1,0:T(8,128)(2,1)}), bf16[32,32,128]{2,1,0:T(8,128)(2,1)S(1)}, u32[]{:S(2)}, u32[]{:S(2)}) async-start(bf16[32,32,128]{2,1,0:T(8,128)(2,1)} %bundle.1), calls=%async_computation.1 | async-start | bytes 524288 | tf_op jit(solution)/shard_map/all_to_all | solution.py:489
  86.5 10.8 %collective-permute-start.12 = (bf16[2,96,128]{2,1,0:T(8,128)(2,1)S(1)}, bf16[2,96,128]{2,1,0:T(8,128)(2,1)S(1)}, u32[]{:S(2)}, u32[]{:S(2)}) collective-permute-start(bf16[2,96,128]{2,1,0:T(8,128)(2,1)S(1)} %get-tuple-element.73), channel_id=1, source_target_pairs={{1,0},{2,1},{3,2},{4,3},{5,4},{6,5},{7,6},{9,8},{10,9},{11,10},{12... | collective-permute-start | bytes 147464 | tf_op jit(solution)/shard_map/ppermute | solution.py:461
  87.8 15.4 %collective-permute-start.11 = (bf16[2,96,128]{2,1,0:T(8,128)(2,1)S(1)}, bf16[2,96,128]{2,1,0:T(8,128)(2,1)S(1)}, u32[]{:S(2)}, u32[]{:S(2)}) collective-permute-start(bf16[2,96,128]{2,1,0:T(8,128)(2,1)S(1)} %get-tuple-element.72), channel_id=1, source_target_pairs={{1,0},{2,1},{3,2},{4,3},{5,4},{6,5},{7,6},{9,8},{10,9},{11,10},{12... | collective-permute-start | bytes 147464 | tf_op jit(solution)/shard_map/ppermute | solution.py:461
  89.1 20.1 %collective-permute-start.10 = (bf16[2,96,128]{2,1,0:T(8,128)(2,1)S(1)}, bf16[2,96,128]{2,1,0:T(8,128)(2,1)S(1)}, u32[]{:S(2)}, u32[]{:S(2)}) collective-permute-start(bf16[2,96,128]{2,1,0:T(8,128)(2,1)S(1)} %get-tuple-element.71), channel_id=1, source_target_pairs={{1,0},{2,1},{3,2},{4,3},{5,4},{6,5},{7,6},{9,8},{10,9},{11,10},{12... | collective-permute-start | bytes 147464 | tf_op jit(solution)/shard_map/ppermute | solution.py:461
  90.4 20.6 %collective-permute-start.9 = (bf16[2,96,128]{2,1,0:T(8,128)(2,1)S(1)}, bf16[2,96,128]{2,1,0:T(8,128)(2,1)S(1)}, u32[]{:S(2)}, u32[]{:S(2)}) collective-permute-start(bf16[2,96,128]{2,1,0:T(8,128)(2,1)S(1)} %get-tuple-element.70), channel_id=1, source_target_pairs={{1,0},{2,1},{3,2},{4,3},{5,4},{6,5},{7,6},{9,8},{10,9},{11,10},{12... | collective-permute-start | bytes 147464 | tf_op jit(solution)/shard_map/ppermute | solution.py:461
  94.3 21.4 %collective-permute-start.13 = (f32[32,128]{1,0:T(8,128)S(1)}, f32[32,128]{1,0:T(8,128)S(1)}, u32[]{:S(2)}, u32[]{:S(2)}) collective-permute-start(f32[32,128]{1,0:T(8,128)S(1)} %total.1.refs_0_), channel_id=1, source_target_pairs={{0,1},{1,2},{2,3},{3,4},{4,5},{5,6},{6,7},{7,0},{8,9},{9,10},{10,1... | collective-permute-start | bytes 49160 | tf_op jit(solution)/shard_map/ppermute | solution.py:492
  97.2 19.1 %collective-permute-start.14 = (f32[32,128]{1,0:T(8,128)S(1)}, f32[32,128]{1,0:T(8,128)S(1)}, u32[]{:S(2)}, u32[]{:S(2)}) collective-permute-start(f32[32,128]{1,0:T(8,128)S(1)} %total.1.refs_0_), channel_id=1, source_target_pairs={{0,2},{1,3},{2,4},{3,5},{4,6},{5,7},{6,0},{7,1},{8,10},{9,11},{10,... | collective-permute-start | bytes 49160 | tf_op jit(solution)/shard_map/ppermute | solution.py:492
  103.1 14.7 %collective-permute-start.15 = (f32[32,128]{1,0:T(8,128)S(1)}, f32[32,128]{1,0:T(8,128)S(1)}, u32[]{:S(2)}, u32[]{:S(2)}) collective-permute-start(f32[32,128]{1,0:T(8,128)S(1)} %total.1.refs_0_), channel_id=1, source_target_pairs={{0,3},{1,4},{2,5},{3,6},{4,7},{5,0},{6,1},{7,2},{8,11},{9,12},{10,... | collective-permute-start | bytes 49160 | tf_op jit(solution)/shard_map/ppermute | solution.py:492
  109.2 8.6 %collective-permute-start.16 = (f32[32,128]{1,0:T(8,128)S(1)}, f32[32,128]{1,0:T(8,128)S(1)}, u32[]{:S(2)}, u32[]{:S(2)}) collective-permute-start(f32[32,128]{1,0:T(8,128)S(1)} %total.1.refs_0_), channel_id=1, source_target_pairs={{0,4},{1,5},{2,6},{3,7},{4,0},{5,1},{6,2},{7,3},{8,12},{9,13},{10,... | collective-permute-start | bytes 49160 | tf_op jit(solution)/shard_map/ppermute | solution.py:492
  111.0 6.8 %collective-permute-start.17 = (f32[32,128]{1,0:T(8,128)S(1)}, f32[32,128]{1,0:T(8,128)S(1)}, u32[]{:S(2)}, u32[]{:S(2)}) collective-permute-start(f32[32,128]{1,0:T(8,128)S(1)} %total.1.refs_0_), channel_id=1, source_target_pairs={{0,5},{1,6},{2,7},{3,0},{4,1},{5,2},{6,3},{7,4},{8,13},{9,14},{10,... | collective-permute-start | bytes 49160 | tf_op jit(solution)/shard_map/ppermute | solution.py:492
  115.7 4.6 %collective-permute-start.18 = (f32[32,128]{1,0:T(8,128)S(1)}, f32[32,128]{1,0:T(8,128)S(1)}, u32[]{:S(2)}, u32[]{:S(2)}) collective-permute-start(f32[32,128]{1,0:T(8,128)S(1)} %total.1.refs_0_), channel_id=1, source_target_pairs={{0,6},{1,7},{2,0},{3,1},{4,2},{5,3},{6,4},{7,5},{8,14},{9,15},{10,... | collective-permute-start | bytes 49160 | tf_op jit(solution)/shard_map/ppermute | solution.py:492
  116.4 4.0 %collective-permute-start.19 = (f32[32,128]{1,0:T(8,128)S(1)}, f32[32,128]{1,0:T(8,128)S(1)}, u32[]{:S(2)}, u32[]{:S(2)}) collective-permute-start(f32[32,128]{1,0:T(8,128)S(1)} %total.1.refs_0_), channel_id=1, source_target_pairs={{0,7},{1,0},{2,1},{3,2},{4,3},{5,4},{6,5},{7,6},{8,15},{9,8},{10,9... | collective-permute-start | bytes 49160 | tf_op jit(solution)/shard_map/ppermute | solution.py:492

commit v2 on v1

v2 whole, which is shorter than its diff:
```python
import functools
import math

import jax
import jax.numpy as jnp
from jax import lax
from jax.experimental import pallas as pl
from jax.experimental.pallas import tpu as pltpu
from jax.sharding import PartitionSpec as P

LANES = 128
GROUP = 16
SHORT = 7
ROWS = 128
FULL = 20
STEP = 512
PIECE = 16
SPAN = PIECE + 128
BF = jnp.bfloat16
F32 = jnp.float32


def params(mib):
    return pltpu.CompilerParams(vmem_limit_bytes=mib * 1024 * 1024)


def whole():
    return pl.BlockSpec(memory_space=pltpu.VMEM)


def in_hbm(array):
    return pltpu.with_memory_space_constraint(array, pltpu.HBM)


def anywhere():
    return pl.BlockSpec(memory_space=pl.ANY)


def pack_kernel(short_ref, long_ref, skip_ref, streams_ref, out_ref, tail_ref):
    tail_ref[...] = streams_ref[0]
    short = short_ref[...].astype(F32)
    skip = skip_ref[...].astype(F32)
    nothing = jnp.zeros((1, LANES), F32)
    rows = []
    for part in range(3):
        rows.append(short[:, part * LANES : (part + 1) * LANES])
        rows.append(skip if part == 0 else nothing)
    packed = jnp.concatenate(rows + [long_ref[...].astype(F32)], axis=0).astype(BF)
    out_ref[...] = jnp.broadcast_to(packed[None], out_ref.shape)


def pack(short_filter, long_filter, skip, streams, shards):
    return pl.pallas_call(
        pack_kernel,
        out_shape=(
            jax.ShapeDtypeStruct((shards, 32, LANES), BF),
            jax.ShapeDtypeStruct((16, streams.shape[2]), BF),
        ),
        in_specs=[
            pl.BlockSpec(short_filter.shape, lambda i: (0, 0)),
            pl.BlockSpec(long_filter.shape, lambda i: (0, 0)),
            pl.BlockSpec((1, LANES), lambda i: (0, 0)),
            pl.BlockSpec((1, 16, streams.shape[2]), lambda i: (0, ROWS // 16 - 1, 0)),
        ],
        out_specs=(
            pl.BlockSpec((shards, 32, LANES), lambda i: (0, 0, 0)),
            pl.BlockSpec((16, streams.shape[2]), lambda i: (0, 0)),
        ),
        grid=(1,),
        compiler_params=params(20),
        name="pack",
    )(*(in_hbm(x) for x in (short_filter, long_filter, skip[None], streams)))


def taps_of(table, tile):
    return table[tile // 3, pl.ds(pl.multiple_of(tile % 3 * 8, 8), 8), :]


def mixture(slot, halo, source, taps):
    slot[0:8, :] = halo
    slot[8 : 8 + ROWS, :] = source.astype(F32)
    running = taps[0:1] * slot[8 : 8 + ROWS, :]
    for lag in range(1, SHORT):
        running = running + taps[lag : lag + 1] * slot[8 - lag : 8 - lag + ROWS, :]
    return running


def gates_kernel(first_tile, count, g_ref, sq, sk, sv, hq, hk, hv, cot, prod, gate, key, val, table, ext):
    step = pl.program_id(0)
    tiles = STEP // LANES

    @pl.when(step == 0)
    def _():
        table[...] = g_ref[...].astype(F32)

    for t in range(tiles):
        tile = first_tile + step * tiles + t
        cols = slice(t * LANES, (t + 1) * LANES)
        mixed = []
        for part, (source, halo) in enumerate(((sq, hq), (sk, hk), (sv, hv))):
            taps = taps_of(table, tile + part * count)
            mixed.append(mixture(ext.at[t, part], halo[:, cols].astype(F32)[8:16], source[0, :, cols], taps))
        prod[:, cols] = (mixed[1] * mixed[2]).astype(BF)
        gate[:, cols] = (cot[0, :, cols].astype(F32) * mixed[0]).astype(BF)
        key[:, cols] = mixed[1].astype(BF)
        val[:, cols] = mixed[2].astype(BF)


def stream_specs(lead, blocks):
    def stream(part):
        return pl.BlockSpec((1, ROWS, STEP), lambda i: (0, 0, part * blocks + lead + i))

    def halo(part):
        return pl.BlockSpec((16, STEP), lambda i: (0, part * blocks + lead + i))

    return (
        [stream(part) for part in range(3)]
        + [halo(part) for part in range(3)]
        + [pl.BlockSpec((1, ROWS, STEP), lambda i: (0, 0, lead + i))]
    )


def gates(first, width, gathered, streams, before, grad_out):
    count = grad_out.shape[2] // LANES
    steps = width // STEP
    lead = first // STEP
    out = jax.ShapeDtypeStruct((ROWS, width), BF)
    out_spec = pl.BlockSpec((ROWS, STEP), lambda i: (0, i))
    return pl.pallas_call(
        functools.partial(gates_kernel, first // LANES, count),
        grid=(steps,),
        out_shape=(out,) * 4,
        in_specs=[pl.BlockSpec(gathered.shape, lambda i: (0, 0, 0))]
        + stream_specs(lead, grad_out.shape[2] // STEP),
        out_specs=(out_spec,) * 4,
        scratch_shapes=[
            pltpu.VMEM(gathered.shape, F32),
            pltpu.VMEM((STEP // LANES, 3, 8 + ROWS, LANES), F32),
        ],
        compiler_params=params(FULL),
        cost_estimate=pl.CostEstimate(
            flops=60 * 3 * ROWS * width, bytes_accessed=16 * ROWS * width, transcendentals=0
        ),
        name="gates",
    )(gathered, streams, streams, streams, before, before, before, grad_out)


def windows(block, pair):
    low = 2 * PIECE * pair
    return jnp.concatenate(
        [block[low : low + SPAN], block[low + PIECE : low + PIECE + SPAN]], axis=1
    )


def picked(result, owner):
    out = result[0:PIECE]
    for g in range(1, LANES // GROUP):
        out = jnp.where(owner == g, result[g * PIECE : (g + 1) * PIECE], out)
    return out


def toeplitz_rows(filters, shift):
    pieces = []
    for g in range(LANES // GROUP):
        line = jnp.concatenate([filters[g : g + 1], jnp.zeros((1, LANES), F32)], axis=1)
        line = jnp.broadcast_to(line, (PIECE, 2 * LANES))
        pieces.append(pltpu.roll(line, shift, 1, stride=1, stride_axis=0))
    return jnp.concatenate(pieces, axis=0).astype(BF)


def bands_kernel(tiles, g_ref, forward_ref, backward_ref):
    step = pl.program_id(0)
    flip = (
        lax.broadcasted_iota(jnp.int32, (LANES, LANES), 0)
        + lax.broadcasted_iota(jnp.int32, (LANES, LANES), 1)
        == LANES - 1
    ).astype(F32).astype(BF)
    for t in range(tiles):
        filters = g_ref[step * tiles + t].astype(F32)[24:32]
        flipped = jnp.dot(filters.astype(BF), flip, preferred_element_type=F32)
        forward_ref[t] = toeplitz_rows(flipped, 1)
        backward_ref[t] = toeplitz_rows(filters, 0)


def bands(gathered):
    shards = gathered.shape[0]
    tiles = 8
    out = jax.ShapeDtypeStruct((shards, LANES, 2 * LANES), BF)
    spec = pl.BlockSpec((tiles, LANES, 2 * LANES), lambda i: (i, 0, 0))
    return pl.pallas_call(
        functools.partial(bands_kernel, tiles),
        grid=(shards // tiles,),
        out_shape=(out, out),
        in_specs=[pl.BlockSpec(gathered.shape, lambda i: (0, 0, 0))],
        out_specs=(spec, spec),
        compiler_params=params(FULL),
        cost_estimate=pl.CostEstimate(flops=400000000, bytes_accessed=4000000, transcendentals=0),
        name="bands",
    )(gathered)


def back_kernel(
    first_tile, tiles, count, chained, g_ref, sq, sk, sv, hq, hk, hv, cot, prod, prior, gate, ahead, key, val, fw, bw, *rest
):
    if chained:
        rest = rest[5:]
    gs_ref, tail_ref, head_ref, short_ref, long_ref, table, ext, mixed, corr, held, sems = rest
    step = pl.program_id(0)
    steps = pl.num_programs(0)
    slot = lax.rem(step, 2)
    groups = LANES // GROUP

    def copies(at_step, at_slot):
        place = first_tile + at_step * tiles
        return [
            pltpu.make_async_copy(
                held.at[at_slot, part],
                gs_ref.at[0, :, pl.ds(pl.multiple_of((part * count + place) * LANES, STEP), STEP)],
                sems.at[at_slot, part],
            )
            for part in range(3)
        ]

    @pl.when(step >= 2)
    def _():
        for copy in copies(step - 2, slot):
            copy.wait()

    @pl.when(step == 0)
    def _():
        table[...] = g_ref[...].astype(F32)

    lane = lax.broadcasted_iota(jnp.int32, (1, LANES), 1)
    owner = lane // GROUP
    upside = (
        lax.broadcasted_iota(jnp.int32, (ROWS, ROWS), 0) ^ (PIECE - 1)
        == lax.broadcasted_iota(jnp.int32, (ROWS, ROWS), 1)
    ).astype(F32).astype(BF)
    owners = [(owner == g).astype(F32).astype(BF) for g in range(groups)]
    owners = [jnp.concatenate([m, m], axis=1) for m in owners]

    for t in range(tiles):
        tile = first_tile + step * tiles + t
        cols = slice(t * LANES, (t + 1) * LANES)
        skip = taps_of(table, tile * 3)[7:8]
        forward = fw[t, :, :SPAN]
        backward = bw[t, :, :SPAN]
        product = prod[:, cols]
        gated = gate[:, cols]
        context = jnp.concatenate([prior[:, cols], product], axis=0)
        coming = jnp.concatenate([gated, ahead[:, cols]], axis=0)
        turned = jnp.dot(upside, product, preferred_element_type=F32).astype(BF)
        wave, prod_grad = [], []
        lagged = None
        for pair in range(ROWS // (2 * PIECE)):
            low = 2 * PIECE * pair
            result = jnp.dot(forward, windows(context, pair), preferred_element_type=F32)
            wave += [picked(result[:, :LANES], owner), picked(result[:, LANES:], owner)]
            seen = windows(coming, pair)
            result = jnp.dot(backward, seen, preferred_element_type=F32)
            prod_grad += [picked(result[:, :LANES], owner), picked(result[:, LANES:], owner)]
            own = jnp.concatenate([turned[low : low + PIECE], turned[low + PIECE : low + 2 * PIECE]], axis=1)
            masked = jnp.concatenate([own * m for m in owners], axis=0)
            term = lax.dot_general(masked, seen, (((1,), (1,)), ((), ())), preferred_element_type=F32)
            lagged = term if lagged is None else lagged + term
        product = product.astype(F32)
        gated = gated.astype(F32)
        wave = jnp.concatenate(wave, axis=0) + skip * product
        prod_grad = jnp.concatenate(prod_grad, axis=0) + skip * gated
        corr[t, :, :SPAN] = lagged
        for g in range(groups):
            skewed = pltpu.roll(
                corr[t, g * PIECE : (g + 1) * PIECE, :], 2 * LANES - PIECE + 1, 1, stride=1, stride_axis=0
            )
            long_ref[t, g : g + 1, :] = jnp.sum(skewed[:, :LANES], axis=0, keepdims=True)
        long_ref[t, 8:9, :] = jnp.sum(gated * product, axis=0, keepdims=True)
        long_ref[t, 9:16, :] = jnp.zeros((7, LANES), F32)
        features = (
            cot[0, :, cols].astype(F32) * wave,
            prod_grad * val[:, cols].astype(F32),
            prod_grad * key[:, cols].astype(F32),
        )
        for part, (source, halo) in enumerate(((sq, hq), (sk, hk), (sv, hv))):
            taps = taps_of(table, tile + part * count)
            feature = features[part]
            shifted = mixed.at[t, part]
            shifted[0:ROWS, :] = feature
            shifted[ROWS : ROWS + 8, :] = jnp.zeros((8, LANES), F32)
            head_ref[part, :, cols] = feature[0:8].astype(BF)
            early = ext.at[t, part]
            early[0:8, :] = halo[:, cols].astype(F32)[8:16]
            early[8 : 8 + ROWS, :] = source[0, :, cols].astype(F32)
            sums = []
            running = taps[0:1] * feature
            for lag in range(SHORT):
                terms = feature * early[8 - lag : 8 - lag + ROWS, :]
                total = terms[0:8]
                for r in range(1, ROWS // 8):
                    total = total + terms[r * 8 : (r + 1) * 8]
                sums.append(jnp.sum(total, axis=0, keepdims=True))
                if lag > 0:
                    running = running + taps[lag : lag + 1] * shifted[lag : lag + ROWS, :]
            sums.append(jnp.zeros((1, LANES), F32))
            short_ref[part, t, :, :] = jnp.concatenate(sums, axis=0)
            held[slot, part, :, cols] = running.astype(BF)
            tail_ref[part, t] = running[ROWS - 16 :]

    for copy in copies(step, slot):
        copy.start()

    @pl.when(step == steps - 1)
    def _():
        for copy in copies(step, slot):
            copy.wait()

    @pl.when(jnp.logical_and(step == steps - 1, step >= 1))
    def _():
        for copy in copies(step - 1, 1 - slot):
            copy.wait()


def back(first, width, gathered, streams, before, grad_out, made, prior, ahead, filters, chain):
    count = grad_out.shape[2] // LANES
    steps = width // STEP
    tiles = STEP // LANES
    lead = first // STEP
    product, gate, key, value = made

    local = pl.BlockSpec((ROWS, STEP), lambda i: (0, i))
    band = pl.BlockSpec((tiles, LANES, 2 * LANES), lambda i: (lead + i, 0, 0))
    operands = [gathered, streams, streams, streams, before, before, before, grad_out]
    operands += [product, prior, gate, ahead, key, value, *filters]
    in_specs = (
        [pl.BlockSpec(gathered.shape, lambda i: (0, 0, 0))]
        + stream_specs(lead, grad_out.shape[2] // STEP)
        + [local] * 6
        + [band] * 2
    )
    aliases = {}
    if chain is not None:
        aliases = {len(operands) + i: i for i in range(5)}
        operands += chain
        in_specs += [anywhere()] * 5
    return pl.pallas_call(
        functools.partial(back_kernel, first // LANES, tiles, count, chain is not None),
        grid=(steps,),
        out_shape=(
            jax.ShapeDtypeStruct(streams.shape, BF),
            jax.ShapeDtypeStruct((3, count, 16, LANES), F32),
            jax.ShapeDtypeStruct((3, 8, grad_out.shape[2]), BF),
            jax.ShapeDtypeStruct((3, count, 8, LANES), F32),
            jax.ShapeDtypeStruct((count, 16, LANES), F32),
        ),
        in_specs=in_specs,
        out_specs=(
            anywhere(),
            pl.BlockSpec((3, tiles, 16, LANES), lambda i: (0, lead + i, 0, 0)),
            pl.BlockSpec((3, 8, STEP), lambda i: (0, 0, lead + i)),
            pl.BlockSpec((3, tiles, 8, LANES), lambda i: (0, lead + i, 0, 0)),
            pl.BlockSpec((tiles, 16, LANES), lambda i: (lead + i, 0, 0)),
        ),
        scratch_shapes=[
            pltpu.VMEM(gathered.shape, F32),
            pltpu.VMEM((tiles, 3, 8 + ROWS, LANES), F32),
            pltpu.VMEM((tiles, 3, ROWS + 8, LANES), F32),
            pltpu.VMEM((tiles, LANES, 2 * LANES), F32),
            pltpu.VMEM((2, 3, ROWS, STEP), BF),
            pltpu.SemaphoreType.DMA((2, 3)),
        ],
        input_output_aliases=aliases,
        compiler_params=params(FULL),
        cost_estimate=pl.CostEstimate(
            flops=600 * 3 * ROWS * width, bytes_accessed=24 * ROWS * width, transcendentals=0
        ),
        name="back",
    )(*operands)


def finish_kernel(count, g_ref, after_ref, tail_ref, _, gs_ref, strip, sem):
    for part in range(3):
        for here in range(count):
            tile = part * count + here
            taps = g_ref[tile // 3].astype(F32)[tile % 3 * 8 : tile % 3 * 8 + 8]
            after = after_ref[part, :, here * LANES : (here + 1) * LANES].astype(F32)
            after = jnp.concatenate([jnp.zeros((8, LANES), F32), after], axis=0)
            tail = tail_ref[part, here]
            last = tail[8:16]
            for lag in range(1, SHORT):
                last = last + taps[lag : lag + 1] * after[lag : lag + 8]
            strip[:, tile * LANES : (tile + 1) * LANES] = jnp.concatenate([tail[0:8], last], axis=0).astype(BF)
    copy = pltpu.make_async_copy(strip, gs_ref.at[0, pl.ds(ROWS - 16, 16), :], sem)
    copy.start()
    copy.wait()


def finish(gathered, after, tails, grads):
    return pl.pallas_call(
        functools.partial(finish_kernel, tails.shape[1]),
        out_shape=jax.ShapeDtypeStruct(grads.shape, BF),
        in_specs=[whole()] * 3 + [anywhere()],
        out_specs=anywhere(),
        scratch_shapes=[pltpu.VMEM((16, grads.shape[2]), BF), pltpu.SemaphoreType.DMA],
        input_output_aliases={3: 0},
        compiler_params=params(FULL),
        cost_estimate=pl.CostEstimate(flops=10000000, bytes_accessed=2000000, transcendentals=0),
        name="finish",
    )(gathered, after, tails, grads)


def bundle_kernel(shards, short_ref, long_ref, out_ref):
    def short(tile):
        return short_ref[tile // shards, tile % shards]

    for d in range(shards):
        long = long_ref[d]
        rows = [short(3 * d)[0:7], long[8:9], short(3 * d + 1), short(3 * d + 2), long[0:8]]
        out_ref[d] = jnp.concatenate(rows, axis=0).astype(BF)


def bundle(short, long, shards):
    return pl.pallas_call(
        functools.partial(bundle_kernel, shards),
        out_shape=jax.ShapeDtypeStruct((shards, 32, LANES), BF),
        in_specs=[whole()] * 2,
        out_specs=whole(),
        compiler_params=params(16),
        name="bundle",
    )(short, long)


def total_kernel(parts_ref, out_ref):
    out_ref[...] = jnp.broadcast_to(jnp.sum(parts_ref[...].astype(F32), axis=0).astype(BF)[None], out_ref.shape)


def total(parts, copies):
    return pl.pallas_call(
        total_kernel,
        out_shape=jax.ShapeDtypeStruct((copies,) + parts.shape[1:], BF),
        in_specs=[whole()],
        out_specs=whole(),
        compiler_params=params(16),
        name="total",
    )(parts)


def spread_kernel(scale, parts_ref, short_ref, long_ref, skip_ref):
    summed = jnp.sum(parts_ref[...].astype(F32), axis=0) * scale
    for part in range(3):
        short_ref[:, part * LANES : (part + 1) * LANES] = summed[8 * part : 8 * part + SHORT]
    long_ref[...] = summed[24:32]
    skip_ref[...] = summed[7:8]


def spread(parts, scale):
    return pl.pallas_call(
        functools.partial(spread_kernel, scale),
        out_shape=(
            jax.ShapeDtypeStruct((SHORT, 3 * LANES), F32),
            jax.ShapeDtypeStruct((8, LANES), F32),
            jax.ShapeDtypeStruct((1, LANES), F32),
        ),
        in_specs=[whole()],
        out_specs=(whole(),) * 3,
        compiler_params=params(16),
        name="spread",
    )(parts)


def passed_along(block, axis, distance):
    devices = range(lax.axis_size(axis))
    route = [(i - distance, i) for i in devices if i - distance in devices]
    return lax.ppermute(block, axis, route)


CHUNKS = (2560, 1536)


def local(streams, short_filter, long_filter, skip, grad_out):
    shards = lax.axis_size("dp")
    ring = lax.axis_size("seq")
    payload, tail_rows = pack(short_filter, long_filter, skip, streams, shards)
    before = passed_along(tail_rows, "seq", 1)
    gathered = lax.all_to_all(payload, "dp", 0, 0, tiled=True)
    work = []
    first = 0
    for width in CHUNKS:
        made = gates(first, width, gathered, streams, before, grad_out)
        work.append((first, width, made, passed_along(made[0], "seq", 1), passed_along(made[1], "seq", -1)))
        first += width
    filters = bands(gathered)
    chain = None
    for first, width, made, prior, ahead in work:
        chain = back(first, width, gathered, streams, before, grad_out, made, prior, ahead, filters, chain)
    grads, tails, head, short, long = chain
    after = passed_along(head, "seq", -1)
    parts = total(lax.all_to_all(bundle(short, long, shards), "dp", 0, 0, tiled=True), ring)
    parts = lax.all_to_all(parts, "seq", 0, 0, tiled=True)
    scale = 1.0 / math.sqrt(shards * ring * streams.shape[1])
    grad_short, grad_long, grad_skip = spread(parts, scale)
    grads = finish(gathered, after, tails, grads)
    return grads, grad_short, grad_long, grad_skip[0]


def solution(mesh):
    placed = (P("dp", "seq", None), P(None, "dp"), P("dp", None), P("dp"), P("dp", "seq", None))
    return jax.shard_map(
        local,
        mesh=mesh,
        in_specs=placed,
        out_specs=(P("dp", "seq", None), P(None, "dp"), P("dp", None), P("dp")),
        check_vma=False,
    )
```

time: 122 us -> 100 us (0.82)
  starting transfers between devices: 60.2 us -> 28.8 us
  waiting for transfers between devices: 5.15 us -> 22.4 us
  local copies, waits for them, and re-layouts: 5.15 us -> 1.23 us
  Pallas kernels: 34.4 us -> 30.7 us
    ppermute x7 -> x0, starting transfers between devices: 22.1 us -> none  [local(): lax.ppermute(own, 'seq', [(i, (i + distance) % ring) for i in range(ring)])]
    ppermute x13 -> x6, starting transfers between devices: 33.1 us -> 16.3 us  [passed_along(): return lax.ppermute(block, axis, route)]
    all_to_all x1 -> x2, waiting for transfers between devices: 2.59 us -> 13.4 us  [the longest x1 7.02 us: local(): parts = lax.all_to_all(parts, 'seq', 0, 0, tiled=True)]
    ppermute x13 -> x6, waiting for transfers between devices: 0.03 us -> 8.97 us  [passed_along(): return lax.ppermute(block, axis, route)]
    all_to_all x1 -> x2, starting transfers between devices: 4.98 us -> 12.5 us  [the longest x1 7.41 us: local(): parts = lax.all_to_all(parts, 'seq', 0, 0, tiled=True)]
    pallas_call x4 -> x2, Pallas kernels: 25.8 us -> 19.5 us  [back(): pl.pallas_call(functools.partial(back_kernel, first // LANES, tiles, coun...]
    unnamed x14 -> x6, local copies, waits for them, and re-layouts: 5.15 us -> 1.23 us
    ppermute x7 -> x0, waiting for transfers between devices: 2.53 us -> none  [local(): lax.ppermute(own, 'seq', [(i, (i + distance) % ring) for i in range(ring)])]
  transfers between devices with their start and end apart: 21 -> 8, of which waited for: 2 -> 4; matrix products, arithmetic and copies ran while one was open for 0% -> 0% of each run, Pallas kernels for 21% -> 17%
where the time goes in v2:
time: 100 us; the launch traced here: 99 us
  Pallas kernels  30.7 us (31%)
  starting transfers between devices  28.8 us (29%)
  waiting for transfers between devices  22.4 us (22%)
  blocking collectives  15.1 us (15%)
  local copies, waits for them, and re-layouts  1.23 us (1%)
    pallas_call x2, Pallas kernels, back(): pl.pallas_call(functools.partial(back_kernel, first // LANES, tiles, coun...  19.5 us
    ppermute x6, starting transfers between devices, passed_along(): return lax.ppermute(block, axis, route)  16.3 us
    all_to_all x1, blocking collectives, local(): gathered = lax.all_to_all(payload, 'dp', 0, 0, tiled=True)  15.1 us
    ppermute x6, waiting for transfers between devices, passed_along(): return lax.ppermute(block, axis, route)  8.97 us
    all_to_all x1, starting transfers between devices, local(): parts = lax.all_to_all(parts, 'seq', 0, 0, tiled=True)  7.41 us
    all_to_all x1, waiting for transfers between devices, local(): parts = lax.all_to_all(parts, 'seq', 0, 0, tiled=True)  7.02 us
    all_to_all x1, waiting for transfers between devices, local(): lax.all_to_all(bundle(short, long, shards), 'dp', 0, 0, tiled=True)  6.4 us
    pallas_call x2, Pallas kernels, gates(): pl.pallas_call(functools.partial(gates_kernel, first // LANES, count), gr...  5.46 us
  transfers between devices with their start and end apart: 8, of which 4 were waited for; matrix products, arithmetic and copies ran while one was open for 0% of the time, Pallas kernels for 17%

profile of v2, /device:TPU:2, one launch (start us, length us, event | category | flops | bytes accessed | tf_op | source)
XLA Modules:
  0.0 99.0 jit_solution(8727623864710821263)
XLA Ops:
  0.6 0.0 copy-start
  0.6 1.2 %pack.1 = (bf16[32,32,128]{2,1,0:T(8,128)(2,1)S(1)}, bf16[16,12288]{1,0:T(8,128)(2,1)S(1)}) custom-call(bf16[7,384]{1,0:T(8,128)(2,1)} %short_ref.1, bf16[8,128]{1,0:T(8,128)(2,1)} %long_ref.1, bf16[1,128]{1,0:T(2,128)(2,1)} %bitcast.2, bf16[1,128,12288]{2,1,0:T(8,128)(2,1)} %sv.7), custom_call_target="tpu_custom_call" | custom-call | tf_op jit(solution)/shard_map/pack/pallas_call | solution.py:53
  1.9 3.8 %collective-permute-start = (bf16[16,12288]{1,0:T(8,128)(2,1)S(1)}, bf16[16,12288]{1,0:T(8,128)(2,1)S(1)}, u32[]{:S(2)}, u32[]{:S(2)}) collective-permute-start(bf16[16,12288]{1,0:T(8,128)(2,1)S(1)} %get-tuple-element.30), channel_id=1, source_target_pairs={{0,1},{1,2},{2,3},{3,4},{4,5},{5,6},{6,7},{8,9},{9,10},{10,11},{11... | collective-permute-start | bytes 1179656 | tf_op jit(solution)/shard_map/ppermute | solution.py:472
  5.7 15.1 %all_to_all.15.g_ref = bf16[32,32,128]{2,1,0:T(8,128)(2,1)S(1)} all-to-all(bf16[32,32,128]{2,1,0:T(8,128)(2,1)S(1)} %get-tuple-element.29), channel_id=1, replica_groups=mesh['dp'=32,'seq'=8] {'dp'}, dimensions={0} | all-to-all | bytes 524288 | tf_op jit(solution)/shard_map/all_to_all | solution.py:483
  20.8 0.0 collective-permute-done.hq.hk.hv
  20.9 0.0 copy-done
  20.9 0.0 copy-start.1
  20.9 1.2 %copy-done.1 = bf16[1,128,4096]{2,1,0:T(8,128)(2,1)S(1)} copy-done((bf16[1,128,4096]{2,1,0:T(8,128)(2,1)S(1)}, bf16[1,128,4096]{2,1,0:T(8,128)(2,1)}, u32[]{:S(2)}) %copy-start.1) | copy-done | bytes 1048600
  22.1 3.4 %gates.3 = (bf16[128,2560]{1,0:T(8,128)(2,1)S(1)}, bf16[128,2560]{1,0:T(8,128)(2,1)S(1)}, bf16[128,2560]{1,0:T(8,128)(2,1)S(1)}, bf16[128,2560]{1,0:T(8,128)(2,1)S(1)}) custom-call(bf16[32,32,128]{2,1,0:T(8,128)(2,1)S(1)} %all_to_all.15.g_ref, bf16[1,128,12288]{2,1,0:T(8,128)(2,1)S(1)} %copy-done, bf16[1,128,12288]{2,1,0:T(8,128)(2,1)S(1)} %copy-done, ...), custom_call_target="tpu_custom_call" | custom-call | flops 58982400 | bytes 5242880 | tf_op jit(solution)/shard_map/gates/pallas_call | solution.py:129
  25.5 3.8 %collective-permute-start.3 = (bf16[128,2560]{1,0:T(8,128)(2,1)S(1)}, bf16[128,2560]{1,0:T(8,128)(2,1)S(1)}, u32[]{:S(2)}, u32[]{:S(2)}) collective-permute-start(bf16[128,2560]{1,0:T(8,128)(2,1)S(1)} %get-tuple-element.37.prod), channel_id=1, source_target_pairs={{0,1},{1,2},{2,3},{3,4},{4,5},{5,6},{6,7},{8,9},{9,10},{10,11},{11... | collective-permute-start | bytes 1966088 | tf_op jit(solution)/shard_map/ppermute | solution.py:472
  29.3 0.0 copy-start.2
  29.3 1.4 %collective-permute-start.4 = (bf16[128,2560]{1,0:T(8,128)(2,1)S(1)}, bf16[128,2560]{1,0:T(8,128)(2,1)S(1)}, u32[]{:S(2)}, u32[]{:S(2)}) collective-permute-start(bf16[128,2560]{1,0:T(8,128)(2,1)S(1)} %get-tuple-element.38.gate), channel_id=1, source_target_pairs={{1,0},{2,1},{3,2},{4,3},{5,4},{6,5},{7,6},{9,8},{10,9},{11,10},{12... | collective-permute-start | bytes 1966088 | tf_op jit(solution)/shard_map/ppermute | solution.py:472
  30.7 2.1 %gates.2 = (bf16[128,1536]{1,0:T(8,128)(2,1)S(1)}, bf16[128,1536]{1,0:T(8,128)(2,1)S(1)}, bf16[128,1536]{1,0:T(8,128)(2,1)S(1)}, bf16[128,1536]{1,0:T(8,128)(2,1)S(1)}) custom-call(bf16[32,32,128]{2,1,0:T(8,128)(2,1)S(1)} %all_to_all.15.g_ref, bf16[1,128,12288]{2,1,0:T(8,128)(2,1)S(1)} %copy-done, bf16[1,128,12288]{2,1,0:T(8,128)(2,1)S(1)} %copy-done, ...), custom_call_target="tpu_custom_call" | custom-call | flops 35389440 | bytes 3145728 | tf_op jit(solution)/shard_map/gates/pallas_call | solution.py:129
  32.9 4.6 %collective-permute-start.1 = (bf16[128,1536]{1,0:T(8,128)(2,1)S(1)}, bf16[128,1536]{1,0:T(8,128)(2,1)S(1)}, u32[]{:S(2)}, u32[]{:S(2)}) collective-permute-start(bf16[128,1536]{1,0:T(8,128)(2,1)S(1)} %get-tuple-element.31.prod), channel_id=1, source_target_pairs={{0,1},{1,2},{2,3},{3,4},{4,5},{5,6},{6,7},{8,9},{9,10},{10,11},{11... | collective-permute-start | bytes 1179656 | tf_op jit(solution)/shard_map/ppermute | solution.py:472
  37.4 1.3 %collective-permute-start.2 = (bf16[128,1536]{1,0:T(8,128)(2,1)S(1)}, bf16[128,1536]{1,0:T(8,128)(2,1)S(1)}, u32[]{:S(2)}, u32[]{:S(2)}) collective-permute-start(bf16[128,1536]{1,0:T(8,128)(2,1)S(1)} %get-tuple-element.32.gate), channel_id=1, source_target_pairs={{1,0},{2,1},{3,2},{4,3},{5,4},{6,5},{7,6},{9,8},{10,9},{11,10},{12... | collective-permute-start | bytes 1179656 | tf_op jit(solution)/shard_map/ppermute | solution.py:472
  38.7 1.2 %bands.1 = (bf16[32,128,256]{2,1,0:T(8,128)(2,1)S(1)}, bf16[32,128,256]{2,1,0:T(8,128)(2,1)S(1)}) custom-call(bf16[32,32,128]{2,1,0:T(8,128)(2,1)S(1)} %all_to_all.15.g_ref), custom_call_target="tpu_custom_call" | custom-call | flops 400000000 | bytes 4000000 | tf_op jit(solution)/shard_map/bands/pallas_call | solution.py:190
  39.9 4.4 %collective-permute-done.3.prior = bf16[128,2560]{1,0:T(8,128)(2,1)S(1)} collective-permute-done((bf16[128,2560]{1,0:T(8,128)(2,1)S(1)}, bf16[128,2560]{1,0:T(8,128)(2,1)S(1)}, u32[]{:S(2)}, u32[]{:S(2)}) %collective-permute-start.3) | collective-permute-done | bytes 655392 | tf_op jit(solution)/shard_map/ppermute | solution.py:472
  44.3 4.6 %collective-permute-done.4.ahead = bf16[128,2560]{1,0:T(8,128)(2,1)S(1)} collective-permute-done((bf16[128,2560]{1,0:T(8,128)(2,1)S(1)}, bf16[128,2560]{1,0:T(8,128)(2,1)S(1)}, u32[]{:S(2)}, u32[]{:S(2)}) %collective-permute-start.4) | collective-permute-done | bytes 655392 | tf_op jit(solution)/shard_map/ppermute | solution.py:472
  48.9 0.0 copy-done.2
  48.9 11.9 %back.2 = (bf16[1,128,12288]{2,1,0:T(8,128)(2,1)}, f32[3,32,16,128]{3,2,1,0:T(8,128)S(1)}, bf16[3,8,4096]{2,1,0:T(8,128)(2,1)S(1)}, f32[3,32,8,128]{3,2,1,0:T(8,128)S(1)}, f32[32,16,128]{2,1,0:T(8,128)S(1)}) custom-call(bf16[32,32,128]{2,1,0:T(8,128)(2,1)S(1)} %all_to_all.15.g_ref, bf16[1,128,12288]{2,1,0:T(8,128)(2,1)S(1)} %copy-done, ...), custom_call_target="tpu_custom_call" | custom-call | flops 589824000 | bytes 7864320 | tf_op jit(solution)/shard_map/back/pallas_call | solution.py:344
  60.8 0.0 collective-permute-done.1.prior
  60.9 0.0 collective-permute-done.2.ahead
  60.9 7.5 %back.3 = (bf16[1,128,12288]{2,1,0:T(8,128)(2,1)}, f32[3,32,16,128]{3,2,1,0:T(8,128)S(1)}, bf16[3,8,4096]{2,1,0:T(8,128)(2,1)S(1)}, f32[3,32,8,128]{3,2,1,0:T(8,128)S(1)}, f32[32,16,128]{2,1,0:T(8,128)S(1)}) custom-call(bf16[32,32,128]{2,1,0:T(8,128)(2,1)S(1)} %all_to_all.15.g_ref, ...), custom_call_target="tpu_custom_call", output_to_operand_aliasing={{0}: (16, {}), {1}: (17, {}), {2}: (18, {}), {3}: (19, {}),... | custom-call | flops 353894400 | bytes 4718592 | tf_op jit(solution)/shard_map/back/pallas_call | solution.py:344
  68.4 0.7 bundle.1
  69.1 5.1 %all-to-all-start.1 = ((bf16[32,32,128]{2,1,0:T(8,128)(2,1)}), bf16[32,32,128]{2,1,0:T(8,128)(2,1)S(1)}, u32[]{:S(2)}, u32[]{:S(2)}) async-start(bf16[32,32,128]{2,1,0:T(8,128)(2,1)} %bundle.1), calls=%async_computation.1 | async-start | bytes 524288 | tf_op jit(solution)/shard_map/all_to_all | solution.py:496
  74.2 1.3 %collective-permute-start.5 = (bf16[3,8,4096]{2,1,0:T(8,128)(2,1)S(1)}, bf16[3,8,4096]{2,1,0:T(8,128)(2,1)S(1)}, u32[]{:S(2)}, u32[]{:S(2)}) collective-permute-start(bf16[3,8,4096]{2,1,0:T(8,128)(2,1)S(1)} %get-tuple-element.46), channel_id=1, source_target_pairs={{1,0},{2,1},{3,2},{4,3},{5,4},{6,5},{7,6},{9,8},{10,9},{11,10},{12... | collective-permute-start | bytes 589832 | tf_op jit(solution)/shard_map/ppermute | solution.py:472
  75.5 6.4 %all-to-all-done.1.parts_ref = bf16[32,32,128]{2,1,0:T(8,128)(2,1)S(1)} async-done(((bf16[32,32,128]{2,1,0:T(8,128)(2,1)}), bf16[32,32,128]{2,1,0:T(8,128)(2,1)S(1)}, u32[]{:S(2)}, u32[]{:S(2)}) %all-to-all-start.1) | async-done | bytes 262176 | tf_op jit(solution)/shard_map/all_to_all | solution.py:496
  81.9 0.7 total.1
  82.6 7.4 %all-to-all-start.2 = ((bf16[8,32,128]{2,1,0:T(8,128)(2,1)}), bf16[8,32,128]{2,1,0:T(8,128)(2,1)S(1)}, u32[]{:S(2)}, u32[]{:S(2)}) async-start(bf16[8,32,128]{2,1,0:T(8,128)(2,1)} %total.1), calls=%async_computation.2 | async-start | bytes 131072 | tf_op jit(solution)/shard_map/all_to_all | solution.py:497
  90.0 0.0 collective-permute-done.5.after_ref
  90.0 1.3 %finish.1 = bf16[1,128,12288]{2,1,0:T(8,128)(2,1)} custom-call(bf16[32,32,128]{2,1,0:T(8,128)(2,1)S(1)} %all_to_all.15.g_ref, bf16[3,8,4096]{2,1,0:T(8,128)(2,1)S(1)} %collective-permute-done.5.after_ref, f32[3,32,16,128]{3,2,1,0:T(8,128)S(1)} %get-tuple-element.47.tail_ref, bf16[1,128,12288]{2,1,0:T(8,128)(2,1)} %get-tuple-element.48._), custom_call_target="tpu_custom_call", output_to_operand_aliasing={{}: (3, {})} | custom-call | flops 10000000 | bytes 2000000 | tf_op jit(solution)/shard_map/finish/pallas_call | solution.py:397
  91.4 7.0 %all-to-all-done.2.parts_ref = bf16[8,32,128]{2,1,0:T(8,128)(2,1)S(1)} async-done(((bf16[8,32,128]{2,1,0:T(8,128)(2,1)}), bf16[8,32,128]{2,1,0:T(8,128)(2,1)S(1)}, u32[]{:S(2)}, u32[]{:S(2)}) %all-to-all-start.2) | async-done | bytes 65568 | tf_op jit(solution)/shard_map/all_to_all | solution.py:497
  98.4 0.6 spread.1
Async XLA Ops:
  0.6 20.2 %copy-start = (bf16[1,128,12288]{2,1,0:T(8,128)(2,1)S(1)}, bf16[1,128,12288]{2,1,0:T(8,128)(2,1)}, u32[]{:S(2)}) copy-start(bf16[1,128,12288]{2,1,0:T(8,128)(2,1)} %sv.7) | copy-start | bytes 9437188
  1.9 19.0 %collective-permute-start = (bf16[16,12288]{1,0:T(8,128)(2,1)S(1)}, bf16[16,12288]{1,0:T(8,128)(2,1)S(1)}, u32[]{:S(2)}, u32[]{:S(2)}) collective-permute-start(bf16[16,12288]{1,0:T(8,128)(2,1)S(1)} %get-tuple-element.30), channel_id=1, source_target_pairs={{0,1},{1,2},{2,3},{3,4},{4,5},{5,6},{6,7},{8,9},{9,10},{10,11},{11... | collective-permute-start | bytes 1179656 | tf_op jit(solution)/shard_map/ppermute | solution.py:472
  20.9 1.2 %copy-start.1 = (bf16[1,128,4096]{2,1,0:T(8,128)(2,1)S(1)}, bf16[1,128,4096]{2,1,0:T(8,128)(2,1)}, u32[]{:S(2)}) copy-start(bf16[1,128,4096]{2,1,0:T(8,128)(2,1)} %cot.7) | copy-start | bytes 3145732
  25.5 18.8 %collective-permute-start.3 = (bf16[128,2560]{1,0:T(8,128)(2,1)S(1)}, bf16[128,2560]{1,0:T(8,128)(2,1)S(1)}, u32[]{:S(2)}, u32[]{:S(2)}) collective-permute-start(bf16[128,2560]{1,0:T(8,128)(2,1)S(1)} %get-tuple-element.37.prod), channel_id=1, source_target_pairs={{0,1},{1,2},{2,3},{3,4},{4,5},{5,6},{6,7},{8,9},{9,10},{10,11},{11... | collective-permute-start | bytes 1966088 | tf_op jit(solution)/shard_map/ppermute | solution.py:472
  29.3 19.6 %copy-start.2 = (bf16[1,128,4096]{2,1,0:T(8,128)(2,1)S(1)}, bf16[1,128,4096]{2,1,0:T(8,128)(2,1)}, u32[]{:S(2)}) copy-start(bf16[1,128,4096]{2,1,0:T(8,128)(2,1)} %cot.7) | copy-start | bytes 3145732
  29.3 19.6 %collective-permute-start.4 = (bf16[128,2560]{1,0:T(8,128)(2,1)S(1)}, bf16[128,2560]{1,0:T(8,128)(2,1)S(1)}, u32[]{:S(2)}, u32[]{:S(2)}) collective-permute-start(bf16[128,2560]{1,0:T(8,128)(2,1)S(1)} %get-tuple-element.38.gate), channel_id=1, source_target_pairs={{1,0},{2,1},{3,2},{4,3},{5,4},{6,5},{7,6},{9,8},{10,9},{11,10},{12... | collective-permute-start | bytes 1966088 | tf_op jit(solution)/shard_map/ppermute | solution.py:472
  32.9 28.0 %collective-permute-start.1 = (bf16[128,1536]{1,0:T(8,128)(2,1)S(1)}, bf16[128,1536]{1,0:T(8,128)(2,1)S(1)}, u32[]{:S(2)}, u32[]{:S(2)}) collective-permute-start(bf16[128,1536]{1,0:T(8,128)(2,1)S(1)} %get-tuple-element.31.prod), channel_id=1, source_target_pairs={{0,1},{1,2},{2,3},{3,4},{4,5},{5,6},{6,7},{8,9},{9,10},{10,11},{11... | collective-permute-start | bytes 1179656 | tf_op jit(solution)/shard_map/ppermute | solution.py:472
  37.4 23.4 %collective-permute-start.2 = (bf16[128,1536]{1,0:T(8,128)(2,1)S(1)}, bf16[128,1536]{1,0:T(8,128)(2,1)S(1)}, u32[]{:S(2)}, u32[]{:S(2)}) collective-permute-start(bf16[128,1536]{1,0:T(8,128)(2,1)S(1)} %get-tuple-element.32.gate), channel_id=1, source_target_pairs={{1,0},{2,1},{3,2},{4,3},{5,4},{6,5},{7,6},{9,8},{10,9},{11,10},{12... | collective-permute-start | bytes 1179656 | tf_op jit(solution)/shard_map/ppermute | solution.py:472
  69.1 12.8 %all-to-all-start.1 = ((bf16[32,32,128]{2,1,0:T(8,128)(2,1)}), bf16[32,32,128]{2,1,0:T(8,128)(2,1)S(1)}, u32[]{:S(2)}, u32[]{:S(2)}) async-start(bf16[32,32,128]{2,1,0:T(8,128)(2,1)} %bundle.1), calls=%async_computation.1 | async-start | bytes 524288 | tf_op jit(solution)/shard_map/all_to_all | solution.py:496
  74.2 15.8 %collective-permute-start.5 = (bf16[3,8,4096]{2,1,0:T(8,128)(2,1)S(1)}, bf16[3,8,4096]{2,1,0:T(8,128)(2,1)S(1)}, u32[]{:S(2)}, u32[]{:S(2)}) collective-permute-start(bf16[3,8,4096]{2,1,0:T(8,128)(2,1)S(1)} %get-tuple-element.46), channel_id=1, source_target_pairs={{1,0},{2,1},{3,2},{4,3},{5,4},{6,5},{7,6},{9,8},{10,9},{11,10},{12... | collective-permute-start | bytes 589832 | tf_op jit(solution)/shard_map/ppermute | solution.py:472
  82.6 15.8 %all-to-all-start.2 = ((bf16[8,32,128]{2,1,0:T(8,128)(2,1)}), bf16[8,32,128]{2,1,0:T(8,128)(2,1)S(1)}, u32[]{:S(2)}, u32[]{:S(2)}) async-start(bf16[8,32,128]{2,1,0:T(8,128)(2,1)} %total.1), calls=%async_computation.2 | async-start | bytes 131072 | tf_op jit(solution)/shard_map/all_to_all | solution.py:497

commit v3 on v2

v3 whole, which is shorter than its diff:
```python
import functools
import math

import jax
import jax.numpy as jnp
from jax import lax
from jax.experimental import pallas as pl
from jax.experimental.pallas import tpu as pltpu
from jax.sharding import PartitionSpec as P

LANES = 128
GROUP = 16
SHORT = 7
ROWS = 128
FULL = 6
UNROLL = 4
PIECE = 16
SPAN = PIECE + 128
BF = jnp.bfloat16
F32 = jnp.float32


def params(mib):
    return pltpu.CompilerParams(vmem_limit_bytes=mib * 1024 * 1024)


def whole():
    return pl.BlockSpec(memory_space=pltpu.VMEM)


def in_hbm(array):
    return pltpu.with_memory_space_constraint(array, pltpu.HBM)


def anywhere():
    return pl.BlockSpec(memory_space=pl.ANY)


def pack_kernel(short_ref, long_ref, skip_ref, streams_ref, out_ref, tail_ref):
    tail_ref[...] = streams_ref[0]
    short = short_ref[...].astype(F32)
    skip = skip_ref[...].astype(F32)
    nothing = jnp.zeros((1, LANES), F32)
    rows = []
    for part in range(3):
        rows.append(short[:, part * LANES : (part + 1) * LANES])
        rows.append(skip if part == 0 else nothing)
    packed = jnp.concatenate(rows + [long_ref[...].astype(F32)], axis=0).astype(BF)
    out_ref[...] = jnp.broadcast_to(packed[None], out_ref.shape)


def pack(short_filter, long_filter, skip, streams, shards):
    return pl.pallas_call(
        pack_kernel,
        out_shape=(
            jax.ShapeDtypeStruct((shards, 32, LANES), BF),
            jax.ShapeDtypeStruct((16, streams.shape[2]), BF),
        ),
        in_specs=[
            pl.BlockSpec(short_filter.shape, lambda i: (0, 0)),
            pl.BlockSpec(long_filter.shape, lambda i: (0, 0)),
            pl.BlockSpec((1, LANES), lambda i: (0, 0)),
            pl.BlockSpec((1, 16, streams.shape[2]), lambda i: (0, ROWS // 16 - 1, 0)),
        ],
        out_specs=(
            pl.BlockSpec((shards, 32, LANES), lambda i: (0, 0, 0)),
            pl.BlockSpec((16, streams.shape[2]), lambda i: (0, 0)),
        ),
        grid=(1,),
        compiler_params=params(FULL),
        name="pack",
    )(*(in_hbm(x) for x in (short_filter, long_filter, skip[None], streams)))


def taps_of(table, tile):
    return table[tile // 3, pl.ds(pl.multiple_of(tile % 3 * 8, 8), 8), :]


def lanes_of(tile):
    start = tile * LANES
    return pl.ds(start if isinstance(start, int) else pl.multiple_of(start, LANES), LANES)


def mixture(slot, halo, source, taps):
    slot[0:8, :] = halo
    slot[8 : 8 + ROWS, :] = source.astype(F32)
    running = taps[0:1] * slot[8 : 8 + ROWS, :]
    for lag in range(1, SHORT):
        running = running + taps[lag : lag + 1] * slot[8 - lag : 8 - lag + ROWS, :]
    return running


def gates_kernel(first, lead, count, g_ref, streams, before, cot, *rest):
    if lead:
        prod, gate, key, val, table, ext = rest
        table[...] = g_ref[...].astype(F32)
    else:
        prod, gate, key, val, ext = rest
        table = g_ref

    def some(step, _):
        for t in range(UNROLL):
            here = step * UNROLL + t
            tile = first // LANES + here
            cols = lanes_of(here)
            mixed = []
            for part in range(3):
                whence = lanes_of(tile + part * count)
                taps = taps_of(table, tile + part * count)
                halo = before[:, whence].astype(F32)[8:16]
                mixed.append(mixture(ext.at[t, part], halo, streams[0, :, whence], taps))
            prod[:, cols] = (mixed[1] * mixed[2]).astype(BF)
            gate[:, cols] = (cot[0, :, lanes_of(tile)].astype(F32) * mixed[0]).astype(BF)
            key[:, cols] = mixed[1].astype(BF)
            val[:, cols] = mixed[2].astype(BF)
        return 0

    for step in range(prod.shape[1] // LANES // UNROLL):
        some(step, 0)


def gates(first, width, table, streams, before, grad_out, lead):
    count = grad_out.shape[2] // LANES
    outs = [jax.ShapeDtypeStruct((ROWS, width), BF)] * 4
    if lead:
        outs.append(jax.ShapeDtypeStruct(table.shape, F32))
    return pl.pallas_call(
        functools.partial(gates_kernel, first, lead, count),
        out_shape=tuple(outs),
        in_specs=[whole()] * 4,
        out_specs=(whole(),) * len(outs),
        scratch_shapes=[pltpu.VMEM((UNROLL, 3, 8 + ROWS, LANES), F32)],
        compiler_params=params(FULL),
        cost_estimate=pl.CostEstimate(
            flops=60 * 3 * ROWS * width, bytes_accessed=16 * ROWS * width, transcendentals=0
        ),
        name="gates",
    )(table, streams, before, grad_out)


def windows(block, pair):
    low = 2 * PIECE * pair
    return jnp.concatenate(
        [block[low : low + SPAN], block[low + PIECE : low + PIECE + SPAN]], axis=1
    )


def picked(result, owner):
    out = result[0:PIECE]
    for g in range(1, LANES // GROUP):
        out = jnp.where(owner == g, result[g * PIECE : (g + 1) * PIECE], out)
    return out


def toeplitz_rows(filters, shift):
    pieces = []
    for g in range(LANES // GROUP):
        line = jnp.concatenate([filters[g : g + 1], jnp.zeros((1, LANES), F32)], axis=1)
        line = jnp.broadcast_to(line, (PIECE, 2 * LANES))
        pieces.append(pltpu.roll(line, shift, 1, stride=1, stride_axis=0))
    return jnp.concatenate(pieces, axis=0).astype(BF)


def bands_kernel(tiles, g_ref, forward_ref, backward_ref):
    step = pl.program_id(0)
    flip = (
        lax.broadcasted_iota(jnp.int32, (LANES, LANES), 0)
        + lax.broadcasted_iota(jnp.int32, (LANES, LANES), 1)
        == LANES - 1
    ).astype(F32).astype(BF)
    for t in range(tiles):
        filters = g_ref[step * tiles + t, 24:32, :]
        flipped = jnp.dot(filters.astype(BF), flip, preferred_element_type=F32)
        forward_ref[t] = toeplitz_rows(flipped, 1)
        backward_ref[t] = toeplitz_rows(filters, 0)


def bands(gathered):
    shards = gathered.shape[0]
    tiles = 8
    out = jax.ShapeDtypeStruct((shards, LANES, 2 * LANES), BF)
    spec = pl.BlockSpec((tiles, LANES, 2 * LANES), lambda i: (i, 0, 0))
    return pl.pallas_call(
        functools.partial(bands_kernel, tiles),
        grid=(shards // tiles,),
        out_shape=(out, out),
        in_specs=[pl.BlockSpec(gathered.shape, lambda i: (0, 0, 0))],
        out_specs=(spec, spec),
        compiler_params=params(FULL),
        cost_estimate=pl.CostEstimate(flops=400000000, bytes_accessed=4000000, transcendentals=0),
        name="bands",
    )(gathered)


def back_kernel(
    first, count, table, streams, before, cot, prod, gate, key, val, prior, ahead, fw, bw, *rest
):
    if first > 0:
        earlier, *rest = rest
    gs_ref, tail_ref, head_ref, short_ref, long_ref, mixed, corr = rest
    if first > 0:
        head_ref[:, :, :first] = earlier[...]
    groups = LANES // GROUP
    lane = lax.broadcasted_iota(jnp.int32, (1, LANES), 1)
    owner = lane // GROUP
    upside = (
        lax.broadcasted_iota(jnp.int32, (ROWS, ROWS), 0) ^ (PIECE - 1)
        == lax.broadcasted_iota(jnp.int32, (ROWS, ROWS), 1)
    ).astype(F32).astype(BF)
    owners = [(owner == g).astype(F32).astype(BF) for g in range(groups)]
    owners = [jnp.concatenate([m, m], axis=1) for m in owners]

    def one(t, here):
        tile = first // LANES + here
        cols = lanes_of(here)
        skip = taps_of(table, tile * 3)[7:8]
        forward = fw[tile, :, :SPAN]
        backward = bw[tile, :, :SPAN]
        product = prod[:, cols]
        gated = gate[:, cols]
        context = jnp.concatenate([prior[:, cols], product], axis=0)
        coming = jnp.concatenate([gated, ahead[:, cols]], axis=0)
        turned = jnp.dot(upside, product, preferred_element_type=F32).astype(BF)
        wave, prod_grad = [], []
        lagged = None
        for pair in range(ROWS // (2 * PIECE)):
            low = 2 * PIECE * pair
            result = jnp.dot(forward, windows(context, pair), preferred_element_type=F32)
            wave += [picked(result[:, :LANES], owner), picked(result[:, LANES:], owner)]
            seen = windows(coming, pair)
            result = jnp.dot(backward, seen, preferred_element_type=F32)
            prod_grad += [picked(result[:, :LANES], owner), picked(result[:, LANES:], owner)]
            own = jnp.concatenate([turned[low : low + PIECE], turned[low + PIECE : low + 2 * PIECE]], axis=1)
            masked = jnp.concatenate([own * m for m in owners], axis=0)
            term = lax.dot_general(masked, seen, (((1,), (1,)), ((), ())), preferred_element_type=F32)
            lagged = term if lagged is None else lagged + term
        product = product.astype(F32)
        gated = gated.astype(F32)
        wave = jnp.concatenate(wave, axis=0) + skip * product
        prod_grad = jnp.concatenate(prod_grad, axis=0) + skip * gated
        corr[t, :, :SPAN] = lagged
        for g in range(groups):
            skewed = pltpu.roll(
                corr[t, g * PIECE : (g + 1) * PIECE, :], 2 * LANES - PIECE + 1, 1, stride=1, stride_axis=0
            )
            long_ref[here, g : g + 1, :] = jnp.sum(skewed[:, :LANES], axis=0, keepdims=True)
        long_ref[here, 8:9, :] = jnp.sum(gated * product, axis=0, keepdims=True)
        long_ref[here, 9:16, :] = jnp.zeros((7, LANES), F32)
        features = (
            cot[0, :, lanes_of(tile)].astype(F32) * wave,
            prod_grad * val[:, cols].astype(F32),
            prod_grad * key[:, cols].astype(F32),
        )
        for part in range(3):
            whence = lanes_of(tile + part * count)
            taps = taps_of(table, tile + part * count)
            feature = features[part]
            shifted = mixed.at[t, part]
            shifted[0:8, :] = jnp.zeros((8, LANES), F32)
            shifted[8 : 8 + ROWS, :] = feature
            shifted[8 + ROWS : 16 + ROWS, :] = jnp.zeros((8, LANES), F32)
            head_ref[part, :, lanes_of(tile)] = feature[0:8].astype(BF)
            early = before[:, whence].astype(F32)[8:16]
            values = streams[0, :, whence].astype(F32)
            totals = [None if lag == 0 else shifted[lag : lag + 8, :] * early for lag in range(SHORT)]
            done = []
            spread = [jnp.broadcast_to(taps[lag : lag + 1], (8, LANES)) for lag in range(SHORT)]
            for r in range(ROWS // 8):
                running = None
                value = values[r * 8 : (r + 1) * 8]
                for lag in range(SHORT):
                    moved = shifted[8 + r * 8 + lag : 16 + r * 8 + lag, :]
                    term = spread[lag] * moved
                    running = term if running is None else running + term
                    term = moved * value
                    totals[lag] = term if totals[lag] is None else totals[lag] + term
                done.append(running)
            running = jnp.concatenate(done, axis=0)
            sums = [jnp.sum(total, axis=0, keepdims=True) for total in totals]
            sums.append(jnp.zeros((1, LANES), F32))
            short_ref[part, here, :, :] = jnp.concatenate(sums, axis=0)
            gs_ref[part, :, cols] = running.astype(BF)
            tail_ref[part, here] = running[ROWS - 16 :]

    def some(step, _):
        for t in range(UNROLL):
            one(t, step * UNROLL + t)
        return 0

    for step in range(prod.shape[1] // LANES // UNROLL):
        some(step, 0)


def back(first, width, table, streams, before, grad_out, made, prior, ahead, filters, earlier):
    count = grad_out.shape[2] // LANES
    tiles = width // LANES
    outs = (
        jax.ShapeDtypeStruct((3, ROWS, width), BF),
        jax.ShapeDtypeStruct((3, tiles, 16, LANES), F32),
        jax.ShapeDtypeStruct((3, 8, first + width), BF),
        jax.ShapeDtypeStruct((3, tiles, 8, LANES), F32),
        jax.ShapeDtypeStruct((tiles, 16, LANES), F32),
    )
    return pl.pallas_call(
        functools.partial(back_kernel, first, count),
        out_shape=outs,
        in_specs=[whole()] * (12 + len(earlier)),
        out_specs=(whole(),) * len(outs),
        scratch_shapes=[
            pltpu.VMEM((UNROLL, 3, ROWS + 16, LANES), F32),
            pltpu.VMEM((UNROLL, 8 * PIECE, 2 * LANES), F32),
        ],
        compiler_params=params(FULL),
        cost_estimate=pl.CostEstimate(
            flops=600 * 3 * ROWS * width, bytes_accessed=24 * ROWS * width, transcendentals=0
        ),
        name="back",
    )(table, streams, before, grad_out, *made, prior, ahead, *filters, *earlier)


def finish_kernel(chunks, count, table, *refs):
    pieces, tails = refs[:chunks], refs[chunks : 2 * chunks]
    after, out_ref, strip, sems = refs[2 * chunks :]
    copies = []
    first = 0
    for c in range(chunks):
        width = pieces[c].shape[2]
        for part in range(3):
            start = part * count * LANES + first
            copies.append(
                pltpu.make_async_copy(
                    pieces[c].at[part, pl.ds(0, ROWS - 16), :],
                    out_ref.at[0, pl.ds(0, ROWS - 16), pl.ds(start, width)],
                    sems.at[3 * c + part],
                )
            )
            copies[-1].start()
        first += width
    first = 0
    for c in range(chunks):
        for part in range(3):
            for here in range(tails[c].shape[1]):
                tile = part * count + first + here
                taps = taps_of(table, tile)
                rows = after[part, :, lanes_of(first + here)].astype(F32)
                rows = jnp.concatenate([jnp.zeros((8, LANES), F32), rows], axis=0)
                tail = tails[c][part, here]
                last = tail[8:16]
                for lag in range(1, SHORT):
                    last = last + taps[lag : lag + 1] * rows[lag : lag + 8]
                strip[:, tile * LANES : (tile + 1) * LANES] = jnp.concatenate([tail[0:8], last], axis=0).astype(BF)
        first += tails[c].shape[1]
    copies.append(pltpu.make_async_copy(strip, out_ref.at[0, pl.ds(ROWS - 16, 16), :], sems.at[3 * chunks]))
    copies[-1].start()
    for copy in copies:
        copy.wait()


def finish(table, pieces, tails, after, shape):
    chunks = len(pieces)
    return pl.pallas_call(
        functools.partial(finish_kernel, chunks, shape[2] // LANES // 3),
        out_shape=jax.ShapeDtypeStruct(shape, BF),
        in_specs=[whole()] * (2 + 2 * chunks),
        out_specs=anywhere(),
        scratch_shapes=[pltpu.VMEM((16, shape[2]), BF), pltpu.SemaphoreType.DMA((3 * chunks + 1,))],
        compiler_params=params(FULL),
        cost_estimate=pl.CostEstimate(flops=10000000, bytes_accessed=2000000, transcendentals=0),
        name="finish",
    )(table, *pieces, *tails, after)


def bundle_kernel(chunks, shards, *refs):
    shorts, longs, out_ref = refs[:chunks], refs[chunks : 2 * chunks], refs[2 * chunks]
    where = [(c, i) for c in range(chunks) for i in range(longs[c].shape[0])]

    def short(tile):
        c, i = where[tile % shards]
        return shorts[c][tile // shards, i]

    for d in range(shards):
        c, i = where[d]
        long = longs[c][i]
        rows = [short(3 * d)[0:7], long[8:9], short(3 * d + 1), short(3 * d + 2), long[0:8]]
        out_ref[d] = jnp.concatenate(rows, axis=0).astype(BF)


def bundle(shorts, longs, shards):
    return pl.pallas_call(
        functools.partial(bundle_kernel, len(shorts), shards),
        out_shape=jax.ShapeDtypeStruct((shards, 32, LANES), BF),
        in_specs=[whole()] * (2 * len(shorts)),
        out_specs=whole(),
        compiler_params=params(FULL),
        name="bundle",
    )(*shorts, *longs)


def total_kernel(parts_ref, out_ref):
    out_ref[...] = jnp.broadcast_to(jnp.sum(parts_ref[...].astype(F32), axis=0).astype(BF)[None], out_ref.shape)


def total(parts, copies):
    return pl.pallas_call(
        total_kernel,
        out_shape=jax.ShapeDtypeStruct((copies,) + parts.shape[1:], BF),
        in_specs=[whole()],
        out_specs=whole(),
        compiler_params=params(FULL),
        name="total",
    )(parts)


def spread_kernel(scale, parts_ref, short_ref, long_ref, skip_ref):
    summed = jnp.sum(parts_ref[...].astype(F32), axis=0) * scale
    for part in range(3):
        short_ref[:, part * LANES : (part + 1) * LANES] = summed[8 * part : 8 * part + SHORT]
    long_ref[...] = summed[24:32]
    skip_ref[...] = summed[7:8]


def spread(parts, scale):
    return pl.pallas_call(
        functools.partial(spread_kernel, scale),
        out_shape=(
            jax.ShapeDtypeStruct((SHORT, 3 * LANES), F32),
            jax.ShapeDtypeStruct((8, LANES), F32),
            jax.ShapeDtypeStruct((1, LANES), F32),
        ),
        in_specs=[whole()],
        out_specs=(whole(),) * 3,
        compiler_params=params(FULL),
        name="spread",
    )(parts)


def passed_along(block, axis, distance):
    devices = range(lax.axis_size(axis))
    route = [(i - distance, i) for i in devices if i - distance in devices]
    return lax.ppermute(block, axis, route)


CHUNKS = (2560, 1536)


def local(streams, short_filter, long_filter, skip, grad_out):
    shards = lax.axis_size("dp")
    ring = lax.axis_size("seq")
    payload, tail_rows = pack(short_filter, long_filter, skip, streams, shards)
    before = passed_along(tail_rows, "seq", 1)
    gathered = lax.all_to_all(payload, "dp", 0, 0, tiled=True)
    work = []
    table, first = gathered, 0
    for width in CHUNKS:
        made = gates(first, width, table, streams, before, grad_out, first == 0)
        if first == 0:
            table = made[4]
        work.append((first, width, made[:4], passed_along(made[0], "seq", 1), passed_along(made[1], "seq", -1)))
        first += width
    filters = bands(table)
    done = []
    for first, width, made, prior, ahead in work:
        earlier = [done[-1][2]] if done else []
        done.append(back(first, width, table, streams, before, grad_out, made, prior, ahead, filters, earlier))
    pieces, tails, heads, shorts, longs = zip(*done)
    after = passed_along(heads[-1], "seq", -1)
    parts = total(lax.all_to_all(bundle(shorts, longs, shards), "dp", 0, 0, tiled=True), ring)
    parts = lax.all_to_all(parts, "seq", 0, 0, tiled=True)
    scale = 1.0 / math.sqrt(shards * ring * streams.shape[1])
    grad_short, grad_long, grad_skip = spread(parts, scale)
    grads = finish(table, pieces, tails, after, streams.shape)
    return grads, grad_short, grad_long, grad_skip[0]


def solution(mesh):
    placed = (P("dp", "seq", None), P(None, "dp"), P("dp", None), P("dp"), P("dp", "seq", None))
    return jax.shard_map(
        local,
        mesh=mesh,
        in_specs=placed,
        out_specs=(P("dp", "seq", None), P(None, "dp"), P("dp", None), P("dp")),
        check_vma=False,
    )
```

time: 100 us -> 94.5 us (0.945)
  Pallas kernels: 30.7 us -> 24.4 us
  local copies, waits for them, and re-layouts: 1.23 us -> 4.12 us
  waiting for transfers between devices: 22.4 us -> 20.2 us
    pallas_call x6, Pallas kernels: 27 us -> 21.1 us  [the longest x2 13.5 us: back(): pl.pallas_call(functools.partial(back_kernel, first, count), out_shape=ou...]
    unnamed x6 -> x14, local copies, waits for them, and re-layouts: 1.23 us -> 4.12 us
    all_to_all x1, waiting for transfers between devices: 7.02 us -> 4.45 us  [local(): parts = lax.all_to_all(parts, 'seq', 0, 0, tiled=True)]
  transfers between devices with their start and end apart: 8 -> 8, of which waited for: 4 -> 4; matrix products, arithmetic and copies ran while one was open for 0% -> 0% of each run, Pallas kernels for 17% -> 15%
where the time goes in v3:
time: 94.5 us; the launch traced here: 93.2 us
  starting transfers between devices  28.6 us (30%)
  Pallas kernels  24.4 us (26%)
  waiting for transfers between devices  20.2 us (21%)
  blocking collectives  15.1 us (16%)
  local copies, waits for them, and re-layouts  4.12 us (4%)
    ppermute x6, starting transfers between devices, passed_along(): return lax.ppermute(block, axis, route)  16.1 us
    all_to_all x1, blocking collectives, local(): gathered = lax.all_to_all(payload, 'dp', 0, 0, tiled=True)  15.1 us
    pallas_call x2, Pallas kernels, back(): pl.pallas_call(functools.partial(back_kernel, first, count), out_shape=ou...  13.5 us
    ppermute x6, waiting for transfers between devices, passed_along(): return lax.ppermute(block, axis, route)  9.31 us
    all_to_all x1, starting transfers between devices, local(): parts = lax.all_to_all(parts, 'seq', 0, 0, tiled=True)  7.41 us
    all_to_all x1, waiting for transfers between devices, local(): lax.all_to_all(bundle(shorts, longs, shards), 'dp', 0, 0, tiled=True)  6.41 us
    all_to_all x1, starting transfers between devices, local(): lax.all_to_all(bundle(shorts, longs, shards), 'dp', 0, 0, tiled=True)  5.08 us
    all_to_all x1, waiting for transfers between devices, local(): parts = lax.all_to_all(parts, 'seq', 0, 0, tiled=True)  4.45 us
  transfers between devices with their start and end apart: 8, of which 4 were waited for; matrix products, arithmetic and copies ran while one was open for 0% of the time, Pallas kernels for 15%

profile of v3, /device:TPU:2, one launch (start us, length us, event | category | flops | bytes accessed | tf_op | source)
XLA Modules:
  0.0 93.2 jit_solution(11545544547782794008)
XLA Ops:
  0.6 0.0 copy-start
  0.6 1.2 %pack.1 = (bf16[32,32,128]{2,1,0:T(8,128)(2,1)S(1)}, bf16[16,12288]{1,0:T(8,128)(2,1)S(1)}) custom-call(bf16[7,384]{1,0:T(8,128)(2,1)} %short_ref.1, bf16[8,128]{1,0:T(8,128)(2,1)} %long_ref.1, bf16[1,128]{1,0:T(2,128)(2,1)} %bitcast.2, bf16[1,128,12288]{2,1,0:T(8,128)(2,1)} %streams.7), custom_call_target="tpu_custom_call" | custom-call | tf_op jit(solution)/shard_map/pack/pallas_call | solution.py:53
  1.9 3.8 %collective-permute-start = (bf16[16,12288]{1,0:T(8,128)(2,1)S(1)}, bf16[16,12288]{1,0:T(8,128)(2,1)S(1)}, u32[]{:S(2)}, u32[]{:S(2)}) collective-permute-start(bf16[16,12288]{1,0:T(8,128)(2,1)S(1)} %get-tuple-element.31), channel_id=1, source_target_pairs={{0,1},{1,2},{2,3},{3,4},{4,5},{5,6},{6,7},{8,9},{9,10},{10,11},{11... | collective-permute-start | bytes 1179656 | tf_op jit(solution)/shard_map/ppermute | solution.py:440
  5.7 15.1 %all_to_all.15.g_ref = bf16[32,32,128]{2,1,0:T(8,128)(2,1)S(1)} all-to-all(bf16[32,32,128]{2,1,0:T(8,128)(2,1)S(1)} %get-tuple-element.30), channel_id=1, replica_groups=mesh['dp'=32,'seq'=8] {'dp'}, dimensions={0} | all-to-all | bytes 524288 | tf_op jit(solution)/shard_map/all_to_all | solution.py:451
  20.8 0.0 collective-permute-done.before
  20.9 0.0 copy-done
  20.9 0.0 copy-start.1
  20.9 1.2 %copy-done.1 = bf16[1,128,4096]{2,1,0:T(8,128)(2,1)S(1)} copy-done((bf16[1,128,4096]{2,1,0:T(8,128)(2,1)S(1)}, bf16[1,128,4096]{2,1,0:T(8,128)(2,1)}, u32[]{:S(2)}) %copy-start.1) | copy-done | bytes 1048600
  22.1 0.0 copy-start.2
  22.1 2.6 %gates.2 = (bf16[128,2560]{1,0:T(8,128)(2,1)S(1)}, bf16[128,2560]{1,0:T(8,128)(2,1)S(1)}, bf16[128,2560]{1,0:T(8,128)(2,1)S(1)}, bf16[128,2560]{1,0:T(8,128)(2,1)S(1)}, f32[32,32,128]{2,1,0:T(8,128)S(1)}) custom-call(bf16[32,32,128]{2,1,0:T(8,128)(2,1)S(1)} %all_to_all.15.g_ref, bf16[1,128,12288]{2,1,0:T(8,128)(2,1)S(1)} %copy-done, ...), custom_call_target="tpu_custom_call" | custom-call | flops 58982400 | bytes 5242880 | tf_op jit(solution)/shard_map/gates/pallas_call | solution.py:127
  24.7 3.8 %collective-permute-start.1 = (bf16[128,2560]{1,0:T(8,128)(2,1)S(1)}, bf16[128,2560]{1,0:T(8,128)(2,1)S(1)}, u32[]{:S(2)}, u32[]{:S(2)}) collective-permute-start(bf16[128,2560]{1,0:T(8,128)(2,1)S(1)} %get-tuple-element.33.prod), channel_id=1, source_target_pairs={{0,1},{1,2},{2,3},{3,4},{4,5},{5,6},{6,7},{8,9},{9,10},{10,11},{11... | collective-permute-start | bytes 1966088 | tf_op jit(solution)/shard_map/ppermute | solution.py:440
  28.6 1.3 %collective-permute-start.2 = (bf16[128,2560]{1,0:T(8,128)(2,1)S(1)}, bf16[128,2560]{1,0:T(8,128)(2,1)S(1)}, u32[]{:S(2)}, u32[]{:S(2)}) collective-permute-start(bf16[128,2560]{1,0:T(8,128)(2,1)S(1)} %get-tuple-element.34.gate), channel_id=1, source_target_pairs={{1,0},{2,1},{3,2},{4,3},{5,4},{6,5},{7,6},{9,8},{10,9},{11,10},{12... | collective-permute-start | bytes 1966088 | tf_op jit(solution)/shard_map/ppermute | solution.py:440
  29.9 0.0 copy-done.2
  29.9 1.6 %gates.3 = (bf16[128,1536]{1,0:T(8,128)(2,1)S(1)}, bf16[128,1536]{1,0:T(8,128)(2,1)S(1)}, bf16[128,1536]{1,0:T(8,128)(2,1)S(1)}, bf16[128,1536]{1,0:T(8,128)(2,1)S(1)}) custom-call(f32[32,32,128]{2,1,0:T(8,128)S(1)} %get-tuple-element.32.g_ref.table, bf16[1,128,12288]{2,1,0:T(8,128)(2,1)S(1)} %copy-done, bf16[16,12288]{1,0:T(8,128)(2,1)S(1)} %collective-permute-done.before, ...), custom_call_target="tpu_custom_call" | custom-call | flops 35389440 | bytes 3145728 | tf_op jit(solution)/shard_map/gates/pallas_call | solution.py:127
  31.4 4.6 %collective-permute-start.3 = (bf16[128,1536]{1,0:T(8,128)(2,1)S(1)}, bf16[128,1536]{1,0:T(8,128)(2,1)S(1)}, u32[]{:S(2)}, u32[]{:S(2)}) collective-permute-start(bf16[128,1536]{1,0:T(8,128)(2,1)S(1)} %get-tuple-element.40.prod), channel_id=1, source_target_pairs={{0,1},{1,2},{2,3},{3,4},{4,5},{5,6},{6,7},{8,9},{9,10},{10,11},{11... | collective-permute-start | bytes 1179656 | tf_op jit(solution)/shard_map/ppermute | solution.py:440
  36.0 1.3 %collective-permute-start.4 = (bf16[128,1536]{1,0:T(8,128)(2,1)S(1)}, bf16[128,1536]{1,0:T(8,128)(2,1)S(1)}, u32[]{:S(2)}, u32[]{:S(2)}) collective-permute-start(bf16[128,1536]{1,0:T(8,128)(2,1)S(1)} %get-tuple-element.41.gate), channel_id=1, source_target_pairs={{1,0},{2,1},{3,2},{4,3},{5,4},{6,5},{7,6},{9,8},{10,9},{11,10},{12... | collective-permute-start | bytes 1179656 | tf_op jit(solution)/shard_map/ppermute | solution.py:440
  37.3 1.4 %bands.1 = (bf16[32,128,256]{2,1,0:T(8,128)(2,1)S(1)}, bf16[32,128,256]{2,1,0:T(8,128)(2,1)S(1)}) custom-call(f32[32,32,128]{2,1,0:T(8,128)S(1)} %get-tuple-element.32.g_ref.table), custom_call_target="tpu_custom_call" | custom-call | flops 400000000 | bytes 4000000 | tf_op jit(solution)/shard_map/bands/pallas_call | solution.py:183
  38.7 4.8 %collective-permute-done.1.prior = bf16[128,2560]{1,0:T(8,128)(2,1)S(1)} collective-permute-done((bf16[128,2560]{1,0:T(8,128)(2,1)S(1)}, bf16[128,2560]{1,0:T(8,128)(2,1)S(1)}, u32[]{:S(2)}, u32[]{:S(2)}) %collective-permute-start.1) | collective-permute-done | bytes 655392 | tf_op jit(solution)/shard_map/ppermute | solution.py:440
  43.5 4.5 %collective-permute-done.2.ahead = bf16[128,2560]{1,0:T(8,128)(2,1)S(1)} collective-permute-done((bf16[128,2560]{1,0:T(8,128)(2,1)S(1)}, bf16[128,2560]{1,0:T(8,128)(2,1)S(1)}, u32[]{:S(2)}, u32[]{:S(2)}) %collective-permute-start.2) | collective-permute-done | bytes 655392 | tf_op jit(solution)/shard_map/ppermute | solution.py:440
  48.0 8.4 %back.2 = (bf16[3,128,2560]{2,1,0:T(8,128)(2,1)S(1)}, f32[3,20,16,128]{3,2,1,0:T(8,128)S(1)}, bf16[3,8,2560]{2,1,0:T(8,128)(2,1)S(1)}, f32[3,20,8,128]{3,2,1,0:T(8,128)S(1)}, f32[20,16,128]{2,1,0:T(8,128)S(1)}) custom-call(f32[32,32,128]{2,1,0:T(8,128)S(1)} %get-tuple-element.32.g_ref.table, bf16[1,128,12288]{2,1,0:T(8,128)(2,1)S(1)} %copy-done, ...), custom_call_target="tpu_custom_call" | custom-call | flops 589824000 | bytes 7864320 | tf_op jit(solution)/shard_map/back/pallas_call | solution.py:304
  56.4 0.0 collective-permute-done.3.prior
  56.4 0.0 collective-permute-done.4.ahead
  56.4 5.1 %back.3 = (bf16[3,128,1536]{2,1,0:T(8,128)(2,1)S(1)}, f32[3,12,16,128]{3,2,1,0:T(8,128)S(1)}, bf16[3,8,4096]{2,1,0:T(8,128)(2,1)S(1)}, f32[3,12,8,128]{3,2,1,0:T(8,128)S(1)}, f32[12,16,128]{2,1,0:T(8,128)S(1)}) custom-call(f32[32,32,128]{2,1,0:T(8,128)S(1)} %get-tuple-element.32.g_ref.table, bf16[1,128,12288]{2,1,0:T(8,128)(2,1)S(1)} %copy-done, ...), custom_call_target="tpu_custom_call" | custom-call | flops 353894400 | bytes 4718592 | tf_op jit(solution)/shard_map/back/pallas_call | solution.py:304
  61.6 0.0 copy-start.3
  61.6 1.0 %copy-done.3 = bf16[3,128,1536]{2,1,0:T(8,128)(2,1)} copy-done((bf16[3,128,1536]{2,1,0:T(8,128)(2,1)}, bf16[3,128,1536]{2,1,0:T(8,128)(2,1)S(1)}, u32[]{:S(2)}) %copy-start.3) | copy-done | bytes 1179672
  62.6 0.0 copy-start.6
  62.6 0.8 bundle.1
  63.3 0.0 copy-done.6
  63.3 5.1 %all-to-all-start.1 = ((bf16[32,32,128]{2,1,0:T(8,128)(2,1)}), bf16[32,32,128]{2,1,0:T(8,128)(2,1)S(1)}, u32[]{:S(2)}, u32[]{:S(2)}) async-start(bf16[32,32,128]{2,1,0:T(8,128)(2,1)} %bundle.1), calls=%async_computation.1 | async-start | bytes 524288 | tf_op jit(solution)/shard_map/all_to_all | solution.py:467
  68.4 1.3 %collective-permute-start.5 = (bf16[3,8,4096]{2,1,0:T(8,128)(2,1)}, bf16[3,8,4096]{2,1,0:T(8,128)(2,1)}, u32[]{:S(2)}, u32[]{:S(2)}) collective-permute-start(bf16[3,8,4096]{2,1,0:T(8,128)(2,1)} %copy-done.6), channel_id=1, source_target_pairs={{1,0},{2,1},{3,2},{4,3},{5,4},{6,5},{7,6},{9,8},{10,9},{11,10},{12... | collective-permute-start | bytes 589832 | tf_op jit(solution)/shard_map/ppermute | solution.py:440
  69.7 6.4 %all-to-all-done.1.parts_ref = bf16[32,32,128]{2,1,0:T(8,128)(2,1)S(1)} async-done(((bf16[32,32,128]{2,1,0:T(8,128)(2,1)}), bf16[32,32,128]{2,1,0:T(8,128)(2,1)S(1)}, u32[]{:S(2)}, u32[]{:S(2)}) %all-to-all-start.1) | async-done | bytes 262176 | tf_op jit(solution)/shard_map/all_to_all | solution.py:467
  76.2 0.0 copy-start.5
  76.2 0.6 copy-done.5
  76.8 7.4 %all-to-all-start.2 = ((bf16[8,32,128]{2,1,0:T(8,128)(2,1)}), bf16[8,32,128]{2,1,0:T(8,128)(2,1)S(1)}, u32[]{:S(2)}, u32[]{:S(2)}) async-start(bf16[8,32,128]{2,1,0:T(8,128)(2,1)} %copy-done.5), calls=%async_computation.2 | async-start | bytes 131072 | tf_op jit(solution)/shard_map/all_to_all | solution.py:468
  84.2 0.0 collective-permute-done.5.refs_4_
  84.2 0.0 copy-start.4
  84.2 1.3 %copy-done.4 = bf16[3,128,1536]{2,1,0:T(8,128)(2,1)S(1)} copy-done((bf16[3,128,1536]{2,1,0:T(8,128)(2,1)S(1)}, bf16[3,128,1536]{2,1,0:T(8,128)(2,1)}, u32[]{:S(2)}) %copy-start.4) | copy-done | bytes 1179672
  85.5 2.6 %finish.1 = bf16[1,128,12288]{2,1,0:T(8,128)(2,1)} custom-call(f32[32,32,128]{2,1,0:T(8,128)S(1)} %get-tuple-element.32.g_ref.table, bf16[3,128,2560]{2,1,0:T(8,128)(2,1)S(1)} %get-tuple-element.39.refs_0_, bf16[3,128,1536]{2,1,0:T(8,128)(2,1)S(1)} %copy-done.4, f32[3,20,16,128]{3,2,1,0:T(8,128)S(1)} %get-tuple-element.46.refs_2_, ...), custom_call_target="tpu_custom_call" | custom-call | flops 10000000 | bytes 2000000 | tf_op jit(solution)/shard_map/finish/pallas_call | solution.py:361
  88.1 4.5 %all-to-all-done.2.parts_ref = bf16[8,32,128]{2,1,0:T(8,128)(2,1)S(1)} async-done(((bf16[8,32,128]{2,1,0:T(8,128)(2,1)}), bf16[8,32,128]{2,1,0:T(8,128)(2,1)S(1)}, u32[]{:S(2)}, u32[]{:S(2)}) %all-to-all-start.2) | async-done | bytes 65568 | tf_op jit(solution)/shard_map/all_to_all | solution.py:468
  92.6 0.6 spread.1
  (1 shorter events, 0.0 us)
Async XLA Ops:
  0.6 20.2 %copy-start = (bf16[1,128,12288]{2,1,0:T(8,128)(2,1)S(1)}, bf16[1,128,12288]{2,1,0:T(8,128)(2,1)}, u32[]{:S(2)}) copy-start(bf16[1,128,12288]{2,1,0:T(8,128)(2,1)} %streams.7) | copy-start | bytes 9437188
  1.9 19.0 %collective-permute-start = (bf16[16,12288]{1,0:T(8,128)(2,1)S(1)}, bf16[16,12288]{1,0:T(8,128)(2,1)S(1)}, u32[]{:S(2)}, u32[]{:S(2)}) collective-permute-start(bf16[16,12288]{1,0:T(8,128)(2,1)S(1)} %get-tuple-element.31), channel_id=1, source_target_pairs={{0,1},{1,2},{2,3},{3,4},{4,5},{5,6},{6,7},{8,9},{9,10},{10,11},{11... | collective-permute-start | bytes 1179656 | tf_op jit(solution)/shard_map/ppermute | solution.py:440
  20.9 1.2 %copy-start.1 = (bf16[1,128,4096]{2,1,0:T(8,128)(2,1)S(1)}, bf16[1,128,4096]{2,1,0:T(8,128)(2,1)}, u32[]{:S(2)}) copy-start(bf16[1,128,4096]{2,1,0:T(8,128)(2,1)} %cot.7) | copy-start | bytes 3145732
  22.1 7.8 %copy-start.2 = (bf16[1,128,4096]{2,1,0:T(8,128)(2,1)S(1)}, bf16[1,128,4096]{2,1,0:T(8,128)(2,1)}, u32[]{:S(2)}) copy-start(bf16[1,128,4096]{2,1,0:T(8,128)(2,1)} %cot.7) | copy-start | bytes 3145732
  24.7 18.8 %collective-permute-start.1 = (bf16[128,2560]{1,0:T(8,128)(2,1)S(1)}, bf16[128,2560]{1,0:T(8,128)(2,1)S(1)}, u32[]{:S(2)}, u32[]{:S(2)}) collective-permute-start(bf16[128,2560]{1,0:T(8,128)(2,1)S(1)} %get-tuple-element.33.prod), channel_id=1, source_target_pairs={{0,1},{1,2},{2,3},{3,4},{4,5},{5,6},{6,7},{8,9},{9,10},{10,11},{11... | collective-permute-start | bytes 1966088 | tf_op jit(solution)/shard_map/ppermute | solution.py:440
  28.6 19.5 %collective-permute-start.2 = (bf16[128,2560]{1,0:T(8,128)(2,1)S(1)}, bf16[128,2560]{1,0:T(8,128)(2,1)S(1)}, u32[]{:S(2)}, u32[]{:S(2)}) collective-permute-start(bf16[128,2560]{1,0:T(8,128)(2,1)S(1)} %get-tuple-element.34.gate), channel_id=1, source_target_pairs={{1,0},{2,1},{3,2},{4,3},{5,4},{6,5},{7,6},{9,8},{10,9},{11,10},{12... | collective-permute-start | bytes 1966088 | tf_op jit(solution)/shard_map/ppermute | solution.py:440
  31.4 25.0 %collective-permute-start.3 = (bf16[128,1536]{1,0:T(8,128)(2,1)S(1)}, bf16[128,1536]{1,0:T(8,128)(2,1)S(1)}, u32[]{:S(2)}, u32[]{:S(2)}) collective-permute-start(bf16[128,1536]{1,0:T(8,128)(2,1)S(1)} %get-tuple-element.40.prod), channel_id=1, source_target_pairs={{0,1},{1,2},{2,3},{3,4},{4,5},{5,6},{6,7},{8,9},{9,10},{10,11},{11... | collective-permute-start | bytes 1179656 | tf_op jit(solution)/shard_map/ppermute | solution.py:440
  36.0 20.4 %collective-permute-start.4 = (bf16[128,1536]{1,0:T(8,128)(2,1)S(1)}, bf16[128,1536]{1,0:T(8,128)(2,1)S(1)}, u32[]{:S(2)}, u32[]{:S(2)}) collective-permute-start(bf16[128,1536]{1,0:T(8,128)(2,1)S(1)} %get-tuple-element.41.gate), channel_id=1, source_target_pairs={{1,0},{2,1},{3,2},{4,3},{5,4},{6,5},{7,6},{9,8},{10,9},{11,10},{12... | collective-permute-start | bytes 1179656 | tf_op jit(solution)/shard_map/ppermute | solution.py:440
  61.6 1.0 %copy-start.3 = (bf16[3,128,1536]{2,1,0:T(8,128)(2,1)}, bf16[3,128,1536]{2,1,0:T(8,128)(2,1)S(1)}, u32[]{:S(2)}) copy-start(bf16[3,128,1536]{2,1,0:T(8,128)(2,1)S(1)} %get-tuple-element.45.refs_1_) | copy-start | bytes 3538948
  62.6 0.8 copy-start.6
  63.3 12.8 %all-to-all-start.1 = ((bf16[32,32,128]{2,1,0:T(8,128)(2,1)}), bf16[32,32,128]{2,1,0:T(8,128)(2,1)S(1)}, u32[]{:S(2)}, u32[]{:S(2)}) async-start(bf16[32,32,128]{2,1,0:T(8,128)(2,1)} %bundle.1), calls=%async_computation.1 | async-start | bytes 524288 | tf_op jit(solution)/shard_map/all_to_all | solution.py:467
  68.4 15.8 %collective-permute-start.5 = (bf16[3,8,4096]{2,1,0:T(8,128)(2,1)}, bf16[3,8,4096]{2,1,0:T(8,128)(2,1)}, u32[]{:S(2)}, u32[]{:S(2)}) collective-permute-start(bf16[3,8,4096]{2,1,0:T(8,128)(2,1)} %copy-done.6), channel_id=1, source_target_pairs={{1,0},{2,1},{3,2},{4,3},{5,4},{6,5},{7,6},{9,8},{10,9},{11,10},{12... | collective-permute-start | bytes 589832 | tf_op jit(solution)/shard_map/ppermute | solution.py:440
  76.2 0.6 copy-start.5
  76.8 15.8 %all-to-all-start.2 = ((bf16[8,32,128]{2,1,0:T(8,128)(2,1)}), bf16[8,32,128]{2,1,0:T(8,128)(2,1)S(1)}, u32[]{:S(2)}, u32[]{:S(2)}) async-start(bf16[8,32,128]{2,1,0:T(8,128)(2,1)} %copy-done.5), calls=%async_computation.2 | async-start | bytes 131072 | tf_op jit(solution)/shard_map/all_to_all | solution.py:468
  84.2 1.3 %copy-start.4 = (bf16[3,128,1536]{2,1,0:T(8,128)(2,1)S(1)}, bf16[3,128,1536]{2,1,0:T(8,128)(2,1)}, u32[]{:S(2)}) copy-start(bf16[3,128,1536]{2,1,0:T(8,128)(2,1)} %copy-done.3) | copy-start | bytes 3538948

commit v4 on v3

--- a/solution.py
+++ b/solution.py
@@ -22,6 +22,10 @@
 
 def params(mib):
     return pltpu.CompilerParams(vmem_limit_bytes=mib * 1024 * 1024)
+
+
+def lasting(us):
+    return pl.CostEstimate(flops=int(us * 1.1e9), bytes_accessed=0, transcendentals=0)
 
 
 def whole():
@@ -90,52 +94,57 @@
     return running
 
 
-def gates_kernel(first, lead, count, g_ref, streams, before, cot, *rest):
+def gates_kernel(first, lead, count, g_ref, streams, before, cot_hbm, *rest):
+    rest = rest if lead else rest[1:]
     if lead:
-        prod, gate, key, val, table, ext = rest
+        prod, gate, key, val, table, ext, cot, sem = rest
         table[...] = g_ref[...].astype(F32)
     else:
-        prod, gate, key, val, ext = rest
+        prod, gate, key, val, ext, cot, sem = rest
         table = g_ref
-
-    def some(step, _):
-        for t in range(UNROLL):
-            here = step * UNROLL + t
-            tile = first // LANES + here
-            cols = lanes_of(here)
-            mixed = []
-            for part in range(3):
-                whence = lanes_of(tile + part * count)
-                taps = taps_of(table, tile + part * count)
-                halo = before[:, whence].astype(F32)[8:16]
-                mixed.append(mixture(ext.at[t, part], halo, streams[0, :, whence], taps))
-            prod[:, cols] = (mixed[1] * mixed[2]).astype(BF)
-            gate[:, cols] = (cot[0, :, lanes_of(tile)].astype(F32) * mixed[0]).astype(BF)
-            key[:, cols] = mixed[1].astype(BF)
-            val[:, cols] = mixed[2].astype(BF)
-        return 0
-
-    for step in range(prod.shape[1] // LANES // UNROLL):
-        some(step, 0)
-
-
-def gates(first, width, table, streams, before, grad_out, lead):
+    width = prod.shape[1]
+    copy = pltpu.make_async_copy(cot_hbm.at[0, :, pl.ds(first, width)], cot, sem)
+    copy.start()
+
+    def feature(part, here):
+        tile = first // LANES + here + part * count
+        whence = lanes_of(tile)
+        return mixture(
+            ext.at[here % UNROLL, part], before[:, whence].astype(F32)[8:16], streams[0, :, whence], taps_of(table, tile)
+        )
+
+    for here in range(width // LANES):
+        cols = lanes_of(here)
+        keys, values = feature(1, here), feature(2, here)
+        prod[:, cols] = (keys * values).astype(BF)
+        key[:, cols] = keys.astype(BF)
+        val[:, cols] = values.astype(BF)
+    copy.wait()
+    for here in range(width // LANES):
+        cols = lanes_of(here)
+        gate[:, cols] = (cot[:, cols].astype(F32) * feature(0, here)).astype(BF)
+
+
+def gates(first, width, table, streams, before, grad_out, *later):
     count = grad_out.shape[2] // LANES
+    lead = not later
     outs = [jax.ShapeDtypeStruct((ROWS, width), BF)] * 4
     if lead:
         outs.append(jax.ShapeDtypeStruct(table.shape, F32))
     return pl.pallas_call(
         functools.partial(gates_kernel, first, lead, count),
         out_shape=tuple(outs),
-        in_specs=[whole()] * 4,
+        in_specs=[whole()] * 3 + [anywhere()] * (1 + len(later)),
         out_specs=(whole(),) * len(outs),
-        scratch_shapes=[pltpu.VMEM((UNROLL, 3, 8 + ROWS, LANES), F32)],
-        compiler_params=params(FULL),
-        cost_estimate=pl.CostEstimate(
-            flops=60 * 3 * ROWS * width, bytes_accessed=16 * ROWS * width, transcendentals=0
-        ),
+        scratch_shapes=[
+            pltpu.VMEM((UNROLL, 3, 8 + ROWS, LANES), F32),
+            pltpu.VMEM((ROWS, width), BF),
+            pltpu.SemaphoreType.DMA,
+        ],
+        compiler_params=params(FULL),
+        cost_estimate=lasting(width / 1024),
         name="gates",
-    )(table, streams, before, grad_out)
+    )(table, streams, before, in_hbm(grad_out), *later)
 
 
 def windows(block, pair):
@@ -187,7 +196,7 @@
         in_specs=[pl.BlockSpec(gathered.shape, lambda i: (0, 0, 0))],
         out_specs=(spec, spec),
         compiler_params=params(FULL),
-        cost_estimate=pl.CostEstimate(flops=400000000, bytes_accessed=4000000, transcendentals=0),
+        cost_estimate=lasting(1.4),
         name="bands",
     )(gathered)
 
@@ -311,9 +320,7 @@
             pltpu.VMEM((UNROLL, 8 * PIECE, 2 * LANES), F32),
         ],
         compiler_params=params(FULL),
-        cost_estimate=pl.CostEstimate(
-            flops=600 * 3 * ROWS * width, bytes_accessed=24 * ROWS * width, transcendentals=0
-        ),
+        cost_estimate=lasting(3.4 * width / 1024),
         name="back",
     )(table, streams, before, grad_out, *made, prior, ahead, *filters, *earlier)
 
@@ -365,7 +372,7 @@
         out_specs=anywhere(),
         scratch_shapes=[pltpu.VMEM((16, shape[2]), BF), pltpu.SemaphoreType.DMA((3 * chunks + 1,))],
         compiler_params=params(FULL),
-        cost_estimate=pl.CostEstimate(flops=10000000, bytes_accessed=2000000, transcendentals=0),
+        cost_estimate=lasting(2.6),
         name="finish",
     )(table, *pieces, *tails, after)
 
@@ -450,14 +457,14 @@
     before = passed_along(tail_rows, "seq", 1)
     gathered = lax.all_to_all(payload, "dp", 0, 0, tiled=True)
     work = []
-    table, first = gathered, 0
+    table, first, filters = gathered, 0, ()
     for width in CHUNKS:
-        made = gates(first, width, table, streams, before, grad_out, first == 0)
+        made = gates(first, width, table, streams, before, grad_out, *filters[:1])
         if first == 0:
             table = made[4]
+            filters = bands(table)
         work.append((first, width, made[:4], passed_along(made[0], "seq", 1), passed_along(made[1], "seq", -1)))
         first += width
-    filters = bands(table)
     done = []
     for first, width, made, prior, ahead in work:
         earlier = [done[-1][2]] if done else []

time: 94.5 us -> 92.8 us (0.982)
    unnamed x14 -> x12, local copies, waits for them, and re-layouts: 4.12 us -> 3.32 us
where the time goes in v4:
time: 92.8 us; the launch traced here: 91.6 us
  starting transfers between devices  28.8 us (31%)
  Pallas kernels  23.5 us (25%)
  waiting for transfers between devices  20 us (22%)
  blocking collectives  15.1 us (16%)
  local copies, waits for them, and re-layouts  3.32 us (4%)
    ppermute x6, starting transfers between devices, passed_along(): return lax.ppermute(block, axis, route)  16.3 us
    all_to_all x1, blocking collectives, local(): gathered = lax.all_to_all(payload, 'dp', 0, 0, tiled=True)  15.1 us
    pallas_call x2, Pallas kernels, back(): pl.pallas_call(functools.partial(back_kernel, first, count), out_shape=ou...  13.2 us
    ppermute x6, waiting for transfers between devices, passed_along(): return lax.ppermute(block, axis, route)  9.26 us
    all_to_all x1, starting transfers between devices, local(): parts = lax.all_to_all(parts, 'seq', 0, 0, tiled=True)  7.4 us
    all_to_all x1, waiting for transfers between devices, local(): lax.all_to_all(bundle(shorts, longs, shards), 'dp', 0, 0, tiled=True)  6.4 us
    all_to_all x1, starting transfers between devices, local(): lax.all_to_all(bundle(shorts, longs, shards), 'dp', 0, 0, tiled=True)  5.08 us
    all_to_all x1, waiting for transfers between devices, local(): parts = lax.all_to_all(parts, 'seq', 0, 0, tiled=True)  4.35 us
  transfers between devices with their start and end apart: 8, of which 4 were waited for; matrix products, arithmetic and copies ran while one was open for 0% of the time, Pallas kernels for 15%

profile of v4, /device:TPU:2, one launch (start us, length us, event | category | flops | bytes accessed | tf_op | source)
XLA Modules:
  0.0 91.6 jit_solution(5935525250799258342)
XLA Ops:
  0.6 0.0 copy-start
  0.6 1.2 %pack.1 = (bf16[32,32,128]{2,1,0:T(8,128)(2,1)S(1)}, bf16[16,12288]{1,0:T(8,128)(2,1)S(1)}) custom-call(bf16[7,384]{1,0:T(8,128)(2,1)} %short_ref.1, bf16[8,128]{1,0:T(8,128)(2,1)} %long_ref.1, bf16[1,128]{1,0:T(2,128)(2,1)} %bitcast.2, bf16[1,128,12288]{2,1,0:T(8,128)(2,1)} %streams.7), custom_call_target="tpu_custom_call" | custom-call | tf_op jit(solution)/shard_map/pack/pallas_call | solution.py:57
  1.9 3.8 %collective-permute-start = (bf16[16,12288]{1,0:T(8,128)(2,1)S(1)}, bf16[16,12288]{1,0:T(8,128)(2,1)S(1)}, u32[]{:S(2)}, u32[]{:S(2)}) collective-permute-start(bf16[16,12288]{1,0:T(8,128)(2,1)S(1)} %get-tuple-element.31), channel_id=1, source_target_pairs={{0,1},{1,2},{2,3},{3,4},{4,5},{5,6},{6,7},{8,9},{9,10},{10,11},{11... | collective-permute-start | bytes 1179656 | tf_op jit(solution)/shard_map/ppermute | solution.py:447
  5.7 15.1 %all_to_all.15.g_ref = bf16[32,32,128]{2,1,0:T(8,128)(2,1)S(1)} all-to-all(bf16[32,32,128]{2,1,0:T(8,128)(2,1)S(1)} %get-tuple-element.30), channel_id=1, replica_groups=mesh['dp'=32,'seq'=8] {'dp'}, dimensions={0} | all-to-all | bytes 524288 | tf_op jit(solution)/shard_map/all_to_all | solution.py:458
  20.8 0.0 collective-permute-done.before
  20.9 0.0 copy-done
  20.9 2.5 %gates.2 = (bf16[128,2560]{1,0:T(8,128)(2,1)S(1)}, bf16[128,2560]{1,0:T(8,128)(2,1)S(1)}, bf16[128,2560]{1,0:T(8,128)(2,1)S(1)}, bf16[128,2560]{1,0:T(8,128)(2,1)S(1)}, f32[32,32,128]{2,1,0:T(8,128)S(1)}) custom-call(bf16[32,32,128]{2,1,0:T(8,128)(2,1)S(1)} %all_to_all.15.g_ref, bf16[1,128,12288]{2,1,0:T(8,128)(2,1)S(1)} %copy-done, ...), custom_call_target="tpu_custom_call" | custom-call | flops 2750000128 | tf_op jit(solution)/shard_map/gates/pallas_call | solution.py:134
  23.4 3.8 %collective-permute-start.1 = (bf16[128,2560]{1,0:T(8,128)(2,1)S(1)}, bf16[128,2560]{1,0:T(8,128)(2,1)S(1)}, u32[]{:S(2)}, u32[]{:S(2)}) collective-permute-start(bf16[128,2560]{1,0:T(8,128)(2,1)S(1)} %get-tuple-element.33.prod), channel_id=1, source_target_pairs={{0,1},{1,2},{2,3},{3,4},{4,5},{5,6},{6,7},{8,9},{9,10},{10,11},{11... | collective-permute-start | bytes 1966088 | tf_op jit(solution)/shard_map/ppermute | solution.py:447
  27.3 1.3 %collective-permute-start.2 = (bf16[128,2560]{1,0:T(8,128)(2,1)S(1)}, bf16[128,2560]{1,0:T(8,128)(2,1)S(1)}, u32[]{:S(2)}, u32[]{:S(2)}) collective-permute-start(bf16[128,2560]{1,0:T(8,128)(2,1)S(1)} %get-tuple-element.34.gate), channel_id=1, source_target_pairs={{1,0},{2,1},{3,2},{4,3},{5,4},{6,5},{7,6},{9,8},{10,9},{11,10},{12... | collective-permute-start | bytes 1966088 | tf_op jit(solution)/shard_map/ppermute | solution.py:447
  28.6 1.2 %bands.1 = (bf16[32,128,256]{2,1,0:T(8,128)(2,1)S(1)}, bf16[32,128,256]{2,1,0:T(8,128)(2,1)S(1)}) custom-call(f32[32,32,128]{2,1,0:T(8,128)S(1)} %get-tuple-element.32.g_ref.table), custom_call_target="tpu_custom_call" | custom-call | flops 1540000000 | tf_op jit(solution)/shard_map/bands/pallas_call | solution.py:192
  29.8 0.0 copy-start.1
  29.8 1.6 %gates.3 = (bf16[128,1536]{1,0:T(8,128)(2,1)S(1)}, bf16[128,1536]{1,0:T(8,128)(2,1)S(1)}, bf16[128,1536]{1,0:T(8,128)(2,1)S(1)}, bf16[128,1536]{1,0:T(8,128)(2,1)S(1)}) custom-call(f32[32,32,128]{2,1,0:T(8,128)S(1)} %get-tuple-element.32.g_ref.table, bf16[1,128,12288]{2,1,0:T(8,128)(2,1)S(1)} %copy-done, bf16[16,12288]{1,0:T(8,128)(2,1)S(1)} %collective-permute-done.before, ...), custom_call_target="tpu_custom_call" | custom-call | flops 1650000000 | tf_op jit(solution)/shard_map/gates/pallas_call | solution.py:134
  31.4 4.6 %collective-permute-start.3 = (bf16[128,1536]{1,0:T(8,128)(2,1)S(1)}, bf16[128,1536]{1,0:T(8,128)(2,1)S(1)}, u32[]{:S(2)}, u32[]{:S(2)}) collective-permute-start(bf16[128,1536]{1,0:T(8,128)(2,1)S(1)} %get-tuple-element.40.prod), channel_id=1, source_target_pairs={{0,1},{1,2},{2,3},{3,4},{4,5},{5,6},{6,7},{8,9},{9,10},{10,11},{11... | collective-permute-start | bytes 1179656 | tf_op jit(solution)/shard_map/ppermute | solution.py:447
  36.0 1.5 %collective-permute-start.4 = (bf16[128,1536]{1,0:T(8,128)(2,1)S(1)}, bf16[128,1536]{1,0:T(8,128)(2,1)S(1)}, u32[]{:S(2)}, u32[]{:S(2)}) collective-permute-start(bf16[128,1536]{1,0:T(8,128)(2,1)S(1)} %get-tuple-element.41.gate), channel_id=1, source_target_pairs={{1,0},{2,1},{3,2},{4,3},{5,4},{6,5},{7,6},{9,8},{10,9},{11,10},{12... | collective-permute-start | bytes 1179656 | tf_op jit(solution)/shard_map/ppermute | solution.py:447
  37.5 4.8 %collective-permute-done.1.prior = bf16[128,2560]{1,0:T(8,128)(2,1)S(1)} collective-permute-done((bf16[128,2560]{1,0:T(8,128)(2,1)S(1)}, bf16[128,2560]{1,0:T(8,128)(2,1)S(1)}, u32[]{:S(2)}, u32[]{:S(2)}) %collective-permute-start.1) | collective-permute-done | bytes 655392 | tf_op jit(solution)/shard_map/ppermute | solution.py:447
  42.3 4.5 %collective-permute-done.2.ahead = bf16[128,2560]{1,0:T(8,128)(2,1)S(1)} collective-permute-done((bf16[128,2560]{1,0:T(8,128)(2,1)S(1)}, bf16[128,2560]{1,0:T(8,128)(2,1)S(1)}, u32[]{:S(2)}, u32[]{:S(2)}) %collective-permute-start.2) | collective-permute-done | bytes 655392 | tf_op jit(solution)/shard_map/ppermute | solution.py:447
  46.7 0.0 copy-done.1
  46.7 8.2 %back.2 = (bf16[3,128,2560]{2,1,0:T(8,128)(2,1)S(1)}, f32[3,20,16,128]{3,2,1,0:T(8,128)S(1)}, bf16[3,8,2560]{2,1,0:T(8,128)(2,1)S(1)}, f32[3,20,8,128]{3,2,1,0:T(8,128)S(1)}, f32[20,16,128]{2,1,0:T(8,128)S(1)}) custom-call(f32[32,32,128]{2,1,0:T(8,128)S(1)} %get-tuple-element.32.g_ref.table, bf16[1,128,12288]{2,1,0:T(8,128)(2,1)S(1)} %copy-done, ...), custom_call_target="tpu_custom_call" | custom-call | flops 9349999616 | tf_op jit(solution)/shard_map/back/pallas_call | solution.py:313
  54.9 0.0 copy-start.4
  54.9 0.0 collective-permute-done.3.prior
  55.0 0.0 collective-permute-done.4.ahead
  55.0 5.0 %back.3 = (bf16[3,128,1536]{2,1,0:T(8,128)(2,1)S(1)}, f32[3,12,16,128]{3,2,1,0:T(8,128)S(1)}, bf16[3,8,4096]{2,1,0:T(8,128)(2,1)S(1)}, f32[3,12,8,128]{3,2,1,0:T(8,128)S(1)}, f32[12,16,128]{2,1,0:T(8,128)S(1)}) custom-call(f32[32,32,128]{2,1,0:T(8,128)S(1)} %get-tuple-element.32.g_ref.table, bf16[1,128,12288]{2,1,0:T(8,128)(2,1)S(1)} %copy-done, ...), custom_call_target="tpu_custom_call" | custom-call | flops 5609999872 | tf_op jit(solution)/shard_map/back/pallas_call | solution.py:313
  59.9 0.0 copy-done.4
  59.9 0.0 copy-start.2
  60.0 1.0 %copy-done.2 = bf16[3,128,1536]{2,1,0:T(8,128)(2,1)} copy-done((bf16[3,128,1536]{2,1,0:T(8,128)(2,1)}, bf16[3,128,1536]{2,1,0:T(8,128)(2,1)S(1)}, u32[]{:S(2)}) %copy-start.2) | copy-done | bytes 1179672
  61.0 0.7 bundle.1
  61.7 5.1 %all-to-all-start.1 = ((bf16[32,32,128]{2,1,0:T(8,128)(2,1)}), bf16[32,32,128]{2,1,0:T(8,128)(2,1)S(1)}, u32[]{:S(2)}, u32[]{:S(2)}) async-start(bf16[32,32,128]{2,1,0:T(8,128)(2,1)} %bundle.1), calls=%async_computation.1 | async-start | bytes 524288 | tf_op jit(solution)/shard_map/all_to_all | solution.py:474
  66.8 1.3 %collective-permute-start.5 = (bf16[3,8,4096]{2,1,0:T(8,128)(2,1)S(1)}, bf16[3,8,4096]{2,1,0:T(8,128)(2,1)S(1)}, u32[]{:S(2)}, u32[]{:S(2)}) collective-permute-start(bf16[3,8,4096]{2,1,0:T(8,128)(2,1)S(1)} %get-tuple-element.48), channel_id=1, source_target_pairs={{1,0},{2,1},{3,2},{4,3},{5,4},{6,5},{7,6},{9,8},{10,9},{11,10},{12... | collective-permute-start | bytes 589832 | tf_op jit(solution)/shard_map/ppermute | solution.py:447
  68.1 6.4 %all-to-all-done.1.parts_ref = bf16[32,32,128]{2,1,0:T(8,128)(2,1)S(1)} async-done(((bf16[32,32,128]{2,1,0:T(8,128)(2,1)}), bf16[32,32,128]{2,1,0:T(8,128)(2,1)S(1)}, u32[]{:S(2)}, u32[]{:S(2)}) %all-to-all-start.1) | async-done | bytes 262176 | tf_op jit(solution)/shard_map/all_to_all | solution.py:474
  74.5 0.7 total.1
  75.2 7.4 %all-to-all-start.2 = ((bf16[8,32,128]{2,1,0:T(8,128)(2,1)}), bf16[8,32,128]{2,1,0:T(8,128)(2,1)S(1)}, u32[]{:S(2)}, u32[]{:S(2)}) async-start(bf16[8,32,128]{2,1,0:T(8,128)(2,1)} %total.1), calls=%async_computation.2 | async-start | bytes 131072 | tf_op jit(solution)/shard_map/all_to_all | solution.py:475
  82.6 0.0 collective-permute-done.5.refs_4_
  82.6 0.0 copy-start.3
  82.6 1.3 %copy-done.3 = bf16[3,128,1536]{2,1,0:T(8,128)(2,1)S(1)} copy-done((bf16[3,128,1536]{2,1,0:T(8,128)(2,1)S(1)}, bf16[3,128,1536]{2,1,0:T(8,128)(2,1)}, u32[]{:S(2)}) %copy-start.3) | copy-done | bytes 1179672
  83.9 0.0 copy-start.5
  83.9 1.0 %copy-done.5 = f32[3,20,16,128]{3,2,1,0:T(8,128)S(1)} copy-done((f32[3,20,16,128]{3,2,1,0:T(8,128)S(1)}, f32[3,20,16,128]{3,2,1,0:T(8,128)}, u32[]{:S(2)}) %copy-start.5) | copy-done | bytes 491544
  84.9 1.7 %finish.1 = bf16[1,128,12288]{2,1,0:T(8,128)(2,1)} custom-call(f32[32,32,128]{2,1,0:T(8,128)S(1)} %get-tuple-element.32.g_ref.table, bf16[3,128,2560]{2,1,0:T(8,128)(2,1)S(1)} %get-tuple-element.39.refs_0_, bf16[3,128,1536]{2,1,0:T(8,128)(2,1)S(1)} %copy-done.3, f32[3,20,16,128]{3,2,1,0:T(8,128)S(1)} %copy-done.5, ...), custom_call_target="tpu_custom_call" | custom-call | flops 2860000000 | tf_op jit(solution)/shard_map/finish/pallas_call | solution.py:368
  86.6 4.3 %all-to-all-done.2.parts_ref = bf16[8,32,128]{2,1,0:T(8,128)(2,1)S(1)} async-done(((bf16[8,32,128]{2,1,0:T(8,128)(2,1)}), bf16[8,32,128]{2,1,0:T(8,128)(2,1)S(1)}, u32[]{:S(2)}, u32[]{:S(2)}) %all-to-all-start.2) | async-done | bytes 65568 | tf_op jit(solution)/shard_map/all_to_all | solution.py:475
  90.9 0.6 spread.1
Async XLA Ops:
  0.6 20.2 %copy-start = (bf16[1,128,12288]{2,1,0:T(8,128)(2,1)S(1)}, bf16[1,128,12288]{2,1,0:T(8,128)(2,1)}, u32[]{:S(2)}) copy-start(bf16[1,128,12288]{2,1,0:T(8,128)(2,1)} %streams.7) | copy-start | bytes 9437188
  1.9 19.0 %collective-permute-start = (bf16[16,12288]{1,0:T(8,128)(2,1)S(1)}, bf16[16,12288]{1,0:T(8,128)(2,1)S(1)}, u32[]{:S(2)}, u32[]{:S(2)}) collective-permute-start(bf16[16,12288]{1,0:T(8,128)(2,1)S(1)} %get-tuple-element.31), channel_id=1, source_target_pairs={{0,1},{1,2},{2,3},{3,4},{4,5},{5,6},{6,7},{8,9},{9,10},{10,11},{11... | collective-permute-start | bytes 1179656 | tf_op jit(solution)/shard_map/ppermute | solution.py:447
  23.4 18.8 %collective-permute-start.1 = (bf16[128,2560]{1,0:T(8,128)(2,1)S(1)}, bf16[128,2560]{1,0:T(8,128)(2,1)S(1)}, u32[]{:S(2)}, u32[]{:S(2)}) collective-permute-start(bf16[128,2560]{1,0:T(8,128)(2,1)S(1)} %get-tuple-element.33.prod), channel_id=1, source_target_pairs={{0,1},{1,2},{2,3},{3,4},{4,5},{5,6},{6,7},{8,9},{9,10},{10,11},{11... | collective-permute-start | bytes 1966088 | tf_op jit(solution)/shard_map/ppermute | solution.py:447
  27.3 19.5 %collective-permute-start.2 = (bf16[128,2560]{1,0:T(8,128)(2,1)S(1)}, bf16[128,2560]{1,0:T(8,128)(2,1)S(1)}, u32[]{:S(2)}, u32[]{:S(2)}) collective-permute-start(bf16[128,2560]{1,0:T(8,128)(2,1)S(1)} %get-tuple-element.34.gate), channel_id=1, source_target_pairs={{1,0},{2,1},{3,2},{4,3},{5,4},{6,5},{7,6},{9,8},{10,9},{11,10},{12... | collective-permute-start | bytes 1966088 | tf_op jit(solution)/shard_map/ppermute | solution.py:447
  29.8 17.0 %copy-start.1 = (bf16[1,128,4096]{2,1,0:T(8,128)(2,1)S(1)}, bf16[1,128,4096]{2,1,0:T(8,128)(2,1)}, u32[]{:S(2)}) copy-start(bf16[1,128,4096]{2,1,0:T(8,128)(2,1)} %cot.3) | copy-start | bytes 3145732
  31.4 23.6 %collective-permute-start.3 = (bf16[128,1536]{1,0:T(8,128)(2,1)S(1)}, bf16[128,1536]{1,0:T(8,128)(2,1)S(1)}, u32[]{:S(2)}, u32[]{:S(2)}) collective-permute-start(bf16[128,1536]{1,0:T(8,128)(2,1)S(1)} %get-tuple-element.40.prod), channel_id=1, source_target_pairs={{0,1},{1,2},{2,3},{3,4},{4,5},{5,6},{6,7},{8,9},{9,10},{10,11},{11... | collective-permute-start | bytes 1179656 | tf_op jit(solution)/shard_map/ppermute | solution.py:447
  36.0 19.0 %collective-permute-start.4 = (bf16[128,1536]{1,0:T(8,128)(2,1)S(1)}, bf16[128,1536]{1,0:T(8,128)(2,1)S(1)}, u32[]{:S(2)}, u32[]{:S(2)}) collective-permute-start(bf16[128,1536]{1,0:T(8,128)(2,1)S(1)} %get-tuple-element.41.gate), channel_id=1, source_target_pairs={{1,0},{2,1},{3,2},{4,3},{5,4},{6,5},{7,6},{9,8},{10,9},{11,10},{12... | collective-permute-start | bytes 1179656 | tf_op jit(solution)/shard_map/ppermute | solution.py:447
  54.9 5.0 %copy-start.4 = (f32[3,20,16,128]{3,2,1,0:T(8,128)}, f32[3,20,16,128]{3,2,1,0:T(8,128)S(1)}, u32[]{:S(2)}) copy-start(f32[3,20,16,128]{3,2,1,0:T(8,128)S(1)} %get-tuple-element.46.refs_2_) | copy-start | bytes 1474564
  59.9 1.0 %copy-start.2 = (bf16[3,128,1536]{2,1,0:T(8,128)(2,1)}, bf16[3,128,1536]{2,1,0:T(8,128)(2,1)S(1)}, u32[]{:S(2)}) copy-start(bf16[3,128,1536]{2,1,0:T(8,128)(2,1)S(1)} %get-tuple-element.45.refs_1_) | copy-start | bytes 3538948
  61.7 12.8 %all-to-all-start.1 = ((bf16[32,32,128]{2,1,0:T(8,128)(2,1)}), bf16[32,32,128]{2,1,0:T(8,128)(2,1)S(1)}, u32[]{:S(2)}, u32[]{:S(2)}) async-start(bf16[32,32,128]{2,1,0:T(8,128)(2,1)} %bundle.1), calls=%async_computation.1 | async-start | bytes 524288 | tf_op jit(solution)/shard_map/all_to_all | solution.py:474
  66.8 15.8 %collective-permute-start.5 = (bf16[3,8,4096]{2,1,0:T(8,128)(2,1)S(1)}, bf16[3,8,4096]{2,1,0:T(8,128)(2,1)S(1)}, u32[]{:S(2)}, u32[]{:S(2)}) collective-permute-start(bf16[3,8,4096]{2,1,0:T(8,128)(2,1)S(1)} %get-tuple-element.48), channel_id=1, source_target_pairs={{1,0},{2,1},{3,2},{4,3},{5,4},{6,5},{7,6},{9,8},{10,9},{11,10},{12... | collective-permute-start | bytes 589832 | tf_op jit(solution)/shard_map/ppermute | solution.py:447
  75.2 15.8 %all-to-all-start.2 = ((bf16[8,32,128]{2,1,0:T(8,128)(2,1)}), bf16[8,32,128]{2,1,0:T(8,128)(2,1)S(1)}, u32[]{:S(2)}, u32[]{:S(2)}) async-start(bf16[8,32,128]{2,1,0:T(8,128)(2,1)} %total.1), calls=%async_computation.2 | async-start | bytes 131072 | tf_op jit(solution)/shard_map/all_to_all | solution.py:475
  82.6 1.3 %copy-start.3 = (bf16[3,128,1536]{2,1,0:T(8,128)(2,1)S(1)}, bf16[3,128,1536]{2,1,0:T(8,128)(2,1)}, u32[]{:S(2)}) copy-start(bf16[3,128,1536]{2,1,0:T(8,128)(2,1)} %copy-done.2) | copy-start | bytes 3538948
  83.9 1.0 %copy-start.5 = (f32[3,20,16,128]{3,2,1,0:T(8,128)S(1)}, f32[3,20,16,128]{3,2,1,0:T(8,128)}, u32[]{:S(2)}) copy-start(f32[3,20,16,128]{3,2,1,0:T(8,128)} %copy-done.4) | copy-start | bytes 1474564

commit v5 on v4

--- a/solution.py
+++ b/solution.py
@@ -154,11 +154,11 @@
     )
 
 
-def picked(result, owner):
-    out = result[0:PIECE]
-    for g in range(1, LANES // GROUP):
-        out = jnp.where(owner == g, result[g * PIECE : (g + 1) * PIECE], out)
-    return out
+def picked(result, bits):
+    parts = [result[g * PIECE : (g + 1) * PIECE] for g in range(LANES // GROUP)]
+    for bit in bits:
+        parts = [jnp.where(bit, parts[k + 1], parts[k]) for k in range(0, len(parts), 2)]
+    return parts[0]
 
 
 def toeplitz_rows(filters, shift):
@@ -212,6 +212,8 @@
     groups = LANES // GROUP
     lane = lax.broadcasted_iota(jnp.int32, (1, LANES), 1)
     owner = lane // GROUP
+    place = lax.broadcasted_iota(jnp.int32, (PIECE, LANES), 1) // GROUP
+    bits = [(place >> k) % 2 == 1 for k in range(3)]
     upside = (
         lax.broadcasted_iota(jnp.int32, (ROWS, ROWS), 0) ^ (PIECE - 1)
         == lax.broadcasted_iota(jnp.int32, (ROWS, ROWS), 1)
@@ -235,10 +237,10 @@
         for pair in range(ROWS // (2 * PIECE)):
             low = 2 * PIECE * pair
             result = jnp.dot(forward, windows(context, pair), preferred_element_type=F32)
-            wave += [picked(result[:, :LANES], owner), picked(result[:, LANES:], owner)]
+            wave += [picked(result[:, :LANES], bits), picked(result[:, LANES:], bits)]
             seen = windows(coming, pair)
             result = jnp.dot(backward, seen, preferred_element_type=F32)
-            prod_grad += [picked(result[:, :LANES], owner), picked(result[:, LANES:], owner)]
+            prod_grad += [picked(result[:, :LANES], bits), picked(result[:, LANES:], bits)]
             own = jnp.concatenate([turned[low : low + PIECE], turned[low + PIECE : low + 2 * PIECE]], axis=1)
             masked = jnp.concatenate([own * m for m in owners], axis=0)
             term = lax.dot_general(masked, seen, (((1,), (1,)), ((), ())), preferred_element_type=F32)

time: 92.8 us -> 92.9 us (level)
  no operation moved by 1% of the time
where the time goes in v5:
time: 92.9 us; the launch traced here: 91.6 us
  starting transfers between devices  28.8 us (31%)
  Pallas kernels  23.6 us (25%)
  waiting for transfers between devices  20 us (22%)
  blocking collectives  15.1 us (16%)
  local copies, waits for them, and re-layouts  3.32 us (4%)
    ppermute x6, starting transfers between devices, passed_along(): return lax.ppermute(block, axis, route)  16.3 us
    all_to_all x1, blocking collectives, local(): gathered = lax.all_to_all(payload, 'dp', 0, 0, tiled=True)  15.1 us
    pallas_call x2, Pallas kernels, back(): pl.pallas_call(functools.partial(back_kernel, first, count), out_shape=ou...  13.2 us
    ppermute x6, waiting for transfers between devices, passed_along(): return lax.ppermute(block, axis, route)  9.26 us
    all_to_all x1, starting transfers between devices, local(): parts = lax.all_to_all(parts, 'seq', 0, 0, tiled=True)  7.41 us
    all_to_all x1, waiting for transfers between devices, local(): lax.all_to_all(bundle(shorts, longs, shards), 'dp', 0, 0, tiled=True)  6.41 us
    all_to_all x1, starting transfers between devices, local(): lax.all_to_all(bundle(shorts, longs, shards), 'dp', 0, 0, tiled=True)  5.08 us
    all_to_all x1, waiting for transfers between devices, local(): parts = lax.all_to_all(parts, 'seq', 0, 0, tiled=True)  4.35 us
  transfers between devices with their start and end apart: 8, of which 4 were waited for; matrix products, arithmetic and copies ran while one was open for 0% of the time, Pallas kernels for 15%

profile of v5, /device:TPU:2, one launch (start us, length us, event | category | flops | bytes accessed | tf_op | source)
XLA Modules:
  0.0 91.6 jit_solution(15956512883189299960)
XLA Ops:
  0.6 0.0 copy-start
  0.6 1.2 %pack.1 = (bf16[32,32,128]{2,1,0:T(8,128)(2,1)S(1)}, bf16[16,12288]{1,0:T(8,128)(2,1)S(1)}) custom-call(bf16[7,384]{1,0:T(8,128)(2,1)} %short_ref.1, bf16[8,128]{1,0:T(8,128)(2,1)} %long_ref.1, bf16[1,128]{1,0:T(2,128)(2,1)} %bitcast.2, bf16[1,128,12288]{2,1,0:T(8,128)(2,1)} %streams.7), custom_call_target="tpu_custom_call" | custom-call | tf_op jit(solution)/shard_map/pack/pallas_call | solution.py:57
  1.9 3.8 %collective-permute-start = (bf16[16,12288]{1,0:T(8,128)(2,1)S(1)}, bf16[16,12288]{1,0:T(8,128)(2,1)S(1)}, u32[]{:S(2)}, u32[]{:S(2)}) collective-permute-start(bf16[16,12288]{1,0:T(8,128)(2,1)S(1)} %get-tuple-element.31), channel_id=1, source_target_pairs={{0,1},{1,2},{2,3},{3,4},{4,5},{5,6},{6,7},{8,9},{9,10},{10,11},{11... | collective-permute-start | bytes 1179656 | tf_op jit(solution)/shard_map/ppermute | solution.py:449
  5.7 15.1 %all_to_all.15.g_ref = bf16[32,32,128]{2,1,0:T(8,128)(2,1)S(1)} all-to-all(bf16[32,32,128]{2,1,0:T(8,128)(2,1)S(1)} %get-tuple-element.30), channel_id=1, replica_groups=mesh['dp'=32,'seq'=8] {'dp'}, dimensions={0} | all-to-all | bytes 524288 | tf_op jit(solution)/shard_map/all_to_all | solution.py:460
  20.8 0.0 collective-permute-done.before
  20.9 0.0 copy-done
  20.9 2.5 %gates.2 = (bf16[128,2560]{1,0:T(8,128)(2,1)S(1)}, bf16[128,2560]{1,0:T(8,128)(2,1)S(1)}, bf16[128,2560]{1,0:T(8,128)(2,1)S(1)}, bf16[128,2560]{1,0:T(8,128)(2,1)S(1)}, f32[32,32,128]{2,1,0:T(8,128)S(1)}) custom-call(bf16[32,32,128]{2,1,0:T(8,128)(2,1)S(1)} %all_to_all.15.g_ref, bf16[1,128,12288]{2,1,0:T(8,128)(2,1)S(1)} %copy-done, ...), custom_call_target="tpu_custom_call" | custom-call | flops 2750000128 | tf_op jit(solution)/shard_map/gates/pallas_call | solution.py:134
  23.4 3.8 %collective-permute-start.1 = (bf16[128,2560]{1,0:T(8,128)(2,1)S(1)}, bf16[128,2560]{1,0:T(8,128)(2,1)S(1)}, u32[]{:S(2)}, u32[]{:S(2)}) collective-permute-start(bf16[128,2560]{1,0:T(8,128)(2,1)S(1)} %get-tuple-element.33.prod), channel_id=1, source_target_pairs={{0,1},{1,2},{2,3},{3,4},{4,5},{5,6},{6,7},{8,9},{9,10},{10,11},{11... | collective-permute-start | bytes 1966088 | tf_op jit(solution)/shard_map/ppermute | solution.py:449
  27.3 1.3 %collective-permute-start.2 = (bf16[128,2560]{1,0:T(8,128)(2,1)S(1)}, bf16[128,2560]{1,0:T(8,128)(2,1)S(1)}, u32[]{:S(2)}, u32[]{:S(2)}) collective-permute-start(bf16[128,2560]{1,0:T(8,128)(2,1)S(1)} %get-tuple-element.34.gate), channel_id=1, source_target_pairs={{1,0},{2,1},{3,2},{4,3},{5,4},{6,5},{7,6},{9,8},{10,9},{11,10},{12... | collective-permute-start | bytes 1966088 | tf_op jit(solution)/shard_map/ppermute | solution.py:449
  28.6 1.2 %bands.1 = (bf16[32,128,256]{2,1,0:T(8,128)(2,1)S(1)}, bf16[32,128,256]{2,1,0:T(8,128)(2,1)S(1)}) custom-call(f32[32,32,128]{2,1,0:T(8,128)S(1)} %get-tuple-element.32.g_ref.table), custom_call_target="tpu_custom_call" | custom-call | flops 1540000000 | tf_op jit(solution)/shard_map/bands/pallas_call | solution.py:192
  29.8 0.0 copy-start.1
  29.8 1.6 %gates.3 = (bf16[128,1536]{1,0:T(8,128)(2,1)S(1)}, bf16[128,1536]{1,0:T(8,128)(2,1)S(1)}, bf16[128,1536]{1,0:T(8,128)(2,1)S(1)}, bf16[128,1536]{1,0:T(8,128)(2,1)S(1)}) custom-call(f32[32,32,128]{2,1,0:T(8,128)S(1)} %get-tuple-element.32.g_ref.table, bf16[1,128,12288]{2,1,0:T(8,128)(2,1)S(1)} %copy-done, bf16[16,12288]{1,0:T(8,128)(2,1)S(1)} %collective-permute-done.before, ...), custom_call_target="tpu_custom_call" | custom-call | flops 1650000000 | tf_op jit(solution)/shard_map/gates/pallas_call | solution.py:134
  31.4 4.6 %collective-permute-start.3 = (bf16[128,1536]{1,0:T(8,128)(2,1)S(1)}, bf16[128,1536]{1,0:T(8,128)(2,1)S(1)}, u32[]{:S(2)}, u32[]{:S(2)}) collective-permute-start(bf16[128,1536]{1,0:T(8,128)(2,1)S(1)} %get-tuple-element.40.prod), channel_id=1, source_target_pairs={{0,1},{1,2},{2,3},{3,4},{4,5},{5,6},{6,7},{8,9},{9,10},{10,11},{11... | collective-permute-start | bytes 1179656 | tf_op jit(solution)/shard_map/ppermute | solution.py:449
  36.0 1.5 %collective-permute-start.4 = (bf16[128,1536]{1,0:T(8,128)(2,1)S(1)}, bf16[128,1536]{1,0:T(8,128)(2,1)S(1)}, u32[]{:S(2)}, u32[]{:S(2)}) collective-permute-start(bf16[128,1536]{1,0:T(8,128)(2,1)S(1)} %get-tuple-element.41.gate), channel_id=1, source_target_pairs={{1,0},{2,1},{3,2},{4,3},{5,4},{6,5},{7,6},{9,8},{10,9},{11,10},{12... | collective-permute-start | bytes 1179656 | tf_op jit(solution)/shard_map/ppermute | solution.py:449
  37.5 4.8 %collective-permute-done.1.prior = bf16[128,2560]{1,0:T(8,128)(2,1)S(1)} collective-permute-done((bf16[128,2560]{1,0:T(8,128)(2,1)S(1)}, bf16[128,2560]{1,0:T(8,128)(2,1)S(1)}, u32[]{:S(2)}, u32[]{:S(2)}) %collective-permute-start.1) | collective-permute-done | bytes 655392 | tf_op jit(solution)/shard_map/ppermute | solution.py:449
  42.3 4.5 %collective-permute-done.2.ahead = bf16[128,2560]{1,0:T(8,128)(2,1)S(1)} collective-permute-done((bf16[128,2560]{1,0:T(8,128)(2,1)S(1)}, bf16[128,2560]{1,0:T(8,128)(2,1)S(1)}, u32[]{:S(2)}, u32[]{:S(2)}) %collective-permute-start.2) | collective-permute-done | bytes 655392 | tf_op jit(solution)/shard_map/ppermute | solution.py:449
  46.7 0.0 copy-done.1
  46.7 8.2 %back.2 = (bf16[3,128,2560]{2,1,0:T(8,128)(2,1)S(1)}, f32[3,20,16,128]{3,2,1,0:T(8,128)S(1)}, bf16[3,8,2560]{2,1,0:T(8,128)(2,1)S(1)}, f32[3,20,8,128]{3,2,1,0:T(8,128)S(1)}, f32[20,16,128]{2,1,0:T(8,128)S(1)}) custom-call(f32[32,32,128]{2,1,0:T(8,128)S(1)} %get-tuple-element.32.g_ref.table, bf16[1,128,12288]{2,1,0:T(8,128)(2,1)S(1)} %copy-done, ...), custom_call_target="tpu_custom_call" | custom-call | flops 9349999616 | tf_op jit(solution)/shard_map/back/pallas_call | solution.py:315
  55.0 0.0 copy-start.4
  55.0 0.0 collective-permute-done.3.prior
  55.0 0.0 collective-permute-done.4.ahead
  55.0 5.0 %back.3 = (bf16[3,128,1536]{2,1,0:T(8,128)(2,1)S(1)}, f32[3,12,16,128]{3,2,1,0:T(8,128)S(1)}, bf16[3,8,4096]{2,1,0:T(8,128)(2,1)S(1)}, f32[3,12,8,128]{3,2,1,0:T(8,128)S(1)}, f32[12,16,128]{2,1,0:T(8,128)S(1)}) custom-call(f32[32,32,128]{2,1,0:T(8,128)S(1)} %get-tuple-element.32.g_ref.table, bf16[1,128,12288]{2,1,0:T(8,128)(2,1)S(1)} %copy-done, ...), custom_call_target="tpu_custom_call" | custom-call | flops 5609999872 | tf_op jit(solution)/shard_map/back/pallas_call | solution.py:315
  60.0 0.0 copy-done.4
  60.0 0.0 copy-start.2
  60.0 1.0 %copy-done.2 = bf16[3,128,1536]{2,1,0:T(8,128)(2,1)} copy-done((bf16[3,128,1536]{2,1,0:T(8,128)(2,1)}, bf16[3,128,1536]{2,1,0:T(8,128)(2,1)S(1)}, u32[]{:S(2)}) %copy-start.2) | copy-done | bytes 1179672
  61.0 0.7 bundle.1
  61.8 5.1 %all-to-all-start.1 = ((bf16[32,32,128]{2,1,0:T(8,128)(2,1)}), bf16[32,32,128]{2,1,0:T(8,128)(2,1)S(1)}, u32[]{:S(2)}, u32[]{:S(2)}) async-start(bf16[32,32,128]{2,1,0:T(8,128)(2,1)} %bundle.1), calls=%async_computation.1 | async-start | bytes 524288 | tf_op jit(solution)/shard_map/all_to_all | solution.py:476
  66.8 1.3 %collective-permute-start.5 = (bf16[3,8,4096]{2,1,0:T(8,128)(2,1)S(1)}, bf16[3,8,4096]{2,1,0:T(8,128)(2,1)S(1)}, u32[]{:S(2)}, u32[]{:S(2)}) collective-permute-start(bf16[3,8,4096]{2,1,0:T(8,128)(2,1)S(1)} %get-tuple-element.48), channel_id=1, source_target_pairs={{1,0},{2,1},{3,2},{4,3},{5,4},{6,5},{7,6},{9,8},{10,9},{11,10},{12... | collective-permute-start | bytes 589832 | tf_op jit(solution)/shard_map/ppermute | solution.py:449
  68.1 6.4 %all-to-all-done.1.parts_ref = bf16[32,32,128]{2,1,0:T(8,128)(2,1)S(1)} async-done(((bf16[32,32,128]{2,1,0:T(8,128)(2,1)}), bf16[32,32,128]{2,1,0:T(8,128)(2,1)S(1)}, u32[]{:S(2)}, u32[]{:S(2)}) %all-to-all-start.1) | async-done | bytes 262176 | tf_op jit(solution)/shard_map/all_to_all | solution.py:476
  74.6 0.7 total.1
  75.2 7.4 %all-to-all-start.2 = ((bf16[8,32,128]{2,1,0:T(8,128)(2,1)}), bf16[8,32,128]{2,1,0:T(8,128)(2,1)S(1)}, u32[]{:S(2)}, u32[]{:S(2)}) async-start(bf16[8,32,128]{2,1,0:T(8,128)(2,1)} %total.1), calls=%async_computation.2 | async-start | bytes 131072 | tf_op jit(solution)/shard_map/all_to_all | solution.py:477
  82.6 0.0 collective-permute-done.5.refs_4_
  82.6 0.0 copy-start.3
  82.6 1.3 %copy-done.3 = bf16[3,128,1536]{2,1,0:T(8,128)(2,1)S(1)} copy-done((bf16[3,128,1536]{2,1,0:T(8,128)(2,1)S(1)}, bf16[3,128,1536]{2,1,0:T(8,128)(2,1)}, u32[]{:S(2)}) %copy-start.3) | copy-done | bytes 1179672
  83.9 0.0 copy-start.5
  83.9 1.0 %copy-done.5 = f32[3,20,16,128]{3,2,1,0:T(8,128)S(1)} copy-done((f32[3,20,16,128]{3,2,1,0:T(8,128)S(1)}, f32[3,20,16,128]{3,2,1,0:T(8,128)}, u32[]{:S(2)}) %copy-start.5) | copy-done | bytes 491544
  84.9 1.7 %finish.1 = bf16[1,128,12288]{2,1,0:T(8,128)(2,1)} custom-call(f32[32,32,128]{2,1,0:T(8,128)S(1)} %get-tuple-element.32.g_ref.table, bf16[3,128,2560]{2,1,0:T(8,128)(2,1)S(1)} %get-tuple-element.39.refs_0_, bf16[3,128,1536]{2,1,0:T(8,128)(2,1)S(1)} %copy-done.3, f32[3,20,16,128]{3,2,1,0:T(8,128)S(1)} %copy-done.5, ...), custom_call_target="tpu_custom_call" | custom-call | flops 2860000000 | tf_op jit(solution)/shard_map/finish/pallas_call | solution.py:370
  86.7 4.3 %all-to-all-done.2.parts_ref = bf16[8,32,128]{2,1,0:T(8,128)(2,1)S(1)} async-done(((bf16[8,32,128]{2,1,0:T(8,128)(2,1)}), bf16[8,32,128]{2,1,0:T(8,128)(2,1)S(1)}, u32[]{:S(2)}, u32[]{:S(2)}) %all-to-all-start.2) | async-done | bytes 65568 | tf_op jit(solution)/shard_map/all_to_all | solution.py:477
  91.0 0.6 spread.1
Async XLA Ops:
  0.6 20.2 %copy-start = (bf16[1,128,12288]{2,1,0:T(8,128)(2,1)S(1)}, bf16[1,128,12288]{2,1,0:T(8,128)(2,1)}, u32[]{:S(2)}) copy-start(bf16[1,128,12288]{2,1,0:T(8,128)(2,1)} %streams.7) | copy-start | bytes 9437188
  1.9 19.0 %collective-permute-start = (bf16[16,12288]{1,0:T(8,128)(2,1)S(1)}, bf16[16,12288]{1,0:T(8,128)(2,1)S(1)}, u32[]{:S(2)}, u32[]{:S(2)}) collective-permute-start(bf16[16,12288]{1,0:T(8,128)(2,1)S(1)} %get-tuple-element.31), channel_id=1, source_target_pairs={{0,1},{1,2},{2,3},{3,4},{4,5},{5,6},{6,7},{8,9},{9,10},{10,11},{11... | collective-permute-start | bytes 1179656 | tf_op jit(solution)/shard_map/ppermute | solution.py:449
  23.4 18.8 %collective-permute-start.1 = (bf16[128,2560]{1,0:T(8,128)(2,1)S(1)}, bf16[128,2560]{1,0:T(8,128)(2,1)S(1)}, u32[]{:S(2)}, u32[]{:S(2)}) collective-permute-start(bf16[128,2560]{1,0:T(8,128)(2,1)S(1)} %get-tuple-element.33.prod), channel_id=1, source_target_pairs={{0,1},{1,2},{2,3},{3,4},{4,5},{5,6},{6,7},{8,9},{9,10},{10,11},{11... | collective-permute-start | bytes 1966088 | tf_op jit(solution)/shard_map/ppermute | solution.py:449
  27.3 19.5 %collective-permute-start.2 = (bf16[128,2560]{1,0:T(8,128)(2,1)S(1)}, bf16[128,2560]{1,0:T(8,128)(2,1)S(1)}, u32[]{:S(2)}, u32[]{:S(2)}) collective-permute-start(bf16[128,2560]{1,0:T(8,128)(2,1)S(1)} %get-tuple-element.34.gate), channel_id=1, source_target_pairs={{1,0},{2,1},{3,2},{4,3},{5,4},{6,5},{7,6},{9,8},{10,9},{11,10},{12... | collective-permute-start | bytes 1966088 | tf_op jit(solution)/shard_map/ppermute | solution.py:449
  29.8 17.0 %copy-start.1 = (bf16[1,128,4096]{2,1,0:T(8,128)(2,1)S(1)}, bf16[1,128,4096]{2,1,0:T(8,128)(2,1)}, u32[]{:S(2)}) copy-start(bf16[1,128,4096]{2,1,0:T(8,128)(2,1)} %cot.3) | copy-start | bytes 3145732
  31.4 23.6 %collective-permute-start.3 = (bf16[128,1536]{1,0:T(8,128)(2,1)S(1)}, bf16[128,1536]{1,0:T(8,128)(2,1)S(1)}, u32[]{:S(2)}, u32[]{:S(2)}) collective-permute-start(bf16[128,1536]{1,0:T(8,128)(2,1)S(1)} %get-tuple-element.40.prod), channel_id=1, source_target_pairs={{0,1},{1,2},{2,3},{3,4},{4,5},{5,6},{6,7},{8,9},{9,10},{10,11},{11... | collective-permute-start | bytes 1179656 | tf_op jit(solution)/shard_map/ppermute | solution.py:449
  36.0 19.0 %collective-permute-start.4 = (bf16[128,1536]{1,0:T(8,128)(2,1)S(1)}, bf16[128,1536]{1,0:T(8,128)(2,1)S(1)}, u32[]{:S(2)}, u32[]{:S(2)}) collective-permute-start(bf16[128,1536]{1,0:T(8,128)(2,1)S(1)} %get-tuple-element.41.gate), channel_id=1, source_target_pairs={{1,0},{2,1},{3,2},{4,3},{5,4},{6,5},{7,6},{9,8},{10,9},{11,10},{12... | collective-permute-start | bytes 1179656 | tf_op jit(solution)/shard_map/ppermute | solution.py:449
  55.0 5.0 %copy-start.4 = (f32[3,20,16,128]{3,2,1,0:T(8,128)}, f32[3,20,16,128]{3,2,1,0:T(8,128)S(1)}, u32[]{:S(2)}) copy-start(f32[3,20,16,128]{3,2,1,0:T(8,128)S(1)} %get-tuple-element.46.refs_2_) | copy-start | bytes 1474564
  60.0 1.0 %copy-start.2 = (bf16[3,128,1536]{2,1,0:T(8,128)(2,1)}, bf16[3,128,1536]{2,1,0:T(8,128)(2,1)S(1)}, u32[]{:S(2)}) copy-start(bf16[3,128,1536]{2,1,0:T(8,128)(2,1)S(1)} %get-tuple-element.45.refs_1_) | copy-start | bytes 3538948
  61.8 12.8 %all-to-all-start.1 = ((bf16[32,32,128]{2,1,0:T(8,128)(2,1)}), bf16[32,32,128]{2,1,0:T(8,128)(2,1)S(1)}, u32[]{:S(2)}, u32[]{:S(2)}) async-start(bf16[32,32,128]{2,1,0:T(8,128)(2,1)} %bundle.1), calls=%async_computation.1 | async-start | bytes 524288 | tf_op jit(solution)/shard_map/all_to_all | solution.py:476
  66.8 15.8 %collective-permute-start.5 = (bf16[3,8,4096]{2,1,0:T(8,128)(2,1)S(1)}, bf16[3,8,4096]{2,1,0:T(8,128)(2,1)S(1)}, u32[]{:S(2)}, u32[]{:S(2)}) collective-permute-start(bf16[3,8,4096]{2,1,0:T(8,128)(2,1)S(1)} %get-tuple-element.48), channel_id=1, source_target_pairs={{1,0},{2,1},{3,2},{4,3},{5,4},{6,5},{7,6},{9,8},{10,9},{11,10},{12... | collective-permute-start | bytes 589832 | tf_op jit(solution)/shard_map/ppermute | solution.py:449
  75.2 15.8 %all-to-all-start.2 = ((bf16[8,32,128]{2,1,0:T(8,128)(2,1)}), bf16[8,32,128]{2,1,0:T(8,128)(2,1)S(1)}, u32[]{:S(2)}, u32[]{:S(2)}) async-start(bf16[8,32,128]{2,1,0:T(8,128)(2,1)} %total.1), calls=%async_computation.2 | async-start | bytes 131072 | tf_op jit(solution)/shard_map/all_to_all | solution.py:477
  82.6 1.3 %copy-start.3 = (bf16[3,128,1536]{2,1,0:T(8,128)(2,1)S(1)}, bf16[3,128,1536]{2,1,0:T(8,128)(2,1)}, u32[]{:S(2)}) copy-start(bf16[3,128,1536]{2,1,0:T(8,128)(2,1)} %copy-done.2) | copy-start | bytes 3538948
  83.9 1.0 %copy-start.5 = (f32[3,20,16,128]{3,2,1,0:T(8,128)S(1)}, f32[3,20,16,128]{3,2,1,0:T(8,128)}, u32[]{:S(2)}) copy-start(f32[3,20,16,128]{3,2,1,0:T(8,128)} %copy-done.4) | copy-start | bytes 1474564
